TPU v7x, 512 devices: a whole 4x8x8 slice. The times are simulated.
512 devices in a mesh: row: 32 (over y_lo, z, core), col: 16 (over y_hi, x).
Axes of the slice: x: 4, y: 8 (y_hi: 4, y_lo: 2; y = y_hi * 2 + y_lo), z: 8, core: 2. Of those that a mesh axis runs over, the one named last changes fastest.
Arguments:
- hessenberg: float32 [16384, 2, 8192], P('row', None, 'col'), may hold values from -6 to 6, as said below
- diag_factors: float32 [32, 512, 512], P('row', 'col'), may hold values from -0.25 to 0.25
- border_factors: float32 [32, 512, 512], P('row', 'col'), may hold values from -0.25 to 0.25
- window_live: int32 [2, 32], replicated, may hold values from 0 to 1, as said below
Outputs:
- updated: float32 [16384, 2, 8192], P('row', None, 'col')
Inputs may be any that keep to these rules, and one draw needn't show every extreme that they name: `hessenberg`: H is upper Hessenberg: entries more than one place below the diagonal are zero. Border windows k < 16 and the last border window of the sweep act: window_live[1, k] = 1 for those k and for k = 30.
All inputs are finite; a program needn't handle non-finite values.
Results may differ from a plain program's by a relative error of at most 0.00011.
Values sent between devices are 32-bit elements; how exact they have to be, the bound alone decides.
No kernel may reach another device: no remote copies, remote signals or barrier semaphores. Data moves between devices by JAX's collectives and lax.ppermute only.
A program may use at most 64 MiB of HBM per device.

v0:
```python
import jax
import jax.numpy as jnp
from jax import lax
from jax.sharding import PartitionSpec as P

precise = lax.Precision.HIGHEST


def passed_along(value, axis, steps):
    count = lax.axis_size(axis)
    first, last = (max(0, -steps), min(count, count - steps))
    return lax.ppermute(value, axis, [(source, source + steps) for source in range(first, last)])


def spread(value, axis, source):
    kept = jnp.where(lax.axis_index(axis) == source, value, 0).astype(value.dtype)
    return lax.psum(kept, axis)


def extended(cells, sides, width, closed):
    for axis, dim in sides:
        count = lax.axis_size(axis)
        ends = count if closed else count - 1
        head = lax.slice_in_dim(cells, 0, width, axis=dim)
        tail = lax.slice_in_dim(cells, cells.shape[dim] - width, cells.shape[dim], axis=dim)
        cells = jnp.concatenate(
            [
                lax.ppermute(tail, axis, [(i, (i + 1) % count) for i in range(ends)]),
                cells,
                lax.ppermute(head, axis, [((i + 1) % count, i) for i in range(ends)]),
            ],
            axis=dim,
        )
    return cells


def slot_product(strips, factors):
    return jnp.einsum(
        "asq,sqb->asb", strips, factors, precision=precise, preferred_element_type=jnp.float32
    )


def transposed_product(factor, strips):
    return jnp.einsum(
        "ka,ksq->asq", factor, strips, precision=precise, preferred_element_type=jnp.float32
    )


def shards(hessenberg, diag_factors, border_factors, window_live):
    window = hessenberg.shape[0]
    slot_count = hessenberg.shape[1]
    halfway = window // 2
    columns = lax.axis_size("col")
    row_here = lax.axis_index("row")
    col_here = lax.axis_index("col")
    tile_count = slot_count * columns
    tile_cols = jnp.arange(slot_count, dtype=jnp.int32) * columns + col_here
    local_cols = jnp.arange(window, dtype=jnp.int32)
    global_rows = row_here * window + jnp.arange(window, dtype=jnp.int32)
    global_cols = tile_cols[:, None] * window + local_cols[None, :]
    diag_live = window_live[0]
    border_live = window_live[1] * (
        jnp.arange(tile_count, dtype=jnp.int32) < tile_count - 1
    ).astype(jnp.int32)
    above_piece = passed_along(border_factors, "row", 1)
    diag_full, border_full, above_full = (
        lax.all_gather(diag_factors, "col", axis=1, tiled=True),
        lax.all_gather(border_factors, "col", axis=1, tiled=True),
        lax.all_gather(above_piece, "col", axis=1, tiled=True),
    )
    diag_own = diag_full[0]
    border_own = border_full[0]
    above_own = above_full[0]
    received = []
    for turn_index in range(slot_count):
        source_row = turn_index * columns + col_here
        pieces = (
            spread(diag_own, "row", source_row),
            spread(border_own, "row", source_row),
            spread(above_own[:, halfway:], "row", source_row),
        )
        received.append(pieces)
    col_diag = jnp.stack([pieces[0] for pieces in received])
    col_border = jnp.stack([pieces[1] for pieces in received])
    col_above = jnp.stack([pieces[2] for pieces in received])
    row_active = lax.dynamic_index_in_dim(diag_live, row_here, 0, keepdims=False) == 1
    turned = transposed_product(diag_own, hessenberg)
    keep_left = (tile_cols >= row_here) & row_active
    section_one = jnp.where(keep_left[None, :, None], turned, hessenberg)
    col_active = jnp.take(diag_live, tile_cols) == 1
    rotated = slot_product(section_one, col_diag)
    keep_right = (row_here <= tile_cols) & col_active
    section_two = jnp.where(keep_right[None, :, None], rotated, section_one)
    own_active = lax.dynamic_index_in_dim(border_live, row_here, 0, keepdims=False) == 1
    prev_active = (row_here >= 1) & (
        lax.dynamic_index_in_dim(border_live, jnp.maximum(row_here - 1, 0), 0, keepdims=False) == 1
    )
    top_rows = section_two[:halfway]
    bottom_rows = section_two[halfway:]
    margin = extended(section_two, (("row", 0),), halfway, False)
    new_top = transposed_product(above_own[:, halfway:], margin[:window])
    new_bottom = transposed_product(border_own[:, :halfway], margin[window:])
    top_keep = (global_cols >= (row_here - 1) * window + halfway) & prev_active
    bottom_keep = (global_cols >= row_here * window + halfway) & own_active
    section_three = jnp.concatenate(
        [
            jnp.where(top_keep[None], new_top, top_rows),
            jnp.where(bottom_keep[None], new_bottom, bottom_rows),
        ],
        0,
    )
    left_part = section_three[:, :, :halfway]
    right_part = section_three[:, :, halfway:]
    margin = extended(section_three, (("col", 2),), halfway, True)
    from_left = margin[:, :, :halfway]
    from_right = margin[:, :, halfway + window :]
    from_left = jnp.where(col_here == 0, jnp.roll(from_left, 1, axis=1), from_left)
    from_right = jnp.where(col_here == columns - 1, jnp.roll(from_right, -1, axis=1), from_right)
    right_half = slot_product(
        jnp.concatenate([right_part, from_right], 2), col_border[:, :, :halfway]
    )
    left_half = slot_product(jnp.concatenate([from_left, left_part], 2), col_above)
    right_active = jnp.take(border_live, tile_cols) == 1
    left_active = (tile_cols >= 1) & (jnp.take(border_live, jnp.maximum(tile_cols - 1, 0)) == 1)
    right_keep = (
        global_rows[:, None] < tile_cols[None, :] * window + window + halfway
    ) & right_active[None, :]
    left_keep = (global_rows[:, None] < tile_cols[None, :] * window + halfway) & left_active[
        None, :
    ]
    return jnp.concatenate(
        [
            jnp.where(left_keep[:, :, None], left_half, left_part),
            jnp.where(right_keep[:, :, None], right_half, right_part),
        ],
        2,
    )


def solution(mesh):
    in_specs = (P("row", None, "col"), P("row", "col", None), P("row", "col", None), P())
    out_specs = P("row", None, "col")
    return jax.shard_map(shards, mesh=mesh, in_specs=in_specs, out_specs=out_specs, check_vma=False)
```

profile of v0, /device:TPU:86, one launch (start us, length us, event | category | flops | bytes accessed | tf_op | source)
XLA Modules:
  0.0 536.6 jit_solution(5122574981199386056)
XLA Ops:
  6.5 0.0 all-gather.8.cloned.1.call-start
  6.5 1.5 copy.23
  8.1 0.0 all-gather.8.cloned.1.call-update
  8.1 0.0 all-gather.6.cloned.1.call-start
  8.1 1.5 copy.25
  9.7 0.0 all-gather.6.cloned.1.call-update
  9.7 0.0 all-gather.4.cloned.1.call-start
  9.8 1.9 collective-permute-start
  11.7 3.9 collective-permute-done
  15.5 0.6 copy-done.5
  16.2 0.0 all-gather.4.cloned.1.call-update
  16.2 0.0 all-reduce.3.cloned.1.call-start
  16.3 54.9 %all-gather.8.cloned.1.call-done = f32[1,512,512]{2,0,1:T(1,128)} async-done(((f32[1,32,512]{2,0,1:T(1,128)}), f32[1,512,512]{2,0,1:T(1,128)}) %all-gather.8.cloned.1.call-update) | async-done | bytes 1048592 | tf_op jit(solution)/shard_map/all_gather | solution.py:68
  71.2 2.3 copy.31
  73.5 56.7 %all-gather.6.cloned.1.call-done = f32[1,512,512]{2,0,1:T(1,128)} async-done(((f32[1,32,512]{2,0,1:T(1,128)}), f32[1,512,512]{2,0,1:T(1,128)}) %all-gather.6.cloned.1.call-update) | async-done | bytes 1048592 | tf_op jit(solution)/shard_map/all_gather | solution.py:67
  130.2 2.3 copy.26
  132.6 1.6 select_bitcast_fusion.1
  134.2 1.7 fusion.44
  135.9 53.4 %all-gather.4.cloned.1.call-done = f32[1,512,512]{2,0,1:T(1,128)} async-done(((f32[1,32,512]{2,0,1:T(1,128)}), f32[1,512,512]{2,0,1:T(1,128)}) %all-gather.4.cloned.1.call-update) | async-done | bytes 1048592 | tf_op jit(solution)/shard_map/all_gather | solution.py:69
  189.2 2.3 copy.24
  191.6 0.0 copy-start
  191.6 1.2 select_bitcast_fusion.3
  192.8 0.0 all-reduce.3.cloned.1.call-update
  192.9 0.0 copy-done
  192.9 0.6 copy-done.6
  193.5 0.6 fusion.57
  194.1 0.6 gather_fusion.1
  194.8 0.7 compare_and_fusion.5
  195.4 7.6 %copy_select_fusion = f32[512,2,512]{2,0,1:T(8,128)} fusion(f32[512,2,512]{2,1,0:T(2,128)} %param.6, f32[1,512,512]{1,2,0:T(8,128)S(1)} %copy.26, pred[2]{0:T(512)(128)(4,1)S(1)} %compare_and_fusion.5), kind=kOutput, calls=%fused_computation.25 | convolution fusion | flops 3221749760 | bytes 5242882 | tf_op jit(solution)/shard_map/ka,ksq->asq/dot_general | solution.py:44
  203.1 230.4 %all-reduce.3.cloned.1.call-done = (f32[1,512,512]{1,2,0:T(8,128)}, f32[1,512,512]{1,2,0:T(8,128)}, f32[1,512,512]{1,2,0:T(8,128)}, f32[1,512,512]{1,2,0:T(8,128...) async-done(((f32[1,512,512]{1,2,0:T(8,128)}, f32[1,512,512]{1,2,0:T(8,128)}, f32[1,512,512]{1,2,0:T(8,128)}, f32[1,512,512]{1,2,0:T(8,128)}, f32[1,512,256]{1,2,0:T(8,128)}, ...) | async-done | bytes 5242896 | tf_op jit(solution)/shard_map/psum | solution.py:17
  433.4 6.4 %bitcast_select_fusion = f32[512,2,512]{2,0,1:T(8,128)S(1)} fusion(f32[512,2,512]{2,0,1:T(8,128)} %copy_select_fusion, f32[1,512,512]{1,2,0:T(8,128)} %get-tuple-element.6, f32[1,512,512]{1,2,0:T(8,128)} %get-tuple-element.7, pred[2]{0:T(512)(128)(4,1)S(1)} %compare_and_fusion.6), kind=kOutput, calls=%fused_computation.24 | convolution fusion | flops 3222274048 | bytes 6291458 | tf_op jit(solution)/shard_map/asq,sqb->asb/dot_general | solution.py:38
  439.8 1.5 fusion.53
  441.3 2.0 collective-permute-start.1
  443.3 5.4 %collective-permute-start.2 = (f32[256,2,512]{2,0,1:T(8,128)}, f32[256,2,512]{2,0,1:T(8,128)}, u32[]{:S(2)}, u32[]{:S(2)}) collective-permute-start(f32[256,2,512]{2,0,1:T(8,128)} %get-tuple-element.14), channel_id=1, source_target_pairs={{16,0},{32,16},{48,32},{64,48},{80,64},{96,80},{112,96},{128,112},... | collective-permute-start | bytes 3145736 | tf_op jit(solution)/shard_map/ppermute | solution.py:30
  448.8 0.6 fusion.56
  450.7 0.1 compare_and_fusion.1
  450.8 8.7 %collective-permute-done.1 = f32[256,2,512]{2,0,1:T(8,128)} collective-permute-done((f32[256,2,512]{2,0,1:T(8,128)}, f32[256,2,512]{2,0,1:T(8,128)}, u32[]{:S(2)}, u32[]{:S(2)}) %collective-permute-start.1) | collective-permute-done | bytes 1048608 | tf_op jit(solution)/shard_map/ppermute | solution.py:28
  459.4 3.3 fusion.25
  462.8 0.0 collective-permute-done.2
  462.8 3.2 fusion.24
  466.0 0.2 pad_maximum_fusion.15
  466.2 4.6 collective-permute-start.3
  470.8 0.6 gather_fusion.2
  471.5 0.6 gather_fusion
  472.2 1.9 collective-permute-start.4
  474.1 0.1 compare_and_fusion.3
  474.2 23.8 %collective-permute-done.3 = f32[512,2,256]{2,0,1:T(8,128)S(1)} collective-permute-done((f32[512,2,256]{2,0,1:T(8,128)S(1)}, f32[512,2,256]{2,0,1:T(8,128)S(1)}, u32[]{:S(2)}, u32[]{:S(2)}) %collective-permute-start.3) | collective-permute-done | bytes 1048608 | tf_op jit(solution)/shard_map/ppermute | solution.py:28
  498.0 0.1 fusion.54
  498.1 0.0 copy-start.3
  498.1 0.0 copy-start.4
  498.1 0.1 maximum_select_fusion
  498.3 0.9 copy-done.3
  499.1 0.2 copy-done.4
  499.3 2.0 fusion.35
  501.3 20.3 %collective-permute-done.4 = f32[512,2,256]{2,0,1:T(8,128)} collective-permute-done((f32[512,2,256]{2,0,1:T(8,128)S(1)}, f32[512,2,256]{2,0,1:T(8,128)}, u32[]{:S(2)}, u32[]{:S(2)}) %collective-permute-start.4) | collective-permute-done | bytes 1048608 | tf_op jit(solution)/shard_map/ppermute | solution.py:30
  521.6 1.3 fusion.55
  522.9 0.0 copy-start.1
  522.9 0.0 copy-start.2
  522.9 1.5 maximum_select_fusion.1
  524.4 0.0 copy-done.1
  524.4 0.3 copy-done.2
  524.8 2.0 fusion.29
  526.8 0.3 pad_maximum_fusion.4
  527.1 2.9 copy.34
  (13 shorter events, 0.1 us)
Async XLA Ops:
  6.5 64.7 %all-gather.8.cloned.1.call-start = ((), (), s32[]{:S(2)}) async-start(), calls=%async_computation.2 | async-start | bytes 1114112 | tf_op jit(solution)/shard_map/all_gather | solution.py:68
  8.1 122.1 %all-gather.6.cloned.1.call-start = ((), (), s32[]{:S(2)}) async-start(), calls=%async_computation.1 | async-start | bytes 1114112 | tf_op jit(solution)/shard_map/all_gather | solution.py:67
  9.7 179.5 %all-gather.4.cloned.1.call-start = ((), (), s32[]{:S(2)}) async-start(), calls=%async_computation | async-start | bytes 1114112 | tf_op jit(solution)/shard_map/all_gather | solution.py:69
  9.8 5.8 %collective-permute-start = (f32[1,32,512]{2,0,1:T(1,128)}, f32[1,32,512]{2,0,1:T(1,128)S(1)}, u32[]{:S(2)}, u32[]{:S(2)}) collective-permute-start(f32[1,32,512]{2,0,1:T(1,128)} %copy.23), channel_id=1, source_target_pairs={{0,16},{16,32},{32,48},{48,64},{64,80},{80,96},{96,112},{112,128},... | collective-permute-start | bytes 196616 | tf_op jit(solution)/shard_map/ppermute | solution.py:12
  15.5 0.6 copy-start.5
  16.2 417.3 %all-reduce.3.cloned.1.call-start = ((), (), s32[]{:S(2)}) async-start(), calls=%async_computation.3 | async-start | bytes 10485760 | tf_op jit(solution)/shard_map/psum | solution.py:17
  191.6 1.3 copy-start
  192.8 0.7 copy-start.6
  441.3 18.1 %collective-permute-start.1 = (f32[256,2,512]{2,0,1:T(8,128)}, f32[256,2,512]{2,0,1:T(8,128)}, u32[]{:S(2)}, u32[]{:S(2)}) collective-permute-start(f32[256,2,512]{2,0,1:T(8,128)} %get-tuple-element.15), channel_id=1, source_target_pairs={{0,16},{16,32},{32,48},{48,64},{64,80},{80,96},{96,112},{112,128},... | collective-permute-start | bytes 3145736 | tf_op jit(solution)/shard_map/ppermute | solution.py:28
  443.3 19.5 %collective-permute-start.2 = (f32[256,2,512]{2,0,1:T(8,128)}, f32[256,2,512]{2,0,1:T(8,128)}, u32[]{:S(2)}, u32[]{:S(2)}) collective-permute-start(f32[256,2,512]{2,0,1:T(8,128)} %get-tuple-element.14), channel_id=1, source_target_pairs={{16,0},{32,16},{48,32},{64,48},{80,64},{96,80},{112,96},{128,112},... | collective-permute-start | bytes 3145736 | tf_op jit(solution)/shard_map/ppermute | solution.py:30
  466.2 31.8 %collective-permute-start.3 = (f32[512,2,256]{2,0,1:T(8,128)S(1)}, f32[512,2,256]{2,0,1:T(8,128)S(1)}, u32[]{:S(2)}, u32[]{:S(2)}) collective-permute-start(f32[512,2,256]{2,0,1:T(8,128)S(1)} %get-tuple-element.13), channel_id=1, source_target_pairs={{0,1},{1,2},{2,3},{3,4},{4,5},{5,6},{6,7},{7,8},{8,9},{9,10},{10,1... | collective-permute-start | bytes 3145736 | tf_op jit(solution)/shard_map/ppermute | solution.py:28
  472.2 49.5 %collective-permute-start.4 = (f32[512,2,256]{2,0,1:T(8,128)S(1)}, f32[512,2,256]{2,0,1:T(8,128)}, u32[]{:S(2)}, u32[]{:S(2)}) collective-permute-start(f32[512,2,256]{2,0,1:T(8,128)S(1)} %get-tuple-element.12), channel_id=1, source_target_pairs={{1,0},{2,1},{3,2},{4,3},{5,4},{6,5},{7,6},{8,7},{9,8},{10,9},{11,1... | collective-permute-start | bytes 3145736 | tf_op jit(solution)/shard_map/ppermute | solution.py:30
  498.1 1.0 copy-start.3
  498.1 1.2 copy-start.4
  522.9 1.5 copy-start.1
  522.9 1.8 copy-start.2
Sparse Core Ops, SparseCore 0:
  10.4 60.7 all-gather.7
  74.2 55.9 all-gather.5
  133.2 55.9 all-gather.3
  193.0 240.4 all-reduce.2
where the time goes:
time: 537 us
  waiting for transfers between devices  452 us (84%)
  matrix products  24.6 us (5%)
  local copies, waits for them, and re-layouts  21.1 us (4%)
  starting transfers between devices  16 us (3%)
  between operations  14.7 us (3%)
  other arithmetic  8.17 us (2%)
    psum x1, waiting for transfers between devices, spread(): return lax.psum(kept, axis)  230 us
    all_gather x1, waiting for transfers between devices, shards(): lax.all_gather(diag_factors, 'col', axis=1, tiled=True)  56.7 us
    all_gather x1, waiting for transfers between devices, shards(): lax.all_gather(border_factors, 'col', axis=1, tiled=True)  54.9 us
    all_gather x1, waiting for transfers between devices, shards(): lax.all_gather(above_piece, 'col', axis=1, tiled=True)  53.4 us
    ppermute x2, waiting for transfers between devices, extended(): lax.ppermute(tail, axis, [(i, (i + 1) % count) for i in range(ends)])  32.5 us
    ppermute x2, waiting for transfers between devices, extended(): lax.ppermute(head, axis, [((i + 1) % count, i) for i in range(ends)])  20.3 us
    dot_general x3, matrix products, transposed_product(): jnp.einsum('ka,ksq->asq', factor, strips, precision=precise, preferred_el...  14.2 us
  transfers between devices with their start and end apart: 9, of which 8 were waited for; matrix products, arithmetic and copies ran while one was open for 5% of the time, Pallas kernels for 0%

commit v1 on v0

v1 whole, which is shorter than its diff:
```python
import jax
import jax.numpy as jnp
from jax import lax
from jax.sharding import PartitionSpec as P

GRID_ROWS, GRID_COLS = 32, 16
RING = 4


def dot(a, b):
    return jnp.dot(a, b, precision=lax.Precision.HIGH, preferred_element_type=jnp.float32)


def tdot(a, b):
    return lax.dot_general(
        a, b, (((0,), (0,)), ((), ())), precision=lax.Precision.HIGH, preferred_element_type=jnp.float32
    )


def moved(value, axis, target):
    count = lax.axis_size(axis)
    pairs = [(i, target(i)) for i in range(count)]
    return lax.ppermute(value, axis, [(i, j) for i, j in pairs if j is not None and 0 <= j < count])


def moved_on(value, pairs):
    number = [(r * GRID_COLS + c, t * GRID_COLS + d) for (r, c), (t, d) in pairs]
    return lax.ppermute(value, ("row", "col"), number)


def everywhere(test, target):
    return [
        ((r, c), target(r, c)) for r in range(GRID_ROWS) for c in range(GRID_COLS) if test(r, c)
    ]


def ring_gather(piece, shifted, place):
    size = piece.shape[0]
    half = size // 2
    behind = moved(piece, "col", shifted(1))
    ahead = moved(piece, "col", shifted(-1))
    far_a = moved(behind[:half], "col", shifted(1))
    far_b = moved(ahead[half:], "col", shifted(-1))
    around = jnp.concatenate([far_a, far_b, behind, piece, ahead], 0)
    return jnp.roll(around.reshape(RING, size, -1), place - 2, axis=0)


def shards(hessenberg, diag_factors, border_factors, window_live):
    window = hessenberg.shape[0]
    half = window // 2
    row = lax.axis_index("row")
    col = lax.axis_index("col")
    last = 2 * GRID_COLS - 1
    live_d = window_live[0]
    live_b = window_live[1] * (jnp.arange(2 * GRID_COLS) < last)
    tiles = [col, col + GRID_COLS]

    def at(flags, index):
        inside = (index >= 0) & (index <= last)
        return inside & (lax.dynamic_index_in_dim(flags, jnp.clip(index, 0, last), 0, False) == 1)

    own = diag_factors[0]
    border = border_factors[0]
    above = moved(border[:, half:], "row", lambda r: r + 1)
    piece = jnp.concatenate([own, border[:, :half], above], 1)
    turned_piece = moved_on(
        piece, everywhere(lambda r, c: True, lambda r, c: (r // 16 * 16 + c, r % 16))
    )
    by_col = lax.all_gather(turned_piece, "row", axis=0, tiled=True)

    ring_y = ring_gather(piece, lambda s: (lambda c: (c + RING * s) % GRID_COLS), col // RING)
    ring_x = ring_gather(
        ring_y.reshape(RING * piece.shape[0], -1),
        lambda s: (lambda c: c // RING * RING + (c + s) % RING),
        col % RING,
    )
    by_row = ring_x.reshape(RING, RING, piece.shape[0], -1).transpose(1, 0, 2, 3).reshape(window, -1)
    left_d, left_b, left_a = by_row[:, :window], by_row[:, window : window + half], by_row[:, window + half :]

    slots = [hessenberg[:, 0], hessenberg[:, 1]]
    both = jnp.concatenate(slots, 1)
    turned = tdot(left_d, both)
    live_row = at(live_d, row)
    first = []
    for s in range(2):
        keep = (tiles[s] >= row) & live_row
        first.append(jnp.where(keep, turned[:, s * window : (s + 1) * window], slots[s]))
    corner_own = [f[0, window - 1] for f in first]
    packed = jnp.concatenate(first, 1)

    down = everywhere(lambda r, c: r < 31 and c + 16 >= r, lambda r, c: (r + 1, c))
    up = [(b, a) for a, b in down]
    from_above = moved_on(packed[half:], down)
    from_below = moved_on(packed[:half], up)
    own_top, own_bottom, below, corner_below = [], [], [], []
    for s in range(2):
        part = slice(s * window, (s + 1) * window)
        corner_below.append(from_below[0, (s + 1) * window - 1])
        below.append(jnp.where(tiles[s] > row, from_below[:, part], 0))
        own_top.append(jnp.where(tiles[s] >= row, first[s][:half], 0))
        own_bottom.append(first[s][half:])
    new_top = tdot(left_a, jnp.concatenate([from_above, jnp.concatenate(own_top, 1)], 0))
    new_bottom = tdot(left_b, jnp.concatenate([packed[half:], jnp.concatenate(below, 1)], 0))
    prev_active = at(live_b, row - 1)
    own_active = at(live_b, row)

    def sides(s):
        part = slice(s * window, (s + 1) * window)
        tile = tiles[s]
        top = jnp.where((tile >= row - 1) & prev_active, new_top[:, part], own_top[s])
        bottom = jnp.where((tile >= row) & own_active, new_bottom[:, part], own_bottom[s])
        for_right = jnp.concatenate([top, bottom], 0)
        for_left = jnp.concatenate(
            [jnp.where(tile >= row, top, 0), jnp.where(tile == row, own_bottom[s], bottom)], 0
        )
        unit = (jnp.arange(half) == 0).astype(jnp.float32)
        extra_top = jnp.where(prev_active, left_a[half], unit) * jnp.where(tile == row - 1, corner_own[s], 0)
        extra_bottom = left_b[half] * jnp.where((tile == row) & own_active, corner_below[s], 0)
        extra = jnp.concatenate([extra_top, extra_bottom], 0)
        return for_left, for_right, extra

    lefts, rights = [None, None], [None, None]
    prepared = [sides(s) for s in range(2)]
    for s in (1, 0):
        for_left, for_right, extra = prepared[s]
        factor = by_col[s * window : (s + 1) * window]
        live = at(live_d, tiles[s])
        left = jnp.where(live, dot(for_left, factor[:, :half]), for_left[:, :half])
        right = jnp.where(live, dot(for_right, factor[:, half:window]), for_right[:, half:])
        last_col = (jnp.arange(half) == half - 1).astype(jnp.float32)
        lefts[s] = left
        rights[s] = right + extra[:, None] * last_col[None, :]

    reach = lambda s: (lambda r, c: r <= c + 16 * s + 1)
    right_1 = moved_on(rights[1], [p for p in everywhere(reach(1), lambda r, c: (r, c + 1)) if p[1][1] < 16])
    left_1 = moved_on(lefts[1], everywhere(lambda r, c: r <= c + 16, lambda r, c: (r, (c - 1) % 16)))
    right_0 = moved_on(rights[0], everywhere(reach(0), lambda r, c: (r, (c + 1) % 16)))
    left_0 = moved_on(lefts[0], [p for p in everywhere(lambda r, c: r <= c, lambda r, c: (r, c - 1)) if p[1][1] >= 0])
    from_left = [right_0, jnp.where(col == 0, right_0, right_1)]
    from_right = [jnp.where(col == GRID_COLS - 1, left_1, left_0), left_1]
    top_rows = (jnp.arange(window) < half)[:, None]
    outs = []
    for s in range(2):
        tile = tiles[s]
        factor = by_col[s * window : (s + 1) * window]
        new_left = dot(jnp.concatenate([from_left[s], lefts[s]], 1), factor[:, window + half :])
        new_right = dot(jnp.concatenate([rights[s], from_right[s]], 1), factor[:, window : window + half])
        keep_left = ((row < tile) | ((row == tile) & top_rows)) & at(live_b, tile - 1)
        keep_right = ((row <= tile) | ((row == tile + 1) & top_rows)) & at(live_b, tile)
        outs.append(
            jnp.concatenate(
                [jnp.where(keep_left, new_left, lefts[s]), jnp.where(keep_right, new_right, rights[s])], 1
            )
        )
    return jnp.stack(outs, 1)


def solution(mesh):
    in_specs = (P("row", None, "col"), P("row", "col", None), P("row", "col", None), P())
    out_specs = P("row", None, "col")
    return jax.shard_map(shards, mesh=mesh, in_specs=in_specs, out_specs=out_specs, check_vma=False)
```

time: 537 us -> 190 us (0.35)
  the two profiles are of different devices: /device:TPU:86 before, /device:TPU:158 now
where the time goes in v1:
time: 190 us; the launch traced here: 189 us
  waiting for transfers between devices  65.4 us (34%)
  starting transfers between devices  62.4 us (33%)
  between operations  22.6 us (12%)
  local copies, waits for them, and re-layouts  16 us (8%)
  matrix products  13.7 us (7%)
  other arithmetic  8.58 us (5%)
    ppermute x9, starting transfers between devices, moved(): lax.ppermute(value, axis, [(i, j) for i, j in pairs if j is not None and...  41.1 us
    ppermute x7, waiting for transfers between devices, moved_on(): return lax.ppermute(value, ('row', 'col'), number)  41.1 us
    ppermute x9, waiting for transfers between devices, moved(): lax.ppermute(value, axis, [(i, j) for i, j in pairs if j is not None and...  24.2 us
    ppermute x7, starting transfers between devices, moved_on(): return lax.ppermute(value, ('row', 'col'), number)  21.2 us
    dot_general x8, matrix products, dot(): jnp.dot(a, b, precision=lax.Precision.HIGH, preferred_element_type=jnp.fl...  6.99 us
    dot_general x3, matrix products, tdot(): lax.dot_general(a, b, (((0,), (0,)), ((), ())), precision=lax.Precision.H...  6.68 us
    unnamed x41, local copies, waits for them, and re-layouts  4.81 us
  transfers between devices with their start and end apart: 17, of which 10 were waited for; matrix products, arithmetic and copies ran while one was open for 15% of the time, Pallas kernels for 0%

profile of v1, /device:TPU:158, one launch (start us, length us, event | category | flops | bytes accessed | tf_op | source)
XLA Modules:
  0.0 188.6 jit_solution(17058851891279356176)
XLA Ops:
  6.5 0.9 fusion.82
  7.5 1.9 %collective-permute-start = (f32[32,256]{1,0:T(8,128)S(1)}, f32[32,256]{1,0:T(8,128)S(1)}, u32[]{:S(2)}, u32[]{:S(2)}) collective-permute-start(f32[32,256]{1,0:T(8,128)S(1)} %get-tuple-element.33), channel_id=1, source_target_pairs={{0,16},{16,32},{32,48},{48,64},{64,80},{80,96},{96,112},{112,128},... | collective-permute-start | bytes 98312 | tf_op jit(solution)/shard_map/ppermute | solution.py:23
  9.4 3.3 %collective-permute-done = f32[32,256]{1,0:T(8,128)S(1)} collective-permute-done((f32[32,256]{1,0:T(8,128)S(1)}, f32[32,256]{1,0:T(8,128)S(1)}, u32[]{:S(2)}, u32[]{:S(2)}) %collective-permute-start) | collective-permute-done | bytes 32800 | tf_op jit(solution)/shard_map/ppermute | solution.py:23
  12.7 0.8 pad_maximum_fusion.2
  13.5 5.2 %collective-permute-start.11 = (f32[32,1024]{1,0:T(8,128)S(1)}, f32[32,1024]{1,0:T(8,128)S(1)}, u32[]{:S(2)}, u32[]{:S(2)}) collective-permute-start(f32[32,1024]{1,0:T(8,128)S(1)} %pad_maximum_fusion.2), channel_id=1, source_target_pairs={{0,0},{1,16},{2,32},{3,48},{4,64},{5,80},{6,96},{7,112},{8,128},{9... | collective-permute-start | bytes 393224 | tf_op jit(solution)/shard_map/ppermute | solution.py:28
  18.7 4.0 %collective-permute-done.11 = f32[32,1024]{1,0:T(8,128)S(1)} collective-permute-done((f32[32,1024]{1,0:T(8,128)S(1)}, f32[32,1024]{1,0:T(8,128)S(1)}, u32[]{:S(2)}, u32[]{:S(2)}) %collective-permute-start.11) | collective-permute-done | bytes 131104 | tf_op jit(solution)/shard_map/ppermute | solution.py:28
  22.7 0.7 copy-done.15
  23.4 14.7 %collective-permute-start.1 = (f32[32,1024]{1,0:T(8,128)S(1)}, f32[32,1024]{1,0:T(8,128)S(1)}, u32[]{:S(2)}, u32[]{:S(2)}) collective-permute-start(f32[32,1024]{1,0:T(8,128)S(1)} %pad_maximum_fusion.2), channel_id=1, source_target_pairs={{0,4},{1,5},{2,6},{3,7},{4,8},{5,9},{6,10},{7,11},{8,12},{9,13},{1... | collective-permute-start | bytes 393224 | tf_op jit(solution)/shard_map/ppermute | solution.py:23
  38.2 1.9 %collective-permute-start.3 = (f32[32,1024]{1,0:T(8,128)S(1)}, f32[32,1024]{1,0:T(8,128)S(1)}, u32[]{:S(2)}, u32[]{:S(2)}) collective-permute-start(f32[32,1024]{1,0:T(8,128)S(1)} %pad_maximum_fusion.2), channel_id=1, source_target_pairs={{0,12},{1,13},{2,14},{3,15},{4,0},{5,1},{6,2},{7,3},{8,4},{9,5},{1... | collective-permute-start | bytes 393224 | tf_op jit(solution)/shard_map/ppermute | solution.py:23
  40.1 2.9 %collective-permute-done.1 = f32[32,1024]{1,0:T(8,128)S(1)} collective-permute-done((f32[32,1024]{1,0:T(8,128)S(1)}, f32[32,1024]{1,0:T(8,128)S(1)}, u32[]{:S(2)}, u32[]{:S(2)}) %collective-permute-start.1) | collective-permute-done | bytes 131104 | tf_op jit(solution)/shard_map/ppermute | solution.py:23
  43.0 6.5 %collective-permute-start.2 = (f32[16,1024]{1,0:T(8,128)S(1)}, f32[16,1024]{1,0:T(8,128)S(1)}, u32[]{:S(2)}, u32[]{:S(2)}) collective-permute-start(f32[16,1024]{1,0:T(8,128)S(1)} %slice.199), channel_id=1, source_target_pairs={{0,4},{1,5},{2,6},{3,7},{4,8},{5,9},{6,10},{7,11},{8,12},{9,13},{1... | collective-permute-start | bytes 196616 | tf_op jit(solution)/shard_map/ppermute | solution.py:23
  49.6 1.3 collective-permute-done.3
  50.9 1.9 %collective-permute-start.4 = (f32[16,1024]{1,0:T(8,128)S(1)}, f32[16,1024]{1,0:T(8,128)S(1)}, u32[]{:S(2)}, u32[]{:S(2)}) collective-permute-start(f32[16,1024]{1,0:T(8,128)S(1)} %slice.200), channel_id=1, source_target_pairs={{0,12},{1,13},{2,14},{3,15},{4,0},{5,1},{6,2},{7,3},{8,4},{9,5},{1... | collective-permute-start | bytes 196616 | tf_op jit(solution)/shard_map/ppermute | solution.py:23
  52.9 6.5 %collective-permute-done.4 = f32[16,1024]{1,0:T(8,128)S(1)} collective-permute-done((f32[16,1024]{1,0:T(8,128)S(1)}, f32[16,1024]{1,0:T(8,128)S(1)}, u32[]{:S(2)}, u32[]{:S(2)}) %collective-permute-start.4) | collective-permute-done | bytes 65568 | tf_op jit(solution)/shard_map/ppermute | solution.py:23
  59.4 0.9 constant_dynamic-update-slice_fusion.1
  60.4 2.9 %collective-permute-start.7 = (f32[128,1024]{1,0:T(8,128)S(1)}, f32[128,1024]{1,0:T(8,128)S(1)}, u32[]{:S(2)}, u32[]{:S(2)}) collective-permute-start(f32[128,1024]{1,0:T(8,128)S(1)} %bitcast.45), channel_id=1, source_target_pairs={{0,3},{1,0},{2,1},{3,2},{4,7},{5,4},{6,5},{7,6},{8,11},{9,8},{10,9... | collective-permute-start | bytes 1572872 | tf_op jit(solution)/shard_map/ppermute | solution.py:23
  63.2 4.2 %collective-permute-start.5 = (f32[128,1024]{1,0:T(8,128)S(1)}, f32[128,1024]{1,0:T(8,128)S(1)}, u32[]{:S(2)}, u32[]{:S(2)}) collective-permute-start(f32[128,1024]{1,0:T(8,128)S(1)} %bitcast.46), channel_id=1, source_target_pairs={{0,1},{1,2},{2,3},{3,0},{4,5},{5,6},{6,7},{7,4},{8,9},{9,10},{10,1... | collective-permute-start | bytes 1572872 | tf_op jit(solution)/shard_map/ppermute | solution.py:23
  67.4 1.6 fusion.80
  69.1 7.8 %collective-permute-done.7 = f32[128,1024]{1,0:T(8,128)S(1)} collective-permute-done((f32[128,1024]{1,0:T(8,128)S(1)}, f32[128,1024]{1,0:T(8,128)S(1)}, u32[]{:S(2)}, u32[]{:S(2)}) %collective-permute-start.7) | collective-permute-done | bytes 524320 | tf_op jit(solution)/shard_map/ppermute | solution.py:23
  76.9 0.8 slice.202
  77.7 1.9 %collective-permute-start.8 = (f32[64,1024]{1,0:T(8,128)}, f32[64,1024]{1,0:T(8,128)S(1)}, u32[]{:S(2)}, u32[]{:S(2)}) collective-permute-start(f32[64,1024]{1,0:T(8,128)} %slice.202), channel_id=1, source_target_pairs={{0,3},{1,0},{2,1},{3,2},{4,7},{5,4},{6,5},{7,6},{8,11},{9,8},{10,9... | collective-permute-start | bytes 786440 | tf_op jit(solution)/shard_map/ppermute | solution.py:23
  79.6 0.8 slice.201
  80.4 5.1 %collective-permute-start.6 = (f32[64,1024]{1,0:T(8,128)}, f32[64,1024]{1,0:T(8,128)}, u32[]{:S(2)}, u32[]{:S(2)}) collective-permute-start(f32[64,1024]{1,0:T(8,128)} %slice.201), channel_id=1, source_target_pairs={{0,1},{1,2},{2,3},{3,0},{4,5},{5,6},{6,7},{7,4},{8,9},{9,10},{10,1... | collective-permute-start | bytes 786440 | tf_op jit(solution)/shard_map/ppermute | solution.py:23
  85.6 0.2 copy_bitcast_fusion
  85.8 0.4 slice-done
  86.2 0.7 constant_dynamic-slice_fusion.2
  87.6 2.4 %collective-permute-done.6 = f32[64,1024]{1,0:T(8,128)} collective-permute-done((f32[64,1024]{1,0:T(8,128)}, f32[64,1024]{1,0:T(8,128)}, u32[]{:S(2)}, u32[]{:S(2)}) %collective-permute-start.6) | collective-permute-done | bytes 262176 | tf_op jit(solution)/shard_map/ppermute | solution.py:23
  90.0 1.0 constant_dynamic-update-slice_fusion.9
  91.0 1.1 constant_dynamic-update-slice_fusion.7
  92.2 0.5 fusion
  92.7 0.2 copy.27
  93.0 1.3 copy-done.2
  94.3 1.9 %fusion.1 = f32[512,1024]{1,0:T(8,128)S(1)} fusion(f32[512,512]{1,0:T(8,128)S(1)} %get-tuple-element.45, f32[512,512]{1,0:T(8,128)S(1)} %get-tuple-element.46, f32[512,1024]{1,0:T(8,128)S(1)} %bitcast.39), kind=kOutput, calls=%fused_computation.3 | convolution fusion | flops 1611137024 | bytes 5242880 | tf_op jit(solution)/shard_map/dot_general | solution.py:15
  96.3 0.5 slice_select_fusion.1
  96.8 1.5 fusion.19
  98.3 1.9 %collective-permute-start.10 = (f32[256,1024]{1,0:T(8,128)}, f32[256,1024]{1,0:T(8,128)S(1)}, u32[]{:S(2)}, u32[]{:S(2)}) collective-permute-start(f32[256,1024]{1,0:T(8,128)} %get-tuple-element.17), channel_id=1, source_target_pairs={{16,0},{17,1},{18,2},{19,3},{20,4},{21,5},{22,6},{23,7},{24,8},{25... | collective-permute-start | bytes 3145736 | tf_op jit(solution)/shard_map/ppermute | solution.py:28
  100.3 0.7 fusion.83
  106.3 0.6 slice.230
  106.9 0.6 slice.219
  107.5 2.4 %collective-permute-start.9 = (f32[256,1024]{1,0:T(8,128)}, f32[256,1024]{1,0:T(8,128)}, u32[]{:S(2)}, u32[]{:S(2)}) collective-permute-start(f32[256,1024]{1,0:T(8,128)} %get-tuple-element.16), channel_id=1, source_target_pairs={{0,16},{1,17},{2,18},{3,19},{4,20},{5,21},{6,22},{7,23},{8,24},{9,... | collective-permute-start | bytes 3145736 | tf_op jit(solution)/shard_map/ppermute | solution.py:28
  111.1 2.2 %collective-permute-done.10 = f32[256,1024]{1,0:T(8,128)S(1)} collective-permute-done((f32[256,1024]{1,0:T(8,128)}, f32[256,1024]{1,0:T(8,128)S(1)}, u32[]{:S(2)}, u32[]{:S(2)}) %collective-permute-start.10) | collective-permute-done | bytes 1048608 | tf_op jit(solution)/shard_map/ppermute | solution.py:28
  113.4 0.7 fusion.81
  115.3 0.9 slice_multiply_fusion.1
  116.3 0.6 copy-done.3
  117.0 2.4 %fusion.11 = f32[256,1024]{1,0:T(8,128)S(1)} fusion(f32[256,512]{1,0:T(8,128)S(1)} %get-tuple-element.31, f32[256,512]{1,0:T(8,128)S(1)} %get-tuple-element.30, f32[256,1024]{1,0:T(8,128)} %get-tuple-element.16, f32[512,1024]{1,0:T(8,128)S(1)} %bitcast.41), kind=kOutput, calls=%fused_computation.15 | convolution fusion | flops 806354944 | bytes 3670016 | tf_op jit(solution)/shard_map/dot_general | solution.py:15
  119.3 1.3 slice_select_fusion.11
  120.7 3.2 %collective-permute-done.9 = f32[256,1024]{1,0:T(8,128)} collective-permute-done((f32[256,1024]{1,0:T(8,128)}, f32[256,1024]{1,0:T(8,128)}, u32[]{:S(2)}, u32[]{:S(2)}) %collective-permute-start.9) | collective-permute-done | bytes 1048608 | tf_op jit(solution)/shard_map/ppermute | solution.py:28
  123.9 2.4 %fusion.5 = f32[256,1024]{1,0:T(8,128)S(1)} fusion(f32[256,512]{1,0:T(8,128)S(1)} %get-tuple-element.28, f32[256,512]{1,0:T(8,128)S(1)} %get-tuple-element.29, f32[256,1024]{1,0:T(8,128)} %collective-permute-done.9, f32[512,1024]{1,0:T(8,128)S(1)} %bitcast.42), kind=kOutput, calls=%fused_computation.9 | convolution fusion | flops 806354944 | bytes 3670016 | tf_op jit(solution)/shard_map/dot_general | solution.py:15
  126.3 1.2 broadcast_select_fusion.1
  127.6 1.8 fusion.18
  129.4 0.7 collective-permute-start.12
  130.1 1.6 convolution_select_fusion.6
  131.7 1.0 collective-permute-start.14
  132.8 0.6 convolution_select_fusion.4
  133.4 1.9 %collective-permute-start.13 = (f32[512,256]{1,0:T(8,128)S(1)}, f32[512,256]{1,0:T(8,128)S(1)}, u32[]{:S(2)}, u32[]{:S(2)}) collective-permute-start(f32[512,256]{1,0:T(8,128)S(1)} %convolution_select_fusion.4), channel_id=1, source_target_pairs={{0,15},{1,0},{2,1},{3,2},{4,3},{5,4},{6,5},{7,6},{8,7},{9,8},{10,9... | collective-permute-start | bytes 1572872 | tf_op jit(solution)/shard_map/ppermute | solution.py:28
  135.3 0.6 fusion.17
  135.9 8.1 %collective-permute-start.15 = (f32[512,256]{1,0:T(8,128)S(1)}, f32[512,256]{1,0:T(8,128)S(1)}, u32[]{:S(2)}, u32[]{:S(2)}) collective-permute-start(f32[512,256]{1,0:T(8,128)S(1)} %fusion.17), channel_id=1, source_target_pairs={{0,1},{1,2},{2,3},{3,4},{4,5},{5,6},{6,7},{7,8},{8,9},{9,10},{10,1... | collective-permute-start | bytes 1572872 | tf_op jit(solution)/shard_map/ppermute | solution.py:28
  144.1 0.6 convolution_select_fusion.5
  144.7 31.6 %collective-permute-done.13 = f32[512,256]{1,0:T(8,128)S(1)} collective-permute-done((f32[512,256]{1,0:T(8,128)S(1)}, f32[512,256]{1,0:T(8,128)S(1)}, u32[]{:S(2)}, u32[]{:S(2)}) %collective-permute-start.13) | collective-permute-done | bytes 524320 | tf_op jit(solution)/shard_map/ppermute | solution.py:28
  176.4 0.6 convolution_select_fusion.3
  177.1 0.6 convolution_select_fusion
  177.8 0.6 convolution_select_fusion.1
  178.6 0.2 pad_maximum_fusion
  178.8 2.9 %copy.38 = f32[512,2,512]{2,1,0:T(2,128)} copy(f32[512,2,512]{2,0,1:T(8,128)S(1)} %pad_maximum_fusion) | data formatting | bytes 4194304 | tf_op jit(solution)/shard_map/stack | solution.py:155
  (65 shorter events, 0.9 us)
Async XLA Ops:
  6.5 60.9 %copy-start.9 = (f32[512,2,512]{2,1,0:T(2,128)S(1)}, f32[512,2,512]{2,1,0:T(2,128)}, u32[]{:S(2)}) copy-start(f32[512,2,512]{2,1,0:T(2,128)} %param.4) | copy-start | bytes 6291460
  6.5 121.0 %all-gather.2.cloned.1.call-start = ((), (), s32[]{:S(2)}) async-start(), calls=%async_computation | async-start | bytes 4325376 | tf_op jit(solution)/shard_map/all_gather | solution.py:69
  7.5 5.2 %collective-permute-start = (f32[32,256]{1,0:T(8,128)S(1)}, f32[32,256]{1,0:T(8,128)S(1)}, u32[]{:S(2)}, u32[]{:S(2)}) collective-permute-start(f32[32,256]{1,0:T(8,128)S(1)} %get-tuple-element.33), channel_id=1, source_target_pairs={{0,16},{16,32},{32,48},{48,64},{64,80},{80,96},{96,112},{112,128},... | collective-permute-start | bytes 98312 | tf_op jit(solution)/shard_map/ppermute | solution.py:23
  13.5 9.2 %collective-permute-start.11 = (f32[32,1024]{1,0:T(8,128)S(1)}, f32[32,1024]{1,0:T(8,128)S(1)}, u32[]{:S(2)}, u32[]{:S(2)}) collective-permute-start(f32[32,1024]{1,0:T(8,128)S(1)} %pad_maximum_fusion.2), channel_id=1, source_target_pairs={{0,0},{1,16},{2,32},{3,48},{4,64},{5,80},{6,96},{7,112},{8,128},{9... | collective-permute-start | bytes 393224 | tf_op jit(solution)/shard_map/ppermute | solution.py:28
  22.7 0.7 copy-start.15
  23.4 19.6 %collective-permute-start.1 = (f32[32,1024]{1,0:T(8,128)S(1)}, f32[32,1024]{1,0:T(8,128)S(1)}, u32[]{:S(2)}, u32[]{:S(2)}) collective-permute-start(f32[32,1024]{1,0:T(8,128)S(1)} %pad_maximum_fusion.2), channel_id=1, source_target_pairs={{0,4},{1,5},{2,6},{3,7},{4,8},{5,9},{6,10},{7,11},{8,12},{9,13},{1... | collective-permute-start | bytes 393224 | tf_op jit(solution)/shard_map/ppermute | solution.py:23
  38.2 12.8 %collective-permute-start.3 = (f32[32,1024]{1,0:T(8,128)S(1)}, f32[32,1024]{1,0:T(8,128)S(1)}, u32[]{:S(2)}, u32[]{:S(2)}) collective-permute-start(f32[32,1024]{1,0:T(8,128)S(1)} %pad_maximum_fusion.2), channel_id=1, source_target_pairs={{0,12},{1,13},{2,14},{3,15},{4,0},{5,1},{6,2},{7,3},{8,4},{9,5},{1... | collective-permute-start | bytes 393224 | tf_op jit(solution)/shard_map/ppermute | solution.py:23
  43.0 9.9 %collective-permute-start.2 = (f32[16,1024]{1,0:T(8,128)S(1)}, f32[16,1024]{1,0:T(8,128)S(1)}, u32[]{:S(2)}, u32[]{:S(2)}) collective-permute-start(f32[16,1024]{1,0:T(8,128)S(1)} %slice.199), channel_id=1, source_target_pairs={{0,4},{1,5},{2,6},{3,7},{4,8},{5,9},{6,10},{7,11},{8,12},{9,13},{1... | collective-permute-start | bytes 196616 | tf_op jit(solution)/shard_map/ppermute | solution.py:23
  50.9 8.4 %collective-permute-start.4 = (f32[16,1024]{1,0:T(8,128)S(1)}, f32[16,1024]{1,0:T(8,128)S(1)}, u32[]{:S(2)}, u32[]{:S(2)}) collective-permute-start(f32[16,1024]{1,0:T(8,128)S(1)} %slice.200), channel_id=1, source_target_pairs={{0,12},{1,13},{2,14},{3,15},{4,0},{5,1},{6,2},{7,3},{8,4},{9,5},{1... | collective-permute-start | bytes 196616 | tf_op jit(solution)/shard_map/ppermute | solution.py:23
  60.4 8.7 %copy-start.10 = (f32[4,32,1024]{2,1,0:T(8,128)}, f32[4,32,1024]{2,1,0:T(8,128)S(1)}, u32[]{:S(2)}) copy-start(f32[4,32,1024]{2,1,0:T(8,128)S(1)} %fusion.45) | copy-start | bytes 1572868
  60.4 16.5 %collective-permute-start.7 = (f32[128,1024]{1,0:T(8,128)S(1)}, f32[128,1024]{1,0:T(8,128)S(1)}, u32[]{:S(2)}, u32[]{:S(2)}) collective-permute-start(f32[128,1024]{1,0:T(8,128)S(1)} %bitcast.45), channel_id=1, source_target_pairs={{0,3},{1,0},{2,1},{3,2},{4,7},{5,4},{6,5},{7,6},{8,11},{9,8},{10,9... | collective-permute-start | bytes 1572872 | tf_op jit(solution)/shard_map/ppermute | solution.py:23
  63.2 16.4 %collective-permute-start.5 = (f32[128,1024]{1,0:T(8,128)S(1)}, f32[128,1024]{1,0:T(8,128)S(1)}, u32[]{:S(2)}, u32[]{:S(2)}) collective-permute-start(f32[128,1024]{1,0:T(8,128)S(1)} %bitcast.46), channel_id=1, source_target_pairs={{0,1},{1,2},{2,3},{3,0},{4,5},{5,6},{6,7},{7,4},{8,9},{9,10},{10,1... | collective-permute-start | bytes 1572872 | tf_op jit(solution)/shard_map/ppermute | solution.py:23
  69.1 16.5 %copy-start = (f32[512,1,512]{2,1,0:T(1,128)}, f32[512,1,512]{2,1,0:T(1,128)S(1)}, u32[]{:S(2)}) copy-start(f32[512,1,512]{2,1,0:T(1,128)S(1)} %get-tuple-element.21) | copy-start | bytes 3145732
  76.9 8.6 %copy-start.12 = (f32[128,1024]{1,0:T(8,128)}, f32[128,1024]{1,0:T(8,128)S(1)}, u32[]{:S(2)}) copy-start(f32[128,1024]{1,0:T(8,128)S(1)} %collective-permute-done.7) | copy-start | bytes 1572868
  77.7 13.2 %collective-permute-start.8 = (f32[64,1024]{1,0:T(8,128)}, f32[64,1024]{1,0:T(8,128)S(1)}, u32[]{:S(2)}, u32[]{:S(2)}) collective-permute-start(f32[64,1024]{1,0:T(8,128)} %slice.202), channel_id=1, source_target_pairs={{0,3},{1,0},{2,1},{3,2},{4,7},{5,4},{6,5},{7,6},{8,11},{9,8},{10,9... | collective-permute-start | bytes 786440 | tf_op jit(solution)/shard_map/ppermute | solution.py:23
  79.6 5.9 %copy-start.14 = (f32[128,1024]{1,0:T(8,128)}, f32[128,1024]{1,0:T(8,128)S(1)}, u32[]{:S(2)}) copy-start(f32[128,1024]{1,0:T(8,128)S(1)} %collective-permute-done.5) | copy-start | bytes 1572868
  80.4 9.6 %collective-permute-start.6 = (f32[64,1024]{1,0:T(8,128)}, f32[64,1024]{1,0:T(8,128)}, u32[]{:S(2)}, u32[]{:S(2)}) collective-permute-start(f32[64,1024]{1,0:T(8,128)} %slice.201), channel_id=1, source_target_pairs={{0,1},{1,2},{2,3},{3,0},{4,5},{5,6},{6,7},{7,4},{8,9},{9,10},{10,1... | collective-permute-start | bytes 786440 | tf_op jit(solution)/shard_map/ppermute | solution.py:23
  85.6 0.7 slice-start
  87.6 4.5 %copy-start.11 = (f32[4,32,1024]{2,1,0:T(8,128)S(1)}, f32[4,32,1024]{2,1,0:T(8,128)}, u32[]{:S(2)}) copy-start(f32[4,32,1024]{2,1,0:T(8,128)} %copy-done.10) | copy-start | bytes 1572868
  87.6 4.6 %copy-start.13 = (f32[128,1024]{1,0:T(8,128)S(1)}, f32[128,1024]{1,0:T(8,128)}, u32[]{:S(2)}) copy-start(f32[128,1024]{1,0:T(8,128)} %copy-done.12) | copy-start | bytes 1572868
  93.0 1.3 copy-start.2
  94.3 1.9 %copy-start.1 = (f32[512,1,512]{2,1,0:T(1,128)S(1)}, f32[512,1,512]{2,1,0:T(1,128)}, u32[]{:S(2)}) copy-start(f32[512,1,512]{2,1,0:T(1,128)} %copy-done) | copy-start | bytes 3145732
  96.7 3.5 %copy-start.16 = (s32[2,32]{1,0:T(2,128)S(1)}, s32[2,32]{1,0:T(2,128)}, u32[]{:S(2)}) copy-start(s32[2,32]{1,0:T(2,128)} %param.7) | copy-start | bytes 772
  98.3 15.1 %collective-permute-start.10 = (f32[256,1024]{1,0:T(8,128)}, f32[256,1024]{1,0:T(8,128)S(1)}, u32[]{:S(2)}, u32[]{:S(2)}) collective-permute-start(f32[256,1024]{1,0:T(8,128)} %get-tuple-element.17), channel_id=1, source_target_pairs={{16,0},{17,1},{18,2},{19,3},{20,4},{21,5},{22,6},{23,7},{24,8},{25... | collective-permute-start | bytes 3145736 | tf_op jit(solution)/shard_map/ppermute | solution.py:28
  107.5 16.4 %collective-permute-start.9 = (f32[256,1024]{1,0:T(8,128)}, f32[256,1024]{1,0:T(8,128)}, u32[]{:S(2)}, u32[]{:S(2)}) collective-permute-start(f32[256,1024]{1,0:T(8,128)} %get-tuple-element.16), channel_id=1, source_target_pairs={{0,16},{1,17},{2,18},{3,19},{4,20},{5,21},{6,22},{7,23},{8,24},{9,... | collective-permute-start | bytes 3145736 | tf_op jit(solution)/shard_map/ppermute | solution.py:28
  115.3 1.6 copy-start.3
  126.3 1.3 copy-start.5
  127.5 2.5 %copy-start.4 = (f32[256,512]{1,0:T(8,128)S(1)}, f32[256,512]{1,0:T(8,128)}, u32[]{:S(2)}) copy-start(f32[256,512]{1,0:T(8,128)} %get-tuple-element.7) | copy-start | bytes 1572868
  127.6 2.5 %copy-start.7 = (f32[256,512]{1,0:T(8,128)S(1)}, f32[256,512]{1,0:T(8,128)}, u32[]{:S(2)}) copy-start(f32[256,512]{1,0:T(8,128)} %get-tuple-element.5) | copy-start | bytes 1572868
  127.6 5.2 %copy-start.8 = (f32[1024,1024]{1,0:T(8,128)S(1)}, f32[1024,1024]{1,0:T(8,128)}, u32[]{:S(2)}) copy-start(f32[1024,1024]{1,0:T(8,128)} %all-gather.2.cloned.1.call-done) | copy-start | bytes 12582916
  129.4 14.7 %collective-permute-start.12 = (f32[512,256]{1,0:T(8,128)S(1)}, f32[512,256]{1,0:T(8,128)S(1)}, u32[]{:S(2)}, u32[]{:S(2)}) collective-permute-start(f32[512,256]{1,0:T(8,128)S(1)} %fusion.18), channel_id=1, source_target_pairs={{0,1},{1,2},{2,3},{3,4},{4,5},{5,6},{6,7},{7,8},{8,9},{9,10},{10,1... | collective-permute-start | bytes 1572872 | tf_op jit(solution)/shard_map/ppermute | solution.py:28
  131.7 3.6 %copy-start.6 = (f32[256,512]{1,0:T(8,128)S(1)}, f32[256,512]{1,0:T(8,128)}, u32[]{:S(2)}) copy-start(f32[256,512]{1,0:T(8,128)} %get-tuple-element.25) | copy-start | bytes 1572868
  131.7 12.9 %collective-permute-start.14 = (f32[512,256]{1,0:T(8,128)S(1)}, f32[512,256]{1,0:T(8,128)S(1)}, u32[]{:S(2)}, u32[]{:S(2)}) collective-permute-start(f32[512,256]{1,0:T(8,128)S(1)} %convolution_select_fusion.6), channel_id=1, source_target_pairs={{1,0},{2,1},{3,2},{4,3},{5,4},{6,5},{7,6},{8,7},{9,8},{10,9},{11,1... | collective-permute-start | bytes 1572872 | tf_op jit(solution)/shard_map/ppermute | solution.py:28
  133.4 42.9 %collective-permute-start.13 = (f32[512,256]{1,0:T(8,128)S(1)}, f32[512,256]{1,0:T(8,128)S(1)}, u32[]{:S(2)}, u32[]{:S(2)}) collective-permute-start(f32[512,256]{1,0:T(8,128)S(1)} %convolution_select_fusion.4), channel_id=1, source_target_pairs={{0,15},{1,0},{2,1},{3,2},{4,3},{5,4},{6,5},{7,6},{8,7},{9,8},{10,9... | collective-permute-start | bytes 1572872 | tf_op jit(solution)/shard_map/ppermute | solution.py:28
  135.9 41.8 %collective-permute-start.15 = (f32[512,256]{1,0:T(8,128)S(1)}, f32[512,256]{1,0:T(8,128)S(1)}, u32[]{:S(2)}, u32[]{:S(2)}) collective-permute-start(f32[512,256]{1,0:T(8,128)S(1)} %fusion.17), channel_id=1, source_target_pairs={{0,1},{1,2},{2,3},{3,4},{4,5},{5,6},{6,7},{7,8},{8,9},{9,10},{10,1... | collective-permute-start | bytes 1572872 | tf_op jit(solution)/shard_map/ppermute | solution.py:28
Sparse Core Ops, SparseCore 0:
  23.5 83.7 all-gather.1

commit v2 on v1

v2 whole, which is shorter than its diff:
```python
import functools

import jax
import jax.numpy as jnp
from jax import lax
from jax.experimental import pallas as pl
from jax.experimental.pallas import tpu as pltpu
from jax.sharding import PartitionSpec as P

GRID_ROWS, GRID_COLS = 32, 16
RING = 4
W = 512
HALF = 256
LAST = 31
BF16, F32 = jnp.bfloat16, jnp.float32
PARAMS = pltpu.CompilerParams(vmem_limit_bytes=28 * 1024 * 1024)
VMEM = pl.BlockSpec(memory_space=pltpu.VMEM)
SMEM = pl.BlockSpec(memory_space=pltpu.SMEM)


def split(x):
    high = x.astype(BF16)
    return high, (x - high.astype(F32)).astype(BF16)


def product(a, b, contract):
    dims = (contract, ((), ()))
    one = lambda x, y: lax.dot_general(x, y, dims, preferred_element_type=F32)
    return one(a[0], b[0]) + (one(a[0], b[1]) + one(a[1], b[0]))


def live(ref, kind, index):
    inside = (index >= 0) & (index <= LAST - kind)
    return inside & (ref[kind, jnp.clip(index, 0, LAST)] == 1)


def moved(value, axis, target):
    count = lax.axis_size(axis)
    pairs = [(i, target(i)) for i in range(count)]
    return lax.ppermute(value, axis, [(i, j) for i, j in pairs if 0 <= j < count])


def moved_on(value, pairs):
    return lax.ppermute(
        value, ("row", "col"), [(r * GRID_COLS + c, t * GRID_COLS + d) for (r, c), (t, d) in pairs]
    )


def everywhere(test, target):
    return [((r, c), target(r, c)) for r in range(GRID_ROWS) for c in range(GRID_COLS) if test(r, c)]


def swapped(value, pairs):
    return moved_on(value, pairs + [(b, a) for a, b in pairs])


def joined(far_a, far_b, behind, own, ahead, out):
    for index, part in enumerate((far_a, far_b)):
        out[index * 16 : index * 16 + 16] = part[...]
    for index, part in enumerate((behind, own, ahead)):
        out[32 * index + 32 : 32 * index + 64] = part[...]


def left_kernel(where, lives, own, behind, ahead, far_a, far_b, h0, h1, send_a, send_b, fb_high, fb_low, d_high, d_low):
    row, col = where[0], where[1]
    ring_y, ring_x = col // RING, col % RING

    def place(ref, rows, x_off, y_offs):
        for index, y_off in enumerate(y_offs):
            at_y = lax.rem(ring_y + y_off + RING, RING)
            at_x = lax.rem(ring_x + x_off + RING, RING)
            start = pl.multiple_of((at_y * RING + at_x) * 32, 32)
            part = ref[rows + 32 * index : rows + 32 * index + 32, :]
            high, low = split(part)
            for side in range(2):
                lanes = slice(W + side * HALF, W + side * HALF + HALF)
                fb_high[side, pl.ds(start, 32), :] = high[:, lanes]
                fb_low[side, pl.ds(start, 32), :] = low[:, lanes]
            d_high[pl.ds(start, 32), :] = high[:, :W]
            d_low[pl.ds(start, 32), :] = low[:, :W]

    place(own, 0, 0, (-2, -1, 0, 1))
    place(behind, 0, -1, (-2, -1, 0, 1))
    place(ahead, 0, 1, (-2, -1, 0, 1))
    place(far_a, 0, 2, (-2, -1))
    place(far_b, 0, 2, (0, 1))
    odd = lax.rem(row, 2) == 1
    live_row = live(lives, 0, row)
    factor = (d_high[...], d_low[...])
    for s, h in enumerate((h0, h1)):
        lanes = slice(s * W, s * W + W)
        value = h[...]
        turned = product(factor, split(value), ((0,), (0,)))
        value = jnp.where((col + GRID_COLS * s >= row) & live_row, turned, value)
        send_a[:, lanes] = jnp.where(odd, value[:HALF], value[HALF:])
        send_b[:, lanes] = jnp.where(odd, value[HALF:], value[:HALF])


def prepare_kernel(gathered, high, low):
    value = gathered[...].reshape(high.shape[1], high.shape[2])
    high[0], low[0] = split(value)


def middle_kernel(first, where, lives, own, got, fb_high, fb_low, c_high, c_low, kept, side, edge0, edge1):
    row, col = where[0], where[1]
    odd = lax.rem(row, 2) == 1
    top = odd if first else ~odd
    top_index = top.astype(jnp.int32)
    active = live(lives, 1, jnp.where(top, row - 1, row))
    factor = (fb_high[top_index], fb_low[top_index])
    below_part = (fb_high[top_index, HALF:, :], fb_low[top_index, HALF:, :])
    odd_col = lax.rem(col, 2) == 1
    is_corner = (lax.broadcasted_iota(jnp.int32, (HALF, 128), 0) == 0) & (
        lax.broadcasted_iota(jnp.int32, (HALF, 128), 1) == 127
    )
    ends = []
    for s in range(2):
        lanes = slice(s * W, s * W + W)
        tile = col + GRID_COLS * s
        own_raw, got_raw = own[:, lanes], got[:, lanes]
        own_value = jnp.where(top & (tile < row), 0.0, own_raw)
        got_value = jnp.where(top | (tile > row), got_raw, 0.0)
        acted = active & (tile >= jnp.where(top, row - 1, row))
        upper, lower = jnp.where(top, got_value, own_value), jnp.where(top, own_value, got_value)
        rows = product(factor, split(jnp.concatenate([upper, lower], 0)), ((0,), (0,)))
        value = jnp.where(acted, rows, own_value)
        for_left = jnp.where(top, jnp.where(tile >= row, value, 0.0), jnp.where(tile == row, own_value, value))
        turns = live(lives, 0, tile)
        matrix = lambda a, b: (c_high[s, :, a:b], c_low[s, :, a:b])
        left = product(split(for_left), matrix(0, HALF), ((1,), (0,)))
        right = product(split(value), matrix(HALF, W), ((1,), (0,)))
        left = jnp.where(turns, left, for_left[:, :HALF])
        right = jnp.where(turns, right, value[:, HALF:])
        kept[2 * s] = left
        kept[2 * s + 1] = right
        has_corner = (top & (tile == row - 1)) | (~top & (tile == row) & acted)
        corner = jnp.where(has_corner & is_corner, jnp.where(top, own_raw[:, W - 128 :], got_raw[:, W - 128 :]), 0.0)
        spread = jnp.where(acted, product(below_part, split(corner), ((0,), (0,))), corner)
        kept[2 * s + 1, :, HALF - 128 :] = kept[2 * s + 1, :, HALF - 128 :] + spread
        right = kept[2 * s + 1]
        side[s] = jnp.where(odd_col, left, right)
        ends.append((left, right))
    crosses = col == 0
    edge0[...] = jnp.where(odd_col, ends[0][1], jnp.where(crosses, ends[1][0], ends[0][0]))
    edge1[...] = jnp.where(odd_col, ends[1][1], ends[1][0])


def last_kernel(first, where, lives, kept, side, edge0, edge1, c_high, c_low, *rest):
    out = rest[-1]
    row, col = where[0], where[1]
    odd = lax.rem(row, 2) == 1
    top = odd if first else ~odd
    odd_col = lax.rem(col, 2) == 1
    for s in range(2):
        tile = col + GRID_COLS * s
        left, right = kept[2 * s], kept[2 * s + 1]
        near = side[s]
        far = (edge0 if s == 0 else edge1)[...]
        if s == 1:
            far = jnp.where(col == 0, edge0[...], far)
        pairs = (
            (jnp.where(odd_col, near, far), left, W + HALF, live(lives, 1, tile - 1) & ((row < tile) | ((row == tile) & top))),
            (right, jnp.where(odd_col, far, near), W, live(lives, 1, tile) & ((row <= tile) | ((row == tile + 1) & top))),
        )
        for index, (one, two, at, keep) in enumerate(pairs):
            factor = (c_high[s, :, at : at + HALF], c_low[s, :, at : at + HALF])
            value = product(split(jnp.concatenate([one, two], 1)), factor, ((1,), (0,)))
            value = jnp.where(keep, value, two if index == 0 else one)
            out[:, s, index * HALF : index * HALF + HALF] = value


def shards(hessenberg, diag_factors, border_factors, window_live):
    row = lax.axis_index("row")
    col = lax.axis_index("col")
    where = jnp.stack([row, col]).astype(jnp.int32)
    shape = jax.ShapeDtypeStruct

    border = border_factors[0]
    above = moved(border[:, HALF:], "row", lambda r: r + 1)
    piece = jnp.concatenate([diag_factors[0], border[:, :HALF], above], 1)

    mine = moved_on(piece, everywhere(lambda r, c: True, lambda r, c: (r // 16 * 16 + c, r % 16)))
    other = moved_on(piece, everywhere(lambda r, c: True, lambda r, c: (16 - r // 16 * 16 + c, r % 16)))
    lower = row >= 16
    both = jnp.concatenate([jnp.where(lower, other, mine), jnp.where(lower, mine, other)], 0)
    groups = [list(range(16)), list(range(16, 32))]
    gathered = lax.all_gather(both, "row", axis=0, tiled=True, axis_index_groups=groups)
    gathered = gathered.reshape(16, 2, 32, 2 * W)

    along_y = lambda s: (lambda c: (c + RING * s) % GRID_COLS)
    along_x = lambda s: (lambda c: c // RING * RING + (c + s) % RING)
    behind = moved(piece, "col", along_y(1))
    ahead = moved(piece, "col", along_y(-1))
    far_a = moved(behind[:16], "col", along_y(1))
    far_b = moved(ahead[16:], "col", along_y(-1))
    block = pl.pallas_call(
        joined, out_shape=shape((128, 2 * W), F32), in_specs=[VMEM] * 5, out_specs=VMEM, name="joined"
    )(far_a, far_b, behind, piece, ahead)
    behind = moved(block, "col", along_x(1))
    ahead = moved(block, "col", along_x(-1))
    far_a = moved(behind[:64], "col", along_x(1))
    far_b = moved(ahead[64:], "col", along_x(-1))

    send_a, send_b, fb_high, fb_low = pl.pallas_call(
        left_kernel,
        out_shape=[shape((HALF, 2 * W), F32)] * 2 + [shape((2, W, HALF), BF16)] * 2,
        in_specs=[SMEM, SMEM] + [VMEM] * 7,
        out_specs=[VMEM] * 4,
        scratch_shapes=[pltpu.VMEM((W, W), BF16)] * 2,
        compiler_params=PARAMS,
        name="left",
    )(where, window_live, block, behind, ahead, far_a, far_b, hessenberg[:, 0], hessenberg[:, 1])

    every_col = range(GRID_COLS)
    got_b = swapped(send_b, [((r, c), (r + 1, c)) for r in range(1, 31, 2) for c in every_col])
    got_a = swapped(send_a, [((r, c), (r + 1, c)) for r in range(0, 32, 2) for c in every_col])

    c_high, c_low = pl.pallas_call(
        prepare_kernel,
        grid=(2,),
        out_shape=[shape((2, W, 2 * W), BF16)] * 2,
        in_specs=[pl.BlockSpec((16, 1, 32, 2 * W), lambda s: (0, s, 0, 0))],
        out_specs=[pl.BlockSpec((1, W, 2 * W), lambda s: (s, 0, 0))] * 2,
        compiler_params=PARAMS,
        name="prepare",
    )(gathered)

    def middle(first, own, got):
        return pl.pallas_call(
            functools.partial(middle_kernel, first),
            out_shape=[shape((4, HALF, HALF), F32), shape((2, HALF, HALF), F32)] + [shape((HALF, HALF), F32)] * 2,
            in_specs=[SMEM, SMEM] + [VMEM] * 6,
            out_specs=[VMEM] * 4,
            compiler_params=PARAMS,
            name="middle",
        )(where, window_live, own, got, fb_high, fb_low, c_high, c_low)

    def exchanged(side, edge0, edge1):
        rows = range(GRID_ROWS)
        edge1 = swapped(edge1, [((r, c), (r, c + 1)) for r in rows for c in range(1, 15, 2) if r <= c + 17])
        edge0 = swapped(edge0, [((r, c), (r, (c + 1) % 16)) for r in rows for c in range(1, 16, 2) if r <= c + 1])
        side = swapped(side, [((r, c), (r, c + 1)) for r in rows for c in range(0, 16, 2) if r <= c + 17])
        return side, edge0, edge1

    def last(first, kept, moved_parts, *done):
        place = lambda i, where: (lax.rem(where[0], 2) ^ (1 if first else 0), 0, 0)
        whole = lambda shape: pl.BlockSpec(shape, lambda i, where: (0,) * len(shape))
        lives = pl.BlockSpec(memory_space=pltpu.SMEM)
        specs = [
            lives,
            whole((4, HALF, HALF)),
            whole((2, HALF, HALF)),
            whole((HALF, HALF)),
            whole((HALF, HALF)),
            whole((2, W, 2 * W)),
            whole((2, W, 2 * W)),
        ]
        return pl.pallas_call(
            functools.partial(last_kernel, first),
            out_shape=shape((W, 2, W), F32),
            grid_spec=pltpu.PrefetchScalarGridSpec(
                num_scalar_prefetch=1,
                grid=(1,),
                in_specs=specs + [pl.BlockSpec(memory_space=pl.ANY)] * len(done),
                out_specs=pl.BlockSpec((HALF, 2, W), place),
            ),
            input_output_aliases={8: 0} if done else {},
            compiler_params=PARAMS,
            name="last",
        )(where, window_live, kept, *moved_parts, c_high, c_low, *done)

    kept_a, *ends_a = middle(True, send_a, got_a)
    parts_a = exchanged(*ends_a)
    kept_b, *ends_b = middle(False, send_b, got_b)
    parts_b = exchanged(*ends_b)
    out = last(True, kept_a, parts_a)
    return last(False, kept_b, parts_b, out)


def solution(mesh):
    in_specs = (P("row", None, "col"), P("row", "col", None), P("row", "col", None), P())
    out_specs = P("row", None, "col")
    return jax.shard_map(shards, mesh=mesh, in_specs=in_specs, out_specs=out_specs, check_vma=False)
```

time: 190 us -> 180 us (0.947)
  the two profiles are of different devices: /device:TPU:158 before, /device:TPU:7 now
where the time goes in v2:
time: 180 us; the launch traced here: 179 us
  starting transfers between devices  87.1 us (48%)
  waiting for transfers between devices  48.2 us (27%)
  Pallas kernels  20.2 us (11%)
  between operations  13.7 us (8%)
  local copies, waits for them, and re-layouts  7.93 us (4%)
    ppermute x9, starting transfers between devices, moved(): lax.ppermute(value, axis, [(i, j) for i, j in pairs if 0 <= j < count])  45.1 us
    ppermute x10, starting transfers between devices, moved_on(): lax.ppermute(value, ('row', 'col'), [(r * GRID_COLS + c, t * GRID_COLS +...  42 us
    ppermute x10, waiting for transfers between devices, moved_on(): lax.ppermute(value, ('row', 'col'), [(r * GRID_COLS + c, t * GRID_COLS +...  31.7 us
    ppermute x9, waiting for transfers between devices, moved(): lax.ppermute(value, axis, [(i, j) for i, j in pairs if 0 <= j < count])  16.4 us
    pallas_call x2, Pallas kernels, middle(): pl.pallas_call(functools.partial(middle_kernel, first), out_shape=[shape(...  6.84 us
    pallas_call x2, Pallas kernels, last(): pl.pallas_call(functools.partial(last_kernel, first), out_shape=shape((W,...  6.8 us
    slice x1, local copies, waits for them, and re-layouts, shards(): hessenberg[:, 1]  4.11 us
    pallas_call x1, Pallas kernels, shards(): pl.pallas_call(left_kernel, out_shape=[shape((HALF, 2 * W), F32)] * 2 + [...  3.69 us
  transfers between devices with their start and end apart: 20, of which 13 were waited for; matrix products, arithmetic and copies ran while one was open for 2% of the time, Pallas kernels for 9%

profile of v2, /device:TPU:7, one launch (start us, length us, event | category | flops | bytes accessed | tf_op | source)
XLA Modules:
  0.0 178.7 jit_solution(10842478393759049917)
XLA Ops:
  6.5 0.0 all-gather.2.cloned.1.call-start
  6.5 0.8 fusion.1
  7.3 4.5 %collective-permute-start = (f32[32,256]{1,0:T(8,128)S(1)}, f32[32,256]{1,0:T(8,128)S(1)}, u32[]{:S(2)}, u32[]{:S(2)}) collective-permute-start(f32[32,256]{1,0:T(8,128)S(1)} %get-tuple-element.38), channel_id=1, source_target_pairs={{0,16},{16,32},{32,48},{48,64},{64,80},{80,96},{96,112},{112,128},... | collective-permute-start | bytes 98312 | tf_op jit(solution)/shard_map/ppermute | solution.py:40
  11.9 1.0 collective-permute-done
  12.9 0.8 pad_maximum_fusion.1.own
  13.7 0.0 copy-start.3
  13.7 4.8 %collective-permute-start.11 = (f32[32,1024]{1,0:T(8,128)S(1)}, f32[32,1024]{1,0:T(8,128)S(1)}, u32[]{:S(2)}, u32[]{:S(2)}) collective-permute-start(f32[32,1024]{1,0:T(8,128)S(1)} %pad_maximum_fusion.1.own), channel_id=1, source_target_pairs={{0,0},{1,16},{2,32},{3,48},{4,64},{5,80},{6,96},{7,112},{8,128},{9... | collective-permute-start | bytes 393224 | tf_op jit(solution)/shard_map/ppermute | solution.py:44
  18.6 3.9 %collective-permute-start.10 = (f32[32,1024]{1,0:T(8,128)S(1)}, f32[32,1024]{1,0:T(8,128)S(1)}, u32[]{:S(2)}, u32[]{:S(2)}) collective-permute-start(f32[32,1024]{1,0:T(8,128)S(1)} %pad_maximum_fusion.1.own), channel_id=1, source_target_pairs={{0,256},{1,272},{2,288},{3,304},{4,320},{5,336},{6,352},{7,368},{8... | collective-permute-start | bytes 393224 | tf_op jit(solution)/shard_map/ppermute | solution.py:44
  22.5 0.8 collective-permute-done.11
  23.3 6.9 %collective-permute-done.10 = f32[32,1024]{1,0:T(8,128)S(1)} collective-permute-done((f32[32,1024]{1,0:T(8,128)S(1)}, f32[32,1024]{1,0:T(8,128)S(1)}, u32[]{:S(2)}, u32[]{:S(2)}) %collective-permute-start.10) | collective-permute-done | bytes 131104 | tf_op jit(solution)/shard_map/ppermute | solution.py:44
  30.3 0.7 pad_maximum_fusion
  31.0 0.0 all-gather.2.cloned.1.call-update
  31.0 15.6 %collective-permute-start.3 = (f32[32,1024]{1,0:T(8,128)S(1)}, f32[32,1024]{1,0:T(8,128)S(1)}, u32[]{:S(2)}, u32[]{:S(2)}) collective-permute-start(f32[32,1024]{1,0:T(8,128)S(1)} %pad_maximum_fusion.1.own), channel_id=1, source_target_pairs={{0,12},{1,13},{2,14},{3,15},{4,0},{5,1},{6,2},{7,3},{8,4},{9,5},{1... | collective-permute-start | bytes 393224 | tf_op jit(solution)/shard_map/ppermute | solution.py:40
  46.6 1.9 %collective-permute-start.1 = (f32[32,1024]{1,0:T(8,128)S(1)}, f32[32,1024]{1,0:T(8,128)S(1)}, u32[]{:S(2)}, u32[]{:S(2)}) collective-permute-start(f32[32,1024]{1,0:T(8,128)S(1)} %pad_maximum_fusion.1.own), channel_id=1, source_target_pairs={{0,4},{1,5},{2,6},{3,7},{4,8},{5,9},{6,10},{7,11},{8,12},{9,13},{1... | collective-permute-start | bytes 393224 | tf_op jit(solution)/shard_map/ppermute | solution.py:40
  48.6 0.0 collective-permute-done.3.ahead
  48.6 0.0 copy-start.4
  48.6 8.0 %collective-permute-start.4 = (f32[16,1024]{1,0:T(8,128)S(1)}, f32[16,1024]{1,0:T(8,128)S(1)}, u32[]{:S(2)}, u32[]{:S(2)}) collective-permute-start(f32[16,1024]{1,0:T(8,128)S(1)} %slice.35), channel_id=1, source_target_pairs={{0,12},{1,13},{2,14},{3,15},{4,0},{5,1},{6,2},{7,3},{8,4},{9,5},{1... | collective-permute-start | bytes 196616 | tf_op jit(solution)/shard_map/ppermute | solution.py:40
  56.6 0.4 collective-permute-done.1.behind
  57.0 2.0 %collective-permute-start.2 = (f32[16,1024]{1,0:T(8,128)S(1)}, f32[16,1024]{1,0:T(8,128)S(1)}, u32[]{:S(2)}, u32[]{:S(2)}) collective-permute-start(f32[16,1024]{1,0:T(8,128)S(1)} %slice.34), channel_id=1, source_target_pairs={{0,4},{1,5},{2,6},{3,7},{4,8},{5,9},{6,10},{7,11},{8,12},{9,13},{1... | collective-permute-start | bytes 196616 | tf_op jit(solution)/shard_map/ppermute | solution.py:40
  59.0 2.6 %collective-permute-done.4.far_b = f32[16,1024]{1,0:T(8,128)S(1)} collective-permute-done((f32[16,1024]{1,0:T(8,128)S(1)}, f32[16,1024]{1,0:T(8,128)S(1)}, u32[]{:S(2)}, u32[]{:S(2)}) %collective-permute-start.4) | collective-permute-done | bytes 65568 | tf_op jit(solution)/shard_map/ppermute | solution.py:40
  61.6 5.4 %collective-permute-done.2.far_a = f32[16,1024]{1,0:T(8,128)S(1)} collective-permute-done((f32[16,1024]{1,0:T(8,128)S(1)}, f32[16,1024]{1,0:T(8,128)S(1)}, u32[]{:S(2)}, u32[]{:S(2)}) %collective-permute-start.2) | collective-permute-done | bytes 65568 | tf_op jit(solution)/shard_map/ppermute | solution.py:40
  67.0 0.0 copy-done.3
  67.0 0.0 copy-done.4
  67.0 0.0 copy-done.5
  67.1 0.6 copy-done.7
  67.7 1.9 %joined.1.own = f32[128,1024]{1,0:T(8,128)} custom-call(f32[16,1024]{1,0:T(8,128)} %copy-done.7, f32[16,1024]{1,0:T(8,128)} %copy-done.6, f32[32,1024]{1,0:T(8,128)} %copy-done.5, f32[32,1024]{1,0:T(8,128)} %copy-done.3, f32[32,1024]{1,0:T(8,128)} %copy-done.4), custom_call_target="tpu_custom_call" | custom-call | tf_op jit(solution)/shard_map/joined/pallas_call | solution.py:196
  69.6 1.9 %collective-permute-start.6 = (f32[128,1024]{1,0:T(8,128)}, f32[128,1024]{1,0:T(8,128)S(1)}, u32[]{:S(2)}, u32[]{:S(2)}) collective-permute-start(f32[128,1024]{1,0:T(8,128)} %joined.1.own), channel_id=1, source_target_pairs={{0,3},{1,0},{2,1},{3,2},{4,7},{5,4},{6,5},{7,6},{8,11},{9,8},{10,9... | collective-permute-start | bytes 1572872 | tf_op jit(solution)/shard_map/ppermute | solution.py:40
  71.5 4.6 %collective-permute-start.5 = (f32[128,1024]{1,0:T(8,128)}, f32[128,1024]{1,0:T(8,128)S(1)}, u32[]{:S(2)}, u32[]{:S(2)}) collective-permute-start(f32[128,1024]{1,0:T(8,128)} %joined.1.own), channel_id=1, source_target_pairs={{0,1},{1,2},{2,3},{3,0},{4,5},{5,6},{6,7},{7,4},{8,9},{9,10},{10,1... | collective-permute-start | bytes 1572872 | tf_op jit(solution)/shard_map/ppermute | solution.py:40
  76.1 0.1 pad_add_fusion.where
  76.2 4.1 %fusion = (f32[512,1,512]{2,1,0:T(1,128)S(1)}, f32[512,1,512]{2,1,0:T(1,128)S(1)}) fusion(f32[512,2,512]{2,1,0:T(2,128)} %param.4), kind=kLoop, calls=%fused_computation.7 | loop fusion | bytes 4194304 | tf_op jit(solution)/shard_map/slice | solution.py:212
  80.3 1.0 collective-permute-done.6.ahead
  81.4 1.9 %collective-permute-start.8 = (f32[64,1024]{1,0:T(8,128)S(1)}, f32[64,1024]{1,0:T(8,128)S(1)}, u32[]{:S(2)}, u32[]{:S(2)}) collective-permute-start(f32[64,1024]{1,0:T(8,128)S(1)} %slice.37), channel_id=1, source_target_pairs={{0,3},{1,0},{2,1},{3,2},{4,7},{5,4},{6,5},{7,6},{8,11},{9,8},{10,9... | collective-permute-start | bytes 786440 | tf_op jit(solution)/shard_map/ppermute | solution.py:40
  83.3 0.0 collective-permute-done.5.behind
  83.3 4.6 %collective-permute-start.7 = (f32[64,1024]{1,0:T(8,128)S(1)}, f32[64,1024]{1,0:T(8,128)S(1)}, u32[]{:S(2)}, u32[]{:S(2)}) collective-permute-start(f32[64,1024]{1,0:T(8,128)S(1)} %slice.36), channel_id=1, source_target_pairs={{0,1},{1,2},{2,3},{3,0},{4,5},{5,6},{6,7},{7,4},{8,9},{9,10},{10,1... | collective-permute-start | bytes 786440 | tf_op jit(solution)/shard_map/ppermute | solution.py:40
  87.9 0.0 copy-start.1
  87.9 0.0 copy-start.2
  87.9 0.2 copy_bitcast_fusion
  88.1 4.8 %collective-permute-done.8.far_b = f32[64,1024]{1,0:T(8,128)S(1)} collective-permute-done((f32[64,1024]{1,0:T(8,128)S(1)}, f32[64,1024]{1,0:T(8,128)S(1)}, u32[]{:S(2)}, u32[]{:S(2)}) %collective-permute-start.8) | collective-permute-done | bytes 262176 | tf_op jit(solution)/shard_map/ppermute | solution.py:40
  92.9 1.1 collective-permute-done.7.far_a
  94.1 0.0 copy-done.2
  94.1 3.7 %left.1 = (f32[256,1024]{1,0:T(8,128)}, f32[256,1024]{1,0:T(8,128)S(1)}, bf16[2,512,256]{2,1,0:T(8,128)(2,1)S(1)}, bf16[2,512,256]{2,1,0:T(8,128)(2,1)S(1)}) custom-call(s32[2]{0:T(128)S(1)} %pad_add_fusion.where, s32[2,32]{1,0:T(2,128)S(1)} %copy-done.2, f32[128,1024]{1,0:T(8,128)S(1)} %copy-done.1, f32[128,1024]{1,0:T(8,128)S(1)} %collective-permute-done.5.behind, ...), custom_call_target="tpu_custom_call" | custom-call | tf_op jit(solution)/shard_map/left/pallas_call | solution.py:204
  97.8 13.1 %collective-permute-start.15 = (f32[256,1024]{1,0:T(8,128)}, f32[256,1024]{1,0:T(8,128)}, u32[]{:S(2)}, u32[]{:S(2)}) collective-permute-start(f32[256,1024]{1,0:T(8,128)} %get-tuple-element.28.own), channel_id=1, source_target_pairs={{0,16},{1,17},{2,18},{3,19},{4,20},{5,21},{6,22},{7,23},{8,24},{9,... | collective-permute-start | bytes 3145736 | tf_op jit(solution)/shard_map/ppermute | solution.py:44
  110.9 1.9 %collective-permute-start.9 = (f32[256,1024]{1,0:T(8,128)S(1)}, f32[256,1024]{1,0:T(8,128)S(1)}, u32[]{:S(2)}, u32[]{:S(2)}) collective-permute-start(f32[256,1024]{1,0:T(8,128)S(1)} %get-tuple-element.19.own), channel_id=1, source_target_pairs={{16,32},{17,33},{18,34},{19,35},{20,36},{21,37},{22,38},{23,39},{2... | collective-permute-start | bytes 3145736 | tf_op jit(solution)/shard_map/ppermute | solution.py:44
  112.8 0.0 all-gather.2.cloned.1.call-done
  112.9 2.2 %copy-done = f32[1024,1024]{1,0:T(8,128)S(1)} copy-done((f32[1024,1024]{1,0:T(8,128)S(1)}, f32[1024,1024]{1,0:T(8,128)}, u32[]{:S(2)}) %copy-start) | copy-done | bytes 4194328
  115.0 0.9 prepare.1
  116.0 0.0 collective-permute-done.15.got
  116.0 3.9 %middle.3 = (f32[4,256,256]{2,1,0:T(8,128)S(1)}, f32[2,256,256]{2,1,0:T(8,128)S(1)}, f32[256,256]{1,0:T(8,128)S(1)}, f32[256,256]{1,0:T(8,128)S(1)}) custom-call(s32[2]{0:T(128)S(1)} %pad_add_fusion.where, s32[2,32]{1,0:T(2,128)S(1)} %copy-done.2, f32[256,1024]{1,0:T(8,128)} %get-tuple-element.28.own, f32[256,1024]{1,0:T(8,128)} %collective-permute-done.15.got, ...), custom_call_target="tpu_custom_call" | custom-call | tf_op jit(solution)/shard_map/middle/pallas_call | solution.py:229
  119.9 1.9 %collective-permute-start.16 = (f32[2,256,256]{2,1,0:T(8,128)S(1)}, f32[2,256,256]{2,1,0:T(8,128)S(1)}, u32[]{:S(2)}, u32[]{:S(2)}) collective-permute-start(f32[2,256,256]{2,1,0:T(8,128)S(1)} %get-tuple-element.30), channel_id=1, source_target_pairs={{0,1},{2,3},{4,5},{6,7},{8,9},{10,11},{12,13},{14,15},{16,17},{18,... | collective-permute-start | bytes 1572872 | tf_op jit(solution)/shard_map/ppermute | solution.py:44
  121.8 3.3 %collective-permute-start.17 = (f32[256,256]{1,0:T(8,128)S(1)}, f32[256,256]{1,0:T(8,128)S(1)}, u32[]{:S(2)}, u32[]{:S(2)}) collective-permute-start(f32[256,256]{1,0:T(8,128)S(1)} %get-tuple-element.31), channel_id=1, source_target_pairs={{1,2},{3,4},{5,6},{7,8},{9,10},{11,12},{13,14},{15,0},{17,18},{19,... | collective-permute-start | bytes 786440 | tf_op jit(solution)/shard_map/ppermute | solution.py:44
  125.1 2.2 %collective-permute-done.9.got = f32[256,1024]{1,0:T(8,128)S(1)} collective-permute-done((f32[256,1024]{1,0:T(8,128)S(1)}, f32[256,1024]{1,0:T(8,128)S(1)}, u32[]{:S(2)}, u32[]{:S(2)}) %collective-permute-start.9) | collective-permute-done | bytes 1048608 | tf_op jit(solution)/shard_map/ppermute | solution.py:44
  127.3 2.9 %middle.2 = (f32[4,256,256]{2,1,0:T(8,128)S(1)}, f32[2,256,256]{2,1,0:T(8,128)S(1)}, f32[256,256]{1,0:T(8,128)S(1)}, f32[256,256]{1,0:T(8,128)S(1)}) custom-call(s32[2]{0:T(128)S(1)} %pad_add_fusion.where, s32[2,32]{1,0:T(2,128)S(1)} %copy-done.2, f32[256,1024]{1,0:T(8,128)S(1)} %get-tuple-element.19.own, f32[256,1024]{1,0:T(8,128)S(1)} %collective-permute-done.9.got, ...), custom_call_target="tpu_custom_call" | custom-call | tf_op jit(solution)/shard_map/middle/pallas_call | solution.py:229
  130.2 2.6 %collective-permute-start.12 = (f32[2,256,256]{2,1,0:T(8,128)S(1)}, f32[2,256,256]{2,1,0:T(8,128)S(1)}, u32[]{:S(2)}, u32[]{:S(2)}) collective-permute-start(f32[2,256,256]{2,1,0:T(8,128)S(1)} %get-tuple-element.25), channel_id=1, source_target_pairs={{0,1},{2,3},{4,5},{6,7},{8,9},{10,11},{12,13},{14,15},{16,17},{18,... | collective-permute-start | bytes 1572872 | tf_op jit(solution)/shard_map/ppermute | solution.py:44
  132.9 2.1 %collective-permute-start.18 = (f32[256,256]{1,0:T(8,128)S(1)}, f32[256,256]{1,0:T(8,128)S(1)}, u32[]{:S(2)}, u32[]{:S(2)}) collective-permute-start(f32[256,256]{1,0:T(8,128)S(1)} %get-tuple-element.32), channel_id=1, source_target_pairs={{1,2},{3,4},{5,6},{7,8},{9,10},{11,12},{13,14},{17,18},{19,20},{21... | collective-permute-start | bytes 786440 | tf_op jit(solution)/shard_map/ppermute | solution.py:44
  135.0 6.2 %collective-permute-start.13 = (f32[256,256]{1,0:T(8,128)S(1)}, f32[256,256]{1,0:T(8,128)S(1)}, u32[]{:S(2)}, u32[]{:S(2)}) collective-permute-start(f32[256,256]{1,0:T(8,128)S(1)} %get-tuple-element.26), channel_id=1, source_target_pairs={{1,2},{3,4},{5,6},{7,8},{9,10},{11,12},{13,14},{15,0},{17,18},{19,... | collective-permute-start | bytes 786440 | tf_op jit(solution)/shard_map/ppermute | solution.py:44
  141.2 0.0 collective-permute-done.17.edge0
  141.2 2.1 %collective-permute-start.14 = (f32[256,256]{1,0:T(8,128)S(1)}, f32[256,256]{1,0:T(8,128)S(1)}, u32[]{:S(2)}, u32[]{:S(2)}) collective-permute-start(f32[256,256]{1,0:T(8,128)S(1)} %get-tuple-element.27), channel_id=1, source_target_pairs={{1,2},{3,4},{5,6},{7,8},{9,10},{11,12},{13,14},{17,18},{19,20},{21... | collective-permute-start | bytes 786440 | tf_op jit(solution)/shard_map/ppermute | solution.py:44
  143.3 5.6 %collective-permute-done.18.edge1 = f32[256,256]{1,0:T(8,128)S(1)} collective-permute-done((f32[256,256]{1,0:T(8,128)S(1)}, f32[256,256]{1,0:T(8,128)S(1)}, u32[]{:S(2)}, u32[]{:S(2)}) %collective-permute-start.18) | collective-permute-done | bytes 262176 | tf_op jit(solution)/shard_map/ppermute | solution.py:44
  148.9 0.0 collective-permute-done.16.side
  148.9 3.4 %last.2.rest_0_ = f32[512,2,512]{2,1,0:T(2,128)} custom-call(s32[2]{0:T(128)S(1)} %pad_add_fusion.where, s32[2,32]{1,0:T(2,128)S(1)} %copy-done.2, f32[4,256,256]{2,1,0:T(8,128)S(1)} %get-tuple-element.29.kept, f32[2,256,256]{2,1,0:T(8,128)S(1)} %collective-permute-done.16.side, f32[256,256]{1,0:T(8,128)S(1)} %collective-permute-done.17.edge0, ...), custom_call_target="tpu_custom_call" | custom-call | tf_op jit(solution)/shard_map/last/pallas_call | solution.py:258
  152.3 10.6 %collective-permute-done.13.edge0 = f32[256,256]{1,0:T(8,128)S(1)} collective-permute-done((f32[256,256]{1,0:T(8,128)S(1)}, f32[256,256]{1,0:T(8,128)S(1)}, u32[]{:S(2)}, u32[]{:S(2)}) %collective-permute-start.13) | collective-permute-done | bytes 262176 | tf_op jit(solution)/shard_map/ppermute | solution.py:44
  162.9 5.6 %collective-permute-done.14.edge1 = f32[256,256]{1,0:T(8,128)S(1)} collective-permute-done((f32[256,256]{1,0:T(8,128)S(1)}, f32[256,256]{1,0:T(8,128)S(1)}, u32[]{:S(2)}, u32[]{:S(2)}) %collective-permute-start.14) | collective-permute-done | bytes 262176 | tf_op jit(solution)/shard_map/ppermute | solution.py:44
  168.5 0.0 collective-permute-done.12.side
  168.5 3.4 %last.3 = f32[512,2,512]{2,1,0:T(2,128)} custom-call(s32[2]{0:T(128)S(1)} %pad_add_fusion.where, s32[2,32]{1,0:T(2,128)S(1)} %copy-done.2, f32[4,256,256]{2,1,0:T(8,128)S(1)} %get-tuple-element.24.kept, f32[2,256,256]{2,1,0:T(8,128)S(1)} %collective-permute-done.12.side, ...), custom_call_target="tpu_custom_call", output_to_operand_aliasing={{}: (8, {})} | custom-call | tf_op jit(solution)/shard_map/last/pallas_call | solution.py:258
  (11 shorter events, 0.1 us)
Async XLA Ops:
  6.5 106.3 %all-gather.2.cloned.1.call-start = ((), (), s32[]{:S(2)}) async-start(), calls=%async_computation | async-start | bytes 4456448 | tf_op jit(solution)/shard_map/all_gather | solution.py:187
  7.3 5.6 %collective-permute-start = (f32[32,256]{1,0:T(8,128)S(1)}, f32[32,256]{1,0:T(8,128)S(1)}, u32[]{:S(2)}, u32[]{:S(2)}) collective-permute-start(f32[32,256]{1,0:T(8,128)S(1)} %get-tuple-element.38), channel_id=1, source_target_pairs={{0,16},{16,32},{32,48},{48,64},{64,80},{80,96},{96,112},{112,128},... | collective-permute-start | bytes 98312 | tf_op jit(solution)/shard_map/ppermute | solution.py:40
  13.7 53.3 %copy-start.3 = (f32[32,1024]{1,0:T(8,128)}, f32[32,1024]{1,0:T(8,128)S(1)}, u32[]{:S(2)}) copy-start(f32[32,1024]{1,0:T(8,128)S(1)} %pad_maximum_fusion.1.own) | copy-start | bytes 393220
  13.7 9.6 %collective-permute-start.11 = (f32[32,1024]{1,0:T(8,128)S(1)}, f32[32,1024]{1,0:T(8,128)S(1)}, u32[]{:S(2)}, u32[]{:S(2)}) collective-permute-start(f32[32,1024]{1,0:T(8,128)S(1)} %pad_maximum_fusion.1.own), channel_id=1, source_target_pairs={{0,0},{1,16},{2,32},{3,48},{4,64},{5,80},{6,96},{7,112},{8,128},{9... | collective-permute-start | bytes 393224 | tf_op jit(solution)/shard_map/ppermute | solution.py:44
  18.6 11.6 %collective-permute-start.10 = (f32[32,1024]{1,0:T(8,128)S(1)}, f32[32,1024]{1,0:T(8,128)S(1)}, u32[]{:S(2)}, u32[]{:S(2)}) collective-permute-start(f32[32,1024]{1,0:T(8,128)S(1)} %pad_maximum_fusion.1.own), channel_id=1, source_target_pairs={{0,256},{1,272},{2,288},{3,304},{4,320},{5,336},{6,352},{7,368},{8... | collective-permute-start | bytes 393224 | tf_op jit(solution)/shard_map/ppermute | solution.py:44
  31.0 17.6 %collective-permute-start.3 = (f32[32,1024]{1,0:T(8,128)S(1)}, f32[32,1024]{1,0:T(8,128)S(1)}, u32[]{:S(2)}, u32[]{:S(2)}) collective-permute-start(f32[32,1024]{1,0:T(8,128)S(1)} %pad_maximum_fusion.1.own), channel_id=1, source_target_pairs={{0,12},{1,13},{2,14},{3,15},{4,0},{5,1},{6,2},{7,3},{8,4},{9,5},{1... | collective-permute-start | bytes 393224 | tf_op jit(solution)/shard_map/ppermute | solution.py:40
  46.6 10.4 %collective-permute-start.1 = (f32[32,1024]{1,0:T(8,128)S(1)}, f32[32,1024]{1,0:T(8,128)S(1)}, u32[]{:S(2)}, u32[]{:S(2)}) collective-permute-start(f32[32,1024]{1,0:T(8,128)S(1)} %pad_maximum_fusion.1.own), channel_id=1, source_target_pairs={{0,4},{1,5},{2,6},{3,7},{4,8},{5,9},{6,10},{7,11},{8,12},{9,13},{1... | collective-permute-start | bytes 393224 | tf_op jit(solution)/shard_map/ppermute | solution.py:40
  48.6 18.4 %copy-start.4 = (f32[32,1024]{1,0:T(8,128)}, f32[32,1024]{1,0:T(8,128)S(1)}, u32[]{:S(2)}) copy-start(f32[32,1024]{1,0:T(8,128)S(1)} %collective-permute-done.3.ahead) | copy-start | bytes 393220
  48.6 13.0 %collective-permute-start.4 = (f32[16,1024]{1,0:T(8,128)S(1)}, f32[16,1024]{1,0:T(8,128)S(1)}, u32[]{:S(2)}, u32[]{:S(2)}) collective-permute-start(f32[16,1024]{1,0:T(8,128)S(1)} %slice.35), channel_id=1, source_target_pairs={{0,12},{1,13},{2,14},{3,15},{4,0},{5,1},{6,2},{7,3},{8,4},{9,5},{1... | collective-permute-start | bytes 196616 | tf_op jit(solution)/shard_map/ppermute | solution.py:40
  57.0 10.0 %copy-start.5 = (f32[32,1024]{1,0:T(8,128)}, f32[32,1024]{1,0:T(8,128)S(1)}, u32[]{:S(2)}) copy-start(f32[32,1024]{1,0:T(8,128)S(1)} %collective-permute-done.1.behind) | copy-start | bytes 393220
  57.0 10.0 %collective-permute-start.2 = (f32[16,1024]{1,0:T(8,128)S(1)}, f32[16,1024]{1,0:T(8,128)S(1)}, u32[]{:S(2)}, u32[]{:S(2)}) collective-permute-start(f32[16,1024]{1,0:T(8,128)S(1)} %slice.34), channel_id=1, source_target_pairs={{0,4},{1,5},{2,6},{3,7},{4,8},{5,9},{6,10},{7,11},{8,12},{9,13},{1... | collective-permute-start | bytes 196616 | tf_op jit(solution)/shard_map/ppermute | solution.py:40
  61.6 5.5 %copy-start.6 = (f32[16,1024]{1,0:T(8,128)}, f32[16,1024]{1,0:T(8,128)S(1)}, u32[]{:S(2)}) copy-start(f32[16,1024]{1,0:T(8,128)S(1)} %collective-permute-done.4.far_b) | copy-start | bytes 196612
  67.1 0.6 copy-start.7
  69.6 11.7 %collective-permute-start.6 = (f32[128,1024]{1,0:T(8,128)}, f32[128,1024]{1,0:T(8,128)S(1)}, u32[]{:S(2)}, u32[]{:S(2)}) collective-permute-start(f32[128,1024]{1,0:T(8,128)} %joined.1.own), channel_id=1, source_target_pairs={{0,3},{1,0},{2,1},{3,2},{4,7},{5,4},{6,5},{7,6},{8,11},{9,8},{10,9... | collective-permute-start | bytes 1572872 | tf_op jit(solution)/shard_map/ppermute | solution.py:40
  71.5 11.8 %collective-permute-start.5 = (f32[128,1024]{1,0:T(8,128)}, f32[128,1024]{1,0:T(8,128)S(1)}, u32[]{:S(2)}, u32[]{:S(2)}) collective-permute-start(f32[128,1024]{1,0:T(8,128)} %joined.1.own), channel_id=1, source_target_pairs={{0,1},{1,2},{2,3},{3,0},{4,5},{5,6},{6,7},{7,4},{8,9},{9,10},{10,1... | collective-permute-start | bytes 1572872 | tf_op jit(solution)/shard_map/ppermute | solution.py:40
  81.4 11.6 %collective-permute-start.8 = (f32[64,1024]{1,0:T(8,128)S(1)}, f32[64,1024]{1,0:T(8,128)S(1)}, u32[]{:S(2)}, u32[]{:S(2)}) collective-permute-start(f32[64,1024]{1,0:T(8,128)S(1)} %slice.37), channel_id=1, source_target_pairs={{0,3},{1,0},{2,1},{3,2},{4,7},{5,4},{6,5},{7,6},{8,11},{9,8},{10,9... | collective-permute-start | bytes 786440 | tf_op jit(solution)/shard_map/ppermute | solution.py:40
  83.3 10.7 %collective-permute-start.7 = (f32[64,1024]{1,0:T(8,128)S(1)}, f32[64,1024]{1,0:T(8,128)S(1)}, u32[]{:S(2)}, u32[]{:S(2)}) collective-permute-start(f32[64,1024]{1,0:T(8,128)S(1)} %slice.36), channel_id=1, source_target_pairs={{0,1},{1,2},{2,3},{3,0},{4,5},{5,6},{6,7},{7,4},{8,9},{9,10},{10,1... | collective-permute-start | bytes 786440 | tf_op jit(solution)/shard_map/ppermute | solution.py:40
  87.9 6.2 %copy-start.1 = (f32[128,1024]{1,0:T(8,128)S(1)}, f32[128,1024]{1,0:T(8,128)}, u32[]{:S(2)}) copy-start(f32[128,1024]{1,0:T(8,128)} %joined.1.own) | copy-start | bytes 1572868
  87.9 6.2 %copy-start.2 = (s32[2,32]{1,0:T(2,128)S(1)}, s32[2,32]{1,0:T(2,128)}, u32[]{:S(2)}) copy-start(s32[2,32]{1,0:T(2,128)} %lives.9) | copy-start | bytes 772
  97.8 18.2 %collective-permute-start.15 = (f32[256,1024]{1,0:T(8,128)}, f32[256,1024]{1,0:T(8,128)}, u32[]{:S(2)}, u32[]{:S(2)}) collective-permute-start(f32[256,1024]{1,0:T(8,128)} %get-tuple-element.28.own), channel_id=1, source_target_pairs={{0,16},{1,17},{2,18},{3,19},{4,20},{5,21},{6,22},{7,23},{8,24},{9,... | collective-permute-start | bytes 3145736 | tf_op jit(solution)/shard_map/ppermute | solution.py:44
  110.9 16.4 %collective-permute-start.9 = (f32[256,1024]{1,0:T(8,128)S(1)}, f32[256,1024]{1,0:T(8,128)S(1)}, u32[]{:S(2)}, u32[]{:S(2)}) collective-permute-start(f32[256,1024]{1,0:T(8,128)S(1)} %get-tuple-element.19.own), channel_id=1, source_target_pairs={{16,32},{17,33},{18,34},{19,35},{20,36},{21,37},{22,38},{23,39},{2... | collective-permute-start | bytes 3145736 | tf_op jit(solution)/shard_map/ppermute | solution.py:44
  112.9 2.2 %copy-start = (f32[1024,1024]{1,0:T(8,128)S(1)}, f32[1024,1024]{1,0:T(8,128)}, u32[]{:S(2)}) copy-start(f32[1024,1024]{1,0:T(8,128)} %all-gather.2.cloned.1.call-done) | copy-start | bytes 12582916
  119.9 29.0 %collective-permute-start.16 = (f32[2,256,256]{2,1,0:T(8,128)S(1)}, f32[2,256,256]{2,1,0:T(8,128)S(1)}, u32[]{:S(2)}, u32[]{:S(2)}) collective-permute-start(f32[2,256,256]{2,1,0:T(8,128)S(1)} %get-tuple-element.30), channel_id=1, source_target_pairs={{0,1},{2,3},{4,5},{6,7},{8,9},{10,11},{12,13},{14,15},{16,17},{18,... | collective-permute-start | bytes 1572872 | tf_op jit(solution)/shard_map/ppermute | solution.py:44
  121.8 19.4 %collective-permute-start.17 = (f32[256,256]{1,0:T(8,128)S(1)}, f32[256,256]{1,0:T(8,128)S(1)}, u32[]{:S(2)}, u32[]{:S(2)}) collective-permute-start(f32[256,256]{1,0:T(8,128)S(1)} %get-tuple-element.31), channel_id=1, source_target_pairs={{1,2},{3,4},{5,6},{7,8},{9,10},{11,12},{13,14},{15,0},{17,18},{19,... | collective-permute-start | bytes 786440 | tf_op jit(solution)/shard_map/ppermute | solution.py:44
  130.2 38.2 %collective-permute-start.12 = (f32[2,256,256]{2,1,0:T(8,128)S(1)}, f32[2,256,256]{2,1,0:T(8,128)S(1)}, u32[]{:S(2)}, u32[]{:S(2)}) collective-permute-start(f32[2,256,256]{2,1,0:T(8,128)S(1)} %get-tuple-element.25), channel_id=1, source_target_pairs={{0,1},{2,3},{4,5},{6,7},{8,9},{10,11},{12,13},{14,15},{16,17},{18,... | collective-permute-start | bytes 1572872 | tf_op jit(solution)/shard_map/ppermute | solution.py:44
  132.9 16.0 %collective-permute-start.18 = (f32[256,256]{1,0:T(8,128)S(1)}, f32[256,256]{1,0:T(8,128)S(1)}, u32[]{:S(2)}, u32[]{:S(2)}) collective-permute-start(f32[256,256]{1,0:T(8,128)S(1)} %get-tuple-element.32), channel_id=1, source_target_pairs={{1,2},{3,4},{5,6},{7,8},{9,10},{11,12},{13,14},{17,18},{19,20},{21... | collective-permute-start | bytes 786440 | tf_op jit(solution)/shard_map/ppermute | solution.py:44
  135.0 27.9 %collective-permute-start.13 = (f32[256,256]{1,0:T(8,128)S(1)}, f32[256,256]{1,0:T(8,128)S(1)}, u32[]{:S(2)}, u32[]{:S(2)}) collective-permute-start(f32[256,256]{1,0:T(8,128)S(1)} %get-tuple-element.26), channel_id=1, source_target_pairs={{1,2},{3,4},{5,6},{7,8},{9,10},{11,12},{13,14},{15,0},{17,18},{19,... | collective-permute-start | bytes 786440 | tf_op jit(solution)/shard_map/ppermute | solution.py:44
  141.2 27.3 %collective-permute-start.14 = (f32[256,256]{1,0:T(8,128)S(1)}, f32[256,256]{1,0:T(8,128)S(1)}, u32[]{:S(2)}, u32[]{:S(2)}) collective-permute-start(f32[256,256]{1,0:T(8,128)S(1)} %get-tuple-element.27), channel_id=1, source_target_pairs={{1,2},{3,4},{5,6},{7,8},{9,10},{11,12},{13,14},{17,18},{19,20},{21... | collective-permute-start | bytes 786440 | tf_op jit(solution)/shard_map/ppermute | solution.py:44
Sparse Core Ops, SparseCore 0:
  31.1 65.8 all-gather.1

commit v3 on v2

v3 whole, which is shorter than its diff:
```python
import functools

import jax
import jax.numpy as jnp
from jax import lax
from jax.experimental import pallas as pl
from jax.experimental.pallas import tpu as pltpu
from jax.sharding import PartitionSpec as P

GRID_ROWS, GRID_COLS = 32, 16
RING = 4
W = 512
HALF = 256
LAST = 31
BF16, F32 = jnp.bfloat16, jnp.float32
PARAMS = pltpu.CompilerParams(vmem_limit_bytes=16 * 1024 * 1024)
VMEM = pl.BlockSpec(memory_space=pltpu.VMEM)
SMEM = pl.BlockSpec(memory_space=pltpu.SMEM)


def split(x):
    high = x.astype(BF16)
    return high, (x - high.astype(F32)).astype(BF16)


def product(a, b, contract):
    dims = (contract, ((), ()))
    one = lambda x, y: lax.dot_general(x, y, dims, preferred_element_type=F32)
    return one(a[0], b[0]) + (one(a[0], b[1]) + one(a[1], b[0]))


def cost(products, megabytes):
    flops = int(products * 3 * 2 * HALF * W * 2 * W)
    return pl.CostEstimate(flops=flops, bytes_accessed=megabytes << 20, transcendentals=0)


def live(ref, kind, index):
    inside = (index >= 0) & (index <= LAST - kind)
    return inside & (ref[kind, jnp.clip(index, 0, LAST)] == 1)


def moved(value, axis, target):
    count = lax.axis_size(axis)
    pairs = [(i, target(i)) for i in range(count)]
    return lax.ppermute(value, axis, [(i, j) for i, j in pairs if 0 <= j < count])


def moved_on(value, pairs):
    return lax.ppermute(
        value, ("row", "col"), [(r * GRID_COLS + c, t * GRID_COLS + d) for (r, c), (t, d) in pairs]
    )


def everywhere(test, target):
    return [((r, c), target(r, c)) for r in range(GRID_ROWS) for c in range(GRID_COLS) if test(r, c)]


def swapped(value, pairs):
    return moved_on(value, pairs + [(b, a) for a, b in pairs])


def left_kernel(where, lives, pieces, h0, h1, send_a, send_b, fb_high, fb_low, d_high, d_low):
    row, col = where[0], where[1]
    for at_x in range(RING):
        for at_y in range(RING):
            rows = slice((at_y * RING + at_x) * 32, (at_y * RING + at_x) * 32 + 32)
            high, low = split(pieces[at_x, at_y])
            for side in range(2):
                lanes = slice(W + side * HALF, W + side * HALF + HALF)
                fb_high[side, rows, :] = high[:, lanes]
                fb_low[side, rows, :] = low[:, lanes]
            d_high[rows, :] = high[:, :W]
            d_low[rows, :] = low[:, :W]
    odd = lax.rem(row, 2) == 1
    live_row = live(lives, 0, row)
    factor = (d_high[...], d_low[...])
    for s, h in enumerate((h0, h1)):
        lanes = slice(s * W, s * W + W)
        value = h[...]
        turned = product(factor, split(value), ((0,), (0,)))
        value = jnp.where((col + GRID_COLS * s >= row) & live_row, turned, value)
        send_a[:, lanes] = jnp.where(odd, value[:HALF], value[HALF:])
        send_b[:, lanes] = jnp.where(odd, value[HALF:], value[:HALF])


def prepare_kernel(where, gathered, high, low):
    for index in range(16):
        rows = slice(32 * index, 32 * index + 32)
        high[0, rows, :], low[0, rows, :] = split(gathered[lax.rem(where[1] + index, 16), 0])


def middle_kernel(s, where, lives, own_a, own_b, got_a, got_b, fb_high, fb_low, c_high, c_low, *rest):
    kept, side, edge = rest[-3:]
    row, col = where[0], where[1]
    lanes = slice(s * W, s * W + W)
    tile = col + GRID_COLS * s
    odd_col = lax.rem(col, 2) == 1
    is_corner = (lax.broadcasted_iota(jnp.int32, (HALF, 128), 0) == 0) & (
        lax.broadcasted_iota(jnp.int32, (HALF, 128), 1) == 127
    )
    for half, (own, got) in enumerate(((own_a, got_a), (own_b, got_b))):
        top = lax.rem(row + half, 2) == 1
        top_index = top.astype(jnp.int32)
        active = live(lives, 1, jnp.where(top, row - 1, row))
        factor = (fb_high[top_index], fb_low[top_index])
        below_part = (fb_high[top_index, HALF:, :], fb_low[top_index, HALF:, :])
        own_raw, got_raw = own[:, lanes], got[:, lanes]
        own_value = jnp.where(top & (tile < row), 0.0, own_raw)
        got_value = jnp.where(top | (tile > row), got_raw, 0.0)
        acted = active & (tile >= jnp.where(top, row - 1, row))
        upper, lower = jnp.where(top, got_value, own_value), jnp.where(top, own_value, got_value)
        rows = product(factor, split(jnp.concatenate([upper, lower], 0)), ((0,), (0,)))
        value = jnp.where(acted, rows, own_value)
        for_left = jnp.where(top, jnp.where(tile >= row, value, 0.0), jnp.where(tile == row, own_value, value))
        turns = live(lives, 0, tile)
        matrix = lambda a, b: (c_high[s, :, a:b], c_low[s, :, a:b])
        left = product(split(for_left), matrix(0, HALF), ((1,), (0,)))
        right = product(split(value), matrix(HALF, W), ((1,), (0,)))
        left = jnp.where(turns, left, for_left[:, :HALF])
        right = jnp.where(turns, right, value[:, HALF:])
        has_corner = (top & (tile == row - 1)) | (~top & (tile == row) & acted)
        corner = jnp.where(has_corner & is_corner, jnp.where(top, own_raw[:, W - 128 :], got_raw[:, W - 128 :]), 0.0)
        spread = jnp.where(acted, product(below_part, split(corner), ((0,), (0,))), corner)
        right = jnp.concatenate([right[:, : HALF - 128], right[:, HALF - 128 :] + spread], 1)
        kept[half, 0], kept[half, 1] = left, right
        inward = jnp.where(odd_col, left, right)
        if s == 0:
            side[0, half] = inward
        else:
            side[half] = inward
        outward = jnp.where(odd_col, right, left)
        if s == 0:
            outward = jnp.where(col == 0, rest[0][half, 0], outward)
            side[1, half] = rest[1][half]
        edge[half] = outward


def border_column(lives, c_high, c_low, row, col, s, half, kept, near, far, part):
    tile = col + GRID_COLS * s
    top = lax.rem(row + half, 2) == 1
    odd_col = lax.rem(col, 2) == 1
    if part == 0:
        one, two, at = jnp.where(odd_col, near, far), kept[half, 0], W + HALF
        own, last_tile = two, tile
    else:
        one, two, at = kept[half, 1], jnp.where(odd_col, far, near), W
        own, last_tile = one, tile + 1
    keep = live(lives, 1, last_tile - 1) & ((row < last_tile) | ((row == last_tile) & top))
    factor = (c_high[s, :, at : at + HALF], c_low[s, :, at : at + HALF])
    value = product(split(jnp.concatenate([one, two], 1)), factor, ((1,), (0,)))
    return jnp.where(keep, value, own)


def second_tile_kernel(where, lives, kept, side, edge, c_high, c_low, out):
    row, col = where[0], where[1]
    for half in range(2):
        for part in range(2):
            value = border_column(lives, c_high, c_low, row, col, 1, half, kept, side[1, half], edge[half], part)
            out[half, :, part * HALF : part * HALF + HALF] = value


def first_tile_kernel(where, lives, kept, kept_1, side, edge, c_high, c_low, second, out):
    row, col = where[0], where[1]
    for half in range(2):
        start = pl.multiple_of(lax.rem(row + half + 1, 2) * HALF, HALF)
        place = pl.ds(start, HALF)
        for part in range(2):
            lanes = slice(part * HALF, part * HALF + HALF)
            out[place, 0, lanes] = border_column(
                lives, c_high, c_low, row, col, 0, half, kept, side[0, half], edge[half], part
            )
        out[place, 1, :] = second[half]

        @pl.when(col == 0)
        def _():
            out[place, 1, :HALF] = border_column(
                lives, c_high, c_low, row, col, 1, half, kept_1, side[1, half], edge[half], 0
            )


def shards(hessenberg, diag_factors, border_factors, window_live):
    row = lax.axis_index("row")
    col = lax.axis_index("col")
    where = jnp.stack([row, col]).astype(jnp.int32)
    shape = jax.ShapeDtypeStruct

    border = border_factors[0]
    above = moved(border[:, HALF:], "row", lambda r: r + 1)
    piece = jnp.concatenate([diag_factors[0], border[:, :HALF], above], 1)

    mine = moved_on(piece, everywhere(lambda r, c: True, lambda r, c: (r // 16 * 16 + (r + c) % 16, r % 16)))
    def shared(value, groups):
        every = jnp.broadcast_to(value[None], (RING, *value.shape))
        return lax.all_to_all(every, "col", 0, 0, axis_index_groups=groups)

    by_y = shared(piece, [[x + RING * y for y in range(RING)] for x in range(RING)])
    mine, by_y = lax.optimization_barrier((mine, by_y))
    other = moved(mine, "row", lambda r: r ^ 16)
    groups = [list(range(16)), list(range(16, 32))]
    gathered = lax.all_gather(jnp.concatenate([mine, other], 0), "row", axis=0, tiled=True, axis_index_groups=groups)
    gathered = gathered.reshape(16, 2, 32, 2 * W)
    by_row = shared(by_y.reshape(RING * 32, 2 * W), [[x + RING * y for x in range(RING)] for y in range(RING)])
    by_row = by_row.reshape(RING, RING, 32, 2 * W)

    send_a, send_b, fb_high, fb_low = pl.pallas_call(
        left_kernel,
        out_shape=[shape((HALF, 2 * W), F32)] * 2 + [shape((2, W, HALF), BF16)] * 2,
        in_specs=[SMEM, SMEM] + [VMEM] * 3,
        out_specs=[VMEM] * 4,
        scratch_shapes=[pltpu.VMEM((W, W), BF16)] * 2,
        compiler_params=PARAMS,
        cost_estimate=cost(2, 7),
        name="left",
    )(where, window_live, by_row, hessenberg[:, 0], hessenberg[:, 1])

    every_col = range(GRID_COLS)
    got_b = swapped(send_b, [((r, c), (r + 1, c)) for r in range(1, 31, 2) for c in every_col])
    got_a = swapped(send_a, [((r, c), (r + 1, c)) for r in range(0, 32, 2) for c in every_col])

    c_high, c_low = pl.pallas_call(
        prepare_kernel,
        out_shape=[shape((2, W, 2 * W), BF16)] * 2,
        grid_spec=pltpu.PrefetchScalarGridSpec(
            num_scalar_prefetch=1,
            grid=(2,),
            in_specs=[pl.BlockSpec((16, 1, 32, 2 * W), lambda s, where: (0, s ^ (where[0] // 16), 0, 0))],
            out_specs=[pl.BlockSpec((1, W, 2 * W), lambda s, where: (s, 0, 0))] * 2,
        ),
        compiler_params=PARAMS,
        cost_estimate=cost(0, 8),
        name="prepare",
    )(where, gathered)

    halves, quarters = shape((2, HALF, HALF), F32), shape((2, 2, HALF, HALF), F32)

    def middle(s, *other):
        return pl.pallas_call(
            functools.partial(middle_kernel, s),
            out_shape=[quarters, halves if s else quarters, halves],
            in_specs=[SMEM, SMEM] + [VMEM] * (8 + len(other)),
            out_specs=[VMEM] * 3,
            compiler_params=PARAMS,
            cost_estimate=cost(2, 4),
            name="middle",
        )(where, window_live, send_a, send_b, got_a, got_b, fb_high, fb_low, c_high, c_low, *other)

    rows = range(GRID_ROWS)
    kept_1, side_1, edge_1 = middle(1)
    edge_1 = swapped(edge_1, [((r, c), (r, c + 1)) for r in rows for c in range(1, 15, 2) if r <= c + 17])
    kept_0, sides, edge_0 = middle(0, kept_1, side_1)
    edge_0 = swapped(edge_0, [((r, c), (r, (c + 1) % 16)) for r in rows for c in range(1, 16, 2) if r <= c + 1])
    sides = swapped(sides, [((r, c), (r, c + 1)) for r in rows for c in range(0, 16, 2) if r <= c + 17])

    second = pl.pallas_call(
        second_tile_kernel,
        out_shape=shape((2, HALF, W), F32),
        in_specs=[SMEM, SMEM] + [VMEM] * 5,
        out_specs=VMEM,
        compiler_params=PARAMS,
        cost_estimate=cost(1, 4),
        name="second",
    )(where, window_live, kept_1, sides, edge_1, c_high, c_low)
    return pl.pallas_call(
        first_tile_kernel,
        out_shape=shape((W, 2, W), F32),
        in_specs=[SMEM, SMEM] + [VMEM] * 7,
        out_specs=VMEM,
        compiler_params=PARAMS,
        cost_estimate=cost(1, 4),
        name="first",
    )(where, window_live, kept_0, kept_1, sides, edge_0, c_high, c_low, second)


def solution(mesh):
    in_specs = (P("row", None, "col"), P("row", "col", None), P("row", "col", None), P())
    out_specs = P("row", None, "col")
    return jax.shard_map(shards, mesh=mesh, in_specs=in_specs, out_specs=out_specs, check_vma=False)
```

time: 180 us -> 182 us (1.011)
  the two profiles are of different devices: /device:TPU:7 before, /device:TPU:249 now
where the time goes in v3:
time: 182 us
  waiting for transfers between devices  102 us (56%)
  starting transfers between devices  32 us (18%)
  local copies, waits for them, and re-layouts  16.4 us (9%)
  Pallas kernels  16.4 us (9%)
  between operations  13.6 us (7%)
    ppermute x6, waiting for transfers between devices, moved_on(): lax.ppermute(value, ('row', 'col'), [(r * GRID_COLS + c, t * GRID_COLS +...  76.9 us
    all_to_all x2, waiting for transfers between devices, shared(): return lax.all_to_all(every, 'col', 0, 0, axis_index_groups=groups)  19.4 us
    ppermute x6, starting transfers between devices, moved_on(): lax.ppermute(value, ('row', 'col'), [(r * GRID_COLS + c, t * GRID_COLS +...  14.3 us
    all_to_all x2, starting transfers between devices, shared(): return lax.all_to_all(every, 'col', 0, 0, axis_index_groups=groups)  10 us
    unnamed x18, local copies, waits for them, and re-layouts  7.97 us
    ppermute x2, starting transfers between devices, moved(): lax.ppermute(value, axis, [(i, j) for i, j in pairs if 0 <= j < count])  7.67 us
    pallas_call x2, Pallas kernels, middle(): pl.pallas_call(functools.partial(middle_kernel, s), out_shape=[quarters,...  7.36 us
    ppermute x2, waiting for transfers between devices, moved(): lax.ppermute(value, axis, [(i, j) for i, j in pairs if 0 <= j < count])  5.27 us
  transfers between devices with their start and end apart: 11, of which 6 were waited for; matrix products, arithmetic and copies ran while one was open for 4% of the time, Pallas kernels for 3%

profile of v3, /device:TPU:249, one launch (start us, length us, event | category | flops | bytes accessed | tf_op | source)
XLA Modules:
  0.0 181.7 jit_solution(3566891479087805192)
XLA Ops:
  6.5 0.8 fusion.1
  7.3 5.8 %collective-permute-start = (f32[32,256]{1,0:T(8,128)S(1)}, f32[32,256]{1,0:T(8,128)S(1)}, u32[]{:S(2)}, u32[]{:S(2)}) collective-permute-start(f32[32,256]{1,0:T(8,128)S(1)} %get-tuple-element.36), channel_id=1, source_target_pairs={{0,16},{16,32},{32,48},{48,64},{64,80},{80,96},{96,112},{112,128},... | collective-permute-start | bytes 98312 | tf_op jit(solution)/shard_map/ppermute | solution.py:45
  13.1 1.0 collective-permute-done
  14.1 0.8 pad_maximum_fusion.1
  14.9 0.8 broadcast_in_dim.6
  15.8 6.4 %all-to-all-start = ((f32[4,32,1024]{2,1,0:T(8,128)}), f32[4,32,1024]{2,1,0:T(8,128)S(1)}, u32[]{:S(2)}, u32[]{:S(2)}) async-start(f32[4,32,1024]{2,1,0:T(8,128)} %broadcast_in_dim.6), calls=%async_computation | async-start | bytes 1048576 | tf_op jit(solution)/shard_map/all_to_all | solution.py:194
  22.2 0.0 all-gather.2.cloned.1.call-start
  22.2 3.1 %collective-permute-start.1 = (f32[32,1024]{1,0:T(8,128)S(1)}, f32[32,1024]{1,0:T(8,128)S(1)}, u32[]{:S(2)}, u32[]{:S(2)}) collective-permute-start(f32[32,1024]{1,0:T(8,128)S(1)} %pad_maximum_fusion.1), channel_id=1, source_target_pairs={{0,0},{1,16},{2,32},{3,48},{4,64},{5,80},{6,96},{7,112},{8,128},{9... | collective-permute-start | bytes 393224 | tf_op jit(solution)/shard_map/ppermute | solution.py:49
  25.4 27.0 %collective-permute-done.1 = f32[32,1024]{1,0:T(8,128)S(1)} collective-permute-done((f32[32,1024]{1,0:T(8,128)S(1)}, f32[32,1024]{1,0:T(8,128)S(1)}, u32[]{:S(2)}, u32[]{:S(2)}) %collective-permute-start.1) | collective-permute-done | bytes 131104 | tf_op jit(solution)/shard_map/ppermute | solution.py:49
  52.4 0.0 all-to-all-done
  52.4 1.9 %collective-permute-start.4 = (f32[32,1024]{1,0:T(8,128)S(1)}, f32[32,1024]{1,0:T(8,128)S(1)}, u32[]{:S(2)}, u32[]{:S(2)}) collective-permute-start(f32[32,1024]{1,0:T(8,128)S(1)} %collective-permute-done.1), channel_id=1, source_target_pairs={{0,256},{16,272},{32,288},{48,304},{64,320},{80,336},{96,352},{112... | collective-permute-start | bytes 393224 | tf_op jit(solution)/shard_map/ppermute | solution.py:45
  54.3 4.3 %collective-permute-done.4 = f32[32,1024]{1,0:T(8,128)S(1)} collective-permute-done((f32[32,1024]{1,0:T(8,128)S(1)}, f32[32,1024]{1,0:T(8,128)S(1)}, u32[]{:S(2)}, u32[]{:S(2)}) %collective-permute-start.4) | collective-permute-done | bytes 131104 | tf_op jit(solution)/shard_map/ppermute | solution.py:45
  58.6 0.7 pad_maximum_fusion
  59.3 0.0 all-gather.2.cloned.1.call-update
  59.3 1.6 broadcast_in_dim.15
  60.9 3.6 %all-to-all-start.1 = ((f32[4,128,1024]{2,1,0:T(8,128)}), f32[4,128,1024]{2,1,0:T(8,128)S(1)}, u32[]{:S(2)}, u32[]{:S(2)}) async-start(f32[4,128,1024]{2,1,0:T(8,128)} %broadcast_in_dim.15), calls=%async_computation.1 | async-start | bytes 4194304 | tf_op jit(solution)/shard_map/all_to_all | solution.py:194
  64.5 0.1 pad_add_fusion.where
  64.6 4.0 %fusion = (f32[512,1,512]{2,1,0:T(1,128)S(1)}, f32[512,1,512]{2,1,0:T(1,128)S(1)}) fusion(f32[512,2,512]{2,1,0:T(2,128)} %param.4), kind=kLoop, calls=%fused_computation.5 | loop fusion | bytes 4194304 | tf_op jit(solution)/shard_map/slice | solution.py:214
  68.6 0.0 copy-start.8
  68.6 1.2 copy_bitcast_fusion
  69.8 19.4 %all-to-all-done.1 = f32[4,128,1024]{2,1,0:T(8,128)S(1)} async-done(((f32[4,128,1024]{2,1,0:T(8,128)}), f32[4,128,1024]{2,1,0:T(8,128)S(1)}, u32[]{:S(2)}, u32[]{:S(2)}) %all-to-all-start.1) | async-done | bytes 2097184 | tf_op jit(solution)/shard_map/all_to_all | solution.py:194
  89.2 0.0 copy-start.5
  89.3 1.3 copy-done.5
  90.6 0.0 copy-done.8
  90.6 0.0 copy-start.6
  90.6 1.6 copy-done.6
  92.2 0.0 copy-start.7
  92.2 1.2 copy-done.7
  93.4 2.6 %left.1 = (f32[256,1024]{1,0:T(8,128)S(1)}, f32[256,1024]{1,0:T(8,128)S(1)}, bf16[2,512,256]{2,1,0:T(8,128)(2,1)S(1)}, bf16[2,512,256]{2,1,0:T(8,128)(2,1)S(1)}) custom-call(s32[2]{0:T(128)S(1)} %pad_add_fusion.where, s32[2,32]{1,0:T(2,128)S(1)} %copy-done.8, f32[4,4,32,1024]{3,2,1,0:T(8,128)S(1)} %bitcast.12, f32[512,512]{1,0:T(8,128)S(1)} %copy-done.7, ...), custom_call_target="tpu_custom_call" | custom-call | flops 1610612736 | bytes 7340032 | tf_op jit(solution)/shard_map/left/pallas_call | solution.py:205
  96.0 0.0 copy-start.1
  96.0 0.8 copy-done.1
  96.8 0.0 copy-start.3
  96.8 0.8 copy-done.3
  97.6 4.4 %collective-permute-start.2 = (f32[256,1024]{1,0:T(8,128)S(1)}, f32[256,1024]{1,0:T(8,128)S(1)}, u32[]{:S(2)}, u32[]{:S(2)}) collective-permute-start(f32[256,1024]{1,0:T(8,128)S(1)} %get-tuple-element.20.own_a), channel_id=1, source_target_pairs={{0,16},{1,17},{2,18},{3,19},{4,20},{5,21},{6,22},{7,23},{8,24},{9,... | collective-permute-start | bytes 3145736 | tf_op jit(solution)/shard_map/ppermute | solution.py:49
  102.0 1.9 %collective-permute-start.3 = (f32[256,1024]{1,0:T(8,128)S(1)}, f32[256,1024]{1,0:T(8,128)}, u32[]{:S(2)}, u32[]{:S(2)}) collective-permute-start(f32[256,1024]{1,0:T(8,128)S(1)} %get-tuple-element.21.own_b), channel_id=1, source_target_pairs={{16,32},{17,33},{18,34},{19,35},{20,36},{21,37},{22,38},{23,39},{2... | collective-permute-start | bytes 3145736 | tf_op jit(solution)/shard_map/ppermute | solution.py:49
  104.0 0.0 all-gather.2.cloned.1.call-done
  104.0 0.0 copy-start
  104.0 2.2 %copy-done = f32[1024,1024]{1,0:T(8,128)S(1)} copy-done((f32[1024,1024]{1,0:T(8,128)S(1)}, f32[1024,1024]{1,0:T(8,128)}, u32[]{:S(2)}) %copy-start) | copy-done | bytes 4194328
  106.2 0.0 copy-start.2
  106.2 0.0 copy-start.4
  106.2 1.4 prepare.1
  107.6 0.0 collective-permute-done.2.got_a
  107.6 11.9 %collective-permute-done.3.got_b = f32[256,1024]{1,0:T(8,128)} collective-permute-done((f32[256,1024]{1,0:T(8,128)S(1)}, f32[256,1024]{1,0:T(8,128)}, u32[]{:S(2)}, u32[]{:S(2)}) %collective-permute-start.3) | collective-permute-done | bytes 1048608 | tf_op jit(solution)/shard_map/ppermute | solution.py:49
  119.5 0.0 copy-done.2
  119.5 0.0 copy-done.4
  119.5 3.7 %middle.2 = (f32[2,2,256,256]{3,2,1,0:T(8,128)S(1)}, f32[2,256,256]{2,1,0:T(8,128)S(1)}, f32[2,256,256]{2,1,0:T(8,128)S(1)}) custom-call(s32[2]{0:T(128)S(1)} %pad_add_fusion.where, s32[2,32]{1,0:T(2,128)S(1)} %copy-done.8, f32[256,1024]{1,0:T(8,128)S(1)} %get-tuple-element.20.own_a, f32[256,1024]{1,0:T(8,128)S(1)} %get-tuple-element.21.own_b, ...), custom_call_target="tpu_custom_call" | custom-call | flops 1610612736 | bytes 4194304 | tf_op jit(solution)/shard_map/middle/pallas_call | solution.py:237
  123.2 3.7 %middle.3 = (f32[2,2,256,256]{3,2,1,0:T(8,128)S(1)}, f32[2,2,256,256]{3,2,1,0:T(8,128)S(1)}, f32[2,256,256]{2,1,0:T(8,128)S(1)}) custom-call(s32[2]{0:T(128)S(1)} %pad_add_fusion.where, s32[2,32]{1,0:T(2,128)S(1)} %copy-done.8, f32[256,1024]{1,0:T(8,128)S(1)} %get-tuple-element.20.own_a, f32[256,1024]{1,0:T(8,128)S(1)} %get-tuple-element.21.own_b, ...), custom_call_target="tpu_custom_call" | custom-call | flops 1610612736 | bytes 4194304 | tf_op jit(solution)/shard_map/middle/pallas_call | solution.py:237
  126.9 2.2 %collective-permute-start.5 = (f32[2,2,256,256]{3,2,1,0:T(8,128)S(1)}, f32[2,2,256,256]{3,2,1,0:T(8,128)S(1)}, u32[]{:S(2)}, u32[]{:S(2)}) collective-permute-start(f32[2,2,256,256]{3,2,1,0:T(8,128)S(1)} %get-tuple-element.30), channel_id=1, source_target_pairs={{0,1},{2,3},{4,5},{6,7},{8,9},{10,11},{12,13},{14,15},{16,17},{18,... | collective-permute-start | bytes 3145736 | tf_op jit(solution)/shard_map/ppermute | solution.py:49
  129.1 1.9 %collective-permute-start.7 = (f32[2,256,256]{2,1,0:T(8,128)S(1)}, f32[2,256,256]{2,1,0:T(8,128)S(1)}, u32[]{:S(2)}, u32[]{:S(2)}) collective-permute-start(f32[2,256,256]{2,1,0:T(8,128)S(1)} %get-tuple-element.32), channel_id=1, source_target_pairs={{1,2},{3,4},{5,6},{7,8},{9,10},{11,12},{13,14},{17,18},{19,20},{21... | collective-permute-start | bytes 1572872 | tf_op jit(solution)/shard_map/ppermute | solution.py:49
  131.0 0.7 collective-permute-start.6
  131.7 38.0 %collective-permute-done.7.edge = f32[2,256,256]{2,1,0:T(8,128)S(1)} collective-permute-done((f32[2,256,256]{2,1,0:T(8,128)S(1)}, f32[2,256,256]{2,1,0:T(8,128)S(1)}, u32[]{:S(2)}, u32[]{:S(2)}) %collective-permute-start.7) | collective-permute-done | bytes 524320 | tf_op jit(solution)/shard_map/ppermute | solution.py:49
  169.8 0.0 collective-permute-done.5.side
  169.8 1.6 second.1
  171.3 0.0 collective-permute-done.6.edge
  171.3 3.5 %first.1 = f32[512,2,512]{2,1,0:T(2,128)} custom-call(s32[2]{0:T(128)S(1)} %pad_add_fusion.where, s32[2,32]{1,0:T(2,128)S(1)} %copy-done.8, f32[2,2,256,256]{3,2,1,0:T(8,128)S(1)} %get-tuple-element.29.kept, f32[2,2,256,256]{3,2,1,0:T(8,128)S(1)} %get-tuple-element.27.rest_0_.kept.kept_1, f32[2,2,256,256]{3,2,1,0:T(8,128)S(1)} %collective-permute-done.5.side, ...), custom_call_target="tpu_custom_call" | custom-call | flops 805306368 | bytes 4194304 | tf_op jit(solution)/shard_map/first/pallas_call | solution.py:263
Async XLA Ops:
  7.3 6.8 %collective-permute-start = (f32[32,256]{1,0:T(8,128)S(1)}, f32[32,256]{1,0:T(8,128)S(1)}, u32[]{:S(2)}, u32[]{:S(2)}) collective-permute-start(f32[32,256]{1,0:T(8,128)S(1)} %get-tuple-element.36), channel_id=1, source_target_pairs={{0,16},{16,32},{32,48},{48,64},{64,80},{80,96},{96,112},{112,128},... | collective-permute-start | bytes 98312 | tf_op jit(solution)/shard_map/ppermute | solution.py:45
  15.8 36.6 %all-to-all-start = ((f32[4,32,1024]{2,1,0:T(8,128)}), f32[4,32,1024]{2,1,0:T(8,128)S(1)}, u32[]{:S(2)}, u32[]{:S(2)}) async-start(f32[4,32,1024]{2,1,0:T(8,128)} %broadcast_in_dim.6), calls=%async_computation | async-start | bytes 1048576 | tf_op jit(solution)/shard_map/all_to_all | solution.py:194
  22.2 81.8 %all-gather.2.cloned.1.call-start = ((), (), s32[]{:S(2)}) async-start(), calls=%async_computation.2 | async-start | bytes 4456448 | tf_op jit(solution)/shard_map/all_gather | solution.py:200
  22.2 30.2 %collective-permute-start.1 = (f32[32,1024]{1,0:T(8,128)S(1)}, f32[32,1024]{1,0:T(8,128)S(1)}, u32[]{:S(2)}, u32[]{:S(2)}) collective-permute-start(f32[32,1024]{1,0:T(8,128)S(1)} %pad_maximum_fusion.1), channel_id=1, source_target_pairs={{0,0},{1,16},{2,32},{3,48},{4,64},{5,80},{6,96},{7,112},{8,128},{9... | collective-permute-start | bytes 393224 | tf_op jit(solution)/shard_map/ppermute | solution.py:49
  52.4 6.2 %collective-permute-start.4 = (f32[32,1024]{1,0:T(8,128)S(1)}, f32[32,1024]{1,0:T(8,128)S(1)}, u32[]{:S(2)}, u32[]{:S(2)}) collective-permute-start(f32[32,1024]{1,0:T(8,128)S(1)} %collective-permute-done.1), channel_id=1, source_target_pairs={{0,256},{16,272},{32,288},{48,304},{64,320},{80,336},{96,352},{112... | collective-permute-start | bytes 393224 | tf_op jit(solution)/shard_map/ppermute | solution.py:45
  60.9 28.3 %all-to-all-start.1 = ((f32[4,128,1024]{2,1,0:T(8,128)}), f32[4,128,1024]{2,1,0:T(8,128)S(1)}, u32[]{:S(2)}, u32[]{:S(2)}) async-start(f32[4,128,1024]{2,1,0:T(8,128)} %broadcast_in_dim.15), calls=%async_computation.1 | async-start | bytes 4194304 | tf_op jit(solution)/shard_map/all_to_all | solution.py:194
  68.6 21.9 %copy-start.8 = (s32[2,32]{1,0:T(2,128)S(1)}, s32[2,32]{1,0:T(2,128)}, u32[]{:S(2)}) copy-start(s32[2,32]{1,0:T(2,128)} %lives.9) | copy-start | bytes 772
  89.2 1.3 copy-start.5
  90.6 1.6 copy-start.6
  92.2 1.2 copy-start.7
  96.0 0.8 copy-start.1
  96.8 0.8 copy-start.3
  97.6 10.0 %collective-permute-start.2 = (f32[256,1024]{1,0:T(8,128)S(1)}, f32[256,1024]{1,0:T(8,128)S(1)}, u32[]{:S(2)}, u32[]{:S(2)}) collective-permute-start(f32[256,1024]{1,0:T(8,128)S(1)} %get-tuple-element.20.own_a), channel_id=1, source_target_pairs={{0,16},{1,17},{2,18},{3,19},{4,20},{5,21},{6,22},{7,23},{8,24},{9,... | collective-permute-start | bytes 3145736 | tf_op jit(solution)/shard_map/ppermute | solution.py:49
  102.0 17.4 %collective-permute-start.3 = (f32[256,1024]{1,0:T(8,128)S(1)}, f32[256,1024]{1,0:T(8,128)}, u32[]{:S(2)}, u32[]{:S(2)}) collective-permute-start(f32[256,1024]{1,0:T(8,128)S(1)} %get-tuple-element.21.own_b), channel_id=1, source_target_pairs={{16,32},{17,33},{18,34},{19,35},{20,36},{21,37},{22,38},{23,39},{2... | collective-permute-start | bytes 3145736 | tf_op jit(solution)/shard_map/ppermute | solution.py:49
  104.0 2.2 %copy-start = (f32[1024,1024]{1,0:T(8,128)S(1)}, f32[1024,1024]{1,0:T(8,128)}, u32[]{:S(2)}) copy-start(f32[1024,1024]{1,0:T(8,128)} %all-gather.2.cloned.1.call-done) | copy-start | bytes 12582916
  106.2 13.3 %copy-start.2 = (bf16[2,512,256]{2,1,0:T(8,128)(2,1)S(1)}, bf16[2,512,256]{2,1,0:T(8,128)(2,1)}, u32[]{:S(2)}) copy-start(bf16[2,512,256]{2,1,0:T(8,128)(2,1)} %copy-done.1) | copy-start | bytes 1572868
  106.2 13.3 %copy-start.4 = (bf16[2,512,256]{2,1,0:T(8,128)(2,1)S(1)}, bf16[2,512,256]{2,1,0:T(8,128)(2,1)}, u32[]{:S(2)}) copy-start(bf16[2,512,256]{2,1,0:T(8,128)(2,1)} %copy-done.3) | copy-start | bytes 1572868
  126.9 42.9 %collective-permute-start.5 = (f32[2,2,256,256]{3,2,1,0:T(8,128)S(1)}, f32[2,2,256,256]{3,2,1,0:T(8,128)S(1)}, u32[]{:S(2)}, u32[]{:S(2)}) collective-permute-start(f32[2,2,256,256]{3,2,1,0:T(8,128)S(1)} %get-tuple-element.30), channel_id=1, source_target_pairs={{0,1},{2,3},{4,5},{6,7},{8,9},{10,11},{12,13},{14,15},{16,17},{18,... | collective-permute-start | bytes 3145736 | tf_op jit(solution)/shard_map/ppermute | solution.py:49
  129.1 40.7 %collective-permute-start.7 = (f32[2,256,256]{2,1,0:T(8,128)S(1)}, f32[2,256,256]{2,1,0:T(8,128)S(1)}, u32[]{:S(2)}, u32[]{:S(2)}) collective-permute-start(f32[2,256,256]{2,1,0:T(8,128)S(1)} %get-tuple-element.32), channel_id=1, source_target_pairs={{1,2},{3,4},{5,6},{7,8},{9,10},{11,12},{13,14},{17,18},{19,20},{21... | collective-permute-start | bytes 1572872 | tf_op jit(solution)/shard_map/ppermute | solution.py:49
  131.0 40.3 %collective-permute-start.6 = (f32[2,256,256]{2,1,0:T(8,128)S(1)}, f32[2,256,256]{2,1,0:T(8,128)S(1)}, u32[]{:S(2)}, u32[]{:S(2)}) collective-permute-start(f32[2,256,256]{2,1,0:T(8,128)S(1)} %get-tuple-element.31), channel_id=1, source_target_pairs={{1,2},{3,4},{5,6},{7,8},{9,10},{11,12},{13,14},{15,0},{17,18},{19,... | collective-permute-start | bytes 1572872 | tf_op jit(solution)/shard_map/ppermute | solution.py:49
Sparse Core Ops, SparseCore 0:
  59.4 39.4 all-gather.1

commit v4 on v2

--- a/solution.py
+++ b/solution.py
@@ -13,7 +13,7 @@
 HALF = 256
 LAST = 31
 BF16, F32 = jnp.bfloat16, jnp.float32
-PARAMS = pltpu.CompilerParams(vmem_limit_bytes=28 * 1024 * 1024)
+PARAMS = pltpu.CompilerParams(vmem_limit_bytes=16 * 1024 * 1024)
 VMEM = pl.BlockSpec(memory_space=pltpu.VMEM)
 SMEM = pl.BlockSpec(memory_space=pltpu.SMEM)
 
@@ -29,6 +29,11 @@
     return one(a[0], b[0]) + (one(a[0], b[1]) + one(a[1], b[0]))
 
 
+def cost(products, megabytes):
+    flops = int(products * 3 * 2 * HALF * W * 2 * W)
+    return pl.CostEstimate(flops=flops, bytes_accessed=megabytes << 20, transcendentals=0)
+
+
 def live(ref, kind, index):
     inside = (index >= 0) & (index <= LAST - kind)
     return inside & (ref[kind, jnp.clip(index, 0, LAST)] == 1)
@@ -54,36 +59,27 @@
     return moved_on(value, pairs + [(b, a) for a, b in pairs])
 
 
-def joined(far_a, far_b, behind, own, ahead, out):
-    for index, part in enumerate((far_a, far_b)):
-        out[index * 16 : index * 16 + 16] = part[...]
-    for index, part in enumerate((behind, own, ahead)):
-        out[32 * index + 32 : 32 * index + 64] = part[...]
-
-
-def left_kernel(where, lives, own, behind, ahead, far_a, far_b, h0, h1, send_a, send_b, fb_high, fb_low, d_high, d_low):
+def in_order(pieces, x, y):
+    return slice((y * RING + x) * 32, (y * RING + x) * 32 + 32), split(pieces[x, y])
+
+
+def borders_kernel(pieces, fb_high, fb_low):
+    for x in range(RING):
+        for y in range(RING):
+            rows, (high, low) = in_order(pieces, x, y)
+            for side in range(2):
+                lanes = slice(side * HALF, side * HALF + HALF)
+                fb_high[side, rows, :] = high[:, lanes]
+                fb_low[side, rows, :] = low[:, lanes]
+
+
+def left_kernel(where, lives, pieces, h0, h1, send_a, send_b, d_high, d_low):
     row, col = where[0], where[1]
-    ring_y, ring_x = col // RING, col % RING
-
-    def place(ref, rows, x_off, y_offs):
-        for index, y_off in enumerate(y_offs):
-            at_y = lax.rem(ring_y + y_off + RING, RING)
-            at_x = lax.rem(ring_x + x_off + RING, RING)
-            start = pl.multiple_of((at_y * RING + at_x) * 32, 32)
-            part = ref[rows + 32 * index : rows + 32 * index + 32, :]
-            high, low = split(part)
-            for side in range(2):
-                lanes = slice(W + side * HALF, W + side * HALF + HALF)
-                fb_high[side, pl.ds(start, 32), :] = high[:, lanes]
-                fb_low[side, pl.ds(start, 32), :] = low[:, lanes]
-            d_high[pl.ds(start, 32), :] = high[:, :W]
-            d_low[pl.ds(start, 32), :] = low[:, :W]
-
-    place(own, 0, 0, (-2, -1, 0, 1))
-    place(behind, 0, -1, (-2, -1, 0, 1))
-    place(ahead, 0, 1, (-2, -1, 0, 1))
-    place(far_a, 0, 2, (-2, -1))
-    place(far_b, 0, 2, (0, 1))
+    for x in range(RING):
+        for y in range(RING):
+            rows, (high, low) = in_order(pieces, x, y)
+            d_high[rows, :] = high
+            d_low[rows, :] = low
     odd = lax.rem(row, 2) == 1
     live_row = live(lives, 0, row)
     factor = (d_high[...], d_low[...])
@@ -96,9 +92,10 @@
         send_b[:, lanes] = jnp.where(odd, value[HALF:], value[:HALF])
 
 
-def prepare_kernel(gathered, high, low):
-    value = gathered[...].reshape(high.shape[1], high.shape[2])
-    high[0], low[0] = split(value)
+def prepare_kernel(where, gathered, high, low):
+    for index in range(16):
+        rows = slice(32 * index, 32 * index + 32)
+        high[0, rows, :], low[0, rows, :] = split(gathered[lax.rem(where[1] + index, 16), 0])
 
 
 def middle_kernel(first, where, lives, own, got, fb_high, fb_low, c_high, c_low, kept, side, edge0, edge1):
@@ -145,7 +142,7 @@
     edge1[...] = jnp.where(odd_col, ends[1][1], ends[1][0])
 
 
-def last_kernel(first, where, lives, kept, side, edge0, edge1, c_high, c_low, *rest):
+def last_kernel(first, where, lives, kept, side, edge1, edge0, c_high, c_low, *rest):
     out = rest[-1]
     row, col = where[0], where[1]
     odd = lax.rem(row, 2) == 1
@@ -179,37 +176,42 @@
     above = moved(border[:, HALF:], "row", lambda r: r + 1)
     piece = jnp.concatenate([diag_factors[0], border[:, :HALF], above], 1)
 
-    mine = moved_on(piece, everywhere(lambda r, c: True, lambda r, c: (r // 16 * 16 + c, r % 16)))
-    other = moved_on(piece, everywhere(lambda r, c: True, lambda r, c: (16 - r // 16 * 16 + c, r % 16)))
-    lower = row >= 16
-    both = jnp.concatenate([jnp.where(lower, other, mine), jnp.where(lower, mine, other)], 0)
+    mine = moved_on(piece, everywhere(lambda r, c: True, lambda r, c: (r // 16 * 16 + (r + c) % 16, r % 16)))
+    other = moved(mine, "row", lambda r: r ^ 16)
     groups = [list(range(16)), list(range(16, 32))]
-    gathered = lax.all_gather(both, "row", axis=0, tiled=True, axis_index_groups=groups)
+    gathered = lax.all_gather(jnp.concatenate([mine, other], 0), "row", axis=0, tiled=True, axis_index_groups=groups)
     gathered = gathered.reshape(16, 2, 32, 2 * W)
 
-    along_y = lambda s: (lambda c: (c + RING * s) % GRID_COLS)
-    along_x = lambda s: (lambda c: c // RING * RING + (c + s) % RING)
-    behind = moved(piece, "col", along_y(1))
-    ahead = moved(piece, "col", along_y(-1))
-    far_a = moved(behind[:16], "col", along_y(1))
-    far_b = moved(ahead[16:], "col", along_y(-1))
-    block = pl.pallas_call(
-        joined, out_shape=shape((128, 2 * W), F32), in_specs=[VMEM] * 5, out_specs=VMEM, name="joined"
-    )(far_a, far_b, behind, piece, ahead)
-    behind = moved(block, "col", along_x(1))
-    ahead = moved(block, "col", along_x(-1))
-    far_a = moved(behind[:64], "col", along_x(1))
-    far_b = moved(ahead[64:], "col", along_x(-1))
-
-    send_a, send_b, fb_high, fb_low = pl.pallas_call(
+    def shared(value, groups):
+        every = jnp.broadcast_to(value[None], (RING, *value.shape))
+        return lax.all_to_all(every, "col", 0, 0, axis_index_groups=groups)
+
+    by_y = shared(piece, [[x + RING * y for y in range(RING)] for x in range(RING)])
+    by_y = by_y.reshape(RING * 32, 2 * W)
+    along_x = [[x + RING * y for x in range(RING)] for y in range(RING)]
+    diag_row = shared(by_y[:, :W], along_x).reshape(RING, RING, 32, W)
+    diag_row, border_y = lax.optimization_barrier((diag_row, by_y[:, W:]))
+    border_row = shared(border_y, along_x).reshape(RING, RING, 32, W)
+    fb_high, fb_low = pl.pallas_call(
+        borders_kernel,
+        out_shape=[shape((2, W, HALF), BF16)] * 2,
+        in_specs=[VMEM],
+        out_specs=[VMEM] * 2,
+        compiler_params=PARAMS,
+        cost_estimate=cost(0, 2),
+        name="borders",
+    )(border_row)
+
+    send_a, send_b = pl.pallas_call(
         left_kernel,
-        out_shape=[shape((HALF, 2 * W), F32)] * 2 + [shape((2, W, HALF), BF16)] * 2,
-        in_specs=[SMEM, SMEM] + [VMEM] * 7,
-        out_specs=[VMEM] * 4,
+        out_shape=[shape((HALF, 2 * W), F32)] * 2,
+        in_specs=[SMEM, SMEM] + [VMEM] * 3,
+        out_specs=[VMEM] * 2,
         scratch_shapes=[pltpu.VMEM((W, W), BF16)] * 2,
         compiler_params=PARAMS,
+        cost_estimate=cost(2, 7),
         name="left",
-    )(where, window_live, block, behind, ahead, far_a, far_b, hessenberg[:, 0], hessenberg[:, 1])
+    )(where, window_live, diag_row, hessenberg[:, 0], hessenberg[:, 1])
 
     every_col = range(GRID_COLS)
     got_b = swapped(send_b, [((r, c), (r + 1, c)) for r in range(1, 31, 2) for c in every_col])
@@ -217,13 +219,17 @@
 
     c_high, c_low = pl.pallas_call(
         prepare_kernel,
-        grid=(2,),
         out_shape=[shape((2, W, 2 * W), BF16)] * 2,
-        in_specs=[pl.BlockSpec((16, 1, 32, 2 * W), lambda s: (0, s, 0, 0))],
-        out_specs=[pl.BlockSpec((1, W, 2 * W), lambda s: (s, 0, 0))] * 2,
+        grid_spec=pltpu.PrefetchScalarGridSpec(
+            num_scalar_prefetch=1,
+            grid=(2,),
+            in_specs=[pl.BlockSpec((16, 1, 32, 2 * W), lambda s, where: (0, s ^ (where[0] // 16), 0, 0))],
+            out_specs=[pl.BlockSpec((1, W, 2 * W), lambda s, where: (s, 0, 0))] * 2,
+        ),
         compiler_params=PARAMS,
+        cost_estimate=cost(0, 8),
         name="prepare",
-    )(gathered)
+    )(where, gathered)
 
     def middle(first, own, got):
         return pl.pallas_call(
@@ -232,15 +238,16 @@
             in_specs=[SMEM, SMEM] + [VMEM] * 6,
             out_specs=[VMEM] * 4,
             compiler_params=PARAMS,
+            cost_estimate=cost(2, 4),
             name="middle",
         )(where, window_live, own, got, fb_high, fb_low, c_high, c_low)
 
     def exchanged(side, edge0, edge1):
         rows = range(GRID_ROWS)
+        side = swapped(side, [((r, c), (r, c + 1)) for r in rows for c in range(0, 16, 2) if r <= c + 17])
+        edge0 = swapped(edge0, [((r, c), (r, (c + 1) % 16)) for r in rows for c in range(1, 16, 2) if r <= c + 1])
         edge1 = swapped(edge1, [((r, c), (r, c + 1)) for r in rows for c in range(1, 15, 2) if r <= c + 17])
-        edge0 = swapped(edge0, [((r, c), (r, (c + 1) % 16)) for r in rows for c in range(1, 16, 2) if r <= c + 1])
-        side = swapped(side, [((r, c), (r, c + 1)) for r in rows for c in range(0, 16, 2) if r <= c + 17])
-        return side, edge0, edge1
+        return side, edge1, edge0
 
     def last(first, kept, moved_parts, *done):
         place = lambda i, where: (lax.rem(where[0], 2) ^ (1 if first else 0), 0, 0)
@@ -266,6 +273,7 @@
             ),
             input_output_aliases={8: 0} if done else {},
             compiler_params=PARAMS,
+            cost_estimate=cost(1, 4),
             name="last",
         )(where, window_live, kept, *moved_parts, c_high, c_low, *done)
 

time: 180 us -> 172 us (0.956)
  the two profiles are of different devices: /device:TPU:7 before, /device:TPU:150 now
where the time goes in v4:
time: 172 us; the launch traced here: 171 us
  starting transfers between devices  57.8 us (34%)
  waiting for transfers between devices  50.3 us (29%)
  Pallas kernels  18.8 us (11%)
  blocking collectives  17.1 us (10%)
  between operations  13.6 us (8%)
  local copies, waits for them, and re-layouts  11.6 us (7%)
    ppermute x9, starting transfers between devices, moved_on(): lax.ppermute(value, ('row', 'col'), [(r * GRID_COLS + c, t * GRID_COLS +...  36.8 us
    ppermute x9, waiting for transfers between devices, moved_on(): lax.ppermute(value, ('row', 'col'), [(r * GRID_COLS + c, t * GRID_COLS +...  21 us
    all_to_all x2, waiting for transfers between devices, shared(): return lax.all_to_all(every, 'col', 0, 0, axis_index_groups=groups)  20.2 us
    all_to_all x1, blocking collectives, shared(): return lax.all_to_all(every, 'col', 0, 0, axis_index_groups=groups)  17.1 us
    all_to_all x2, starting transfers between devices, shared(): return lax.all_to_all(every, 'col', 0, 0, axis_index_groups=groups)  16.7 us
    ppermute x2, waiting for transfers between devices, moved(): lax.ppermute(value, axis, [(i, j) for i, j in pairs if 0 <= j < count])  9.08 us
    pallas_call x2, Pallas kernels, middle(): pl.pallas_call(functools.partial(middle_kernel, first), out_shape=[shape(...  7.01 us
    pallas_call x2, Pallas kernels, last(): pl.pallas_call(functools.partial(last_kernel, first), out_shape=shape((W,...  6.79 us
  transfers between devices with their start and end apart: 14, of which 7 were waited for; matrix products, arithmetic and copies ran while one was open for 4% of the time, Pallas kernels for 9%

profile of v4, /device:TPU:150, one launch (start us, length us, event | category | flops | bytes accessed | tf_op | source)
XLA Modules:
  0.0 170.8 jit_solution(3285433135103966174)
XLA Ops:
  6.5 0.0 all-gather.2.cloned.1.call-start
  6.5 0.8 fusion.2
  7.3 1.9 %collective-permute-start = (f32[32,256]{1,0:T(8,128)S(1)}, f32[32,256]{1,0:T(8,128)S(1)}, u32[]{:S(2)}, u32[]{:S(2)}) collective-permute-start(f32[32,256]{1,0:T(8,128)S(1)} %get-tuple-element.42), channel_id=1, source_target_pairs={{0,16},{16,32},{32,48},{48,64},{64,80},{80,96},{96,112},{112,128},... | collective-permute-start | bytes 98312 | tf_op jit(solution)/shard_map/ppermute | solution.py:45
  9.2 3.3 %collective-permute-done = f32[32,256]{1,0:T(8,128)S(1)} collective-permute-done((f32[32,256]{1,0:T(8,128)S(1)}, f32[32,256]{1,0:T(8,128)S(1)}, u32[]{:S(2)}, u32[]{:S(2)}) %collective-permute-start) | collective-permute-done | bytes 32800 | tf_op jit(solution)/shard_map/ppermute | solution.py:45
  12.5 0.8 pad_maximum_fusion.1
  13.4 7.0 %collective-permute-start.2 = (f32[32,1024]{1,0:T(8,128)S(1)}, f32[32,1024]{1,0:T(8,128)S(1)}, u32[]{:S(2)}, u32[]{:S(2)}) collective-permute-start(f32[32,1024]{1,0:T(8,128)S(1)} %pad_maximum_fusion.1), channel_id=1, source_target_pairs={{0,0},{1,16},{2,32},{3,48},{4,64},{5,80},{6,96},{7,112},{8,128},{9... | collective-permute-start | bytes 393224 | tf_op jit(solution)/shard_map/ppermute | solution.py:49
  20.4 8.5 %collective-permute-done.2 = f32[32,1024]{1,0:T(8,128)S(1)} collective-permute-done((f32[32,1024]{1,0:T(8,128)S(1)}, f32[32,1024]{1,0:T(8,128)S(1)}, u32[]{:S(2)}, u32[]{:S(2)}) %collective-permute-start.2) | collective-permute-done | bytes 131104 | tf_op jit(solution)/shard_map/ppermute | solution.py:49
  28.9 2.4 %collective-permute-start.3 = (f32[32,1024]{1,0:T(8,128)S(1)}, f32[32,1024]{1,0:T(8,128)S(1)}, u32[]{:S(2)}, u32[]{:S(2)}) collective-permute-start(f32[32,1024]{1,0:T(8,128)S(1)} %collective-permute-done.2), channel_id=1, source_target_pairs={{0,256},{16,272},{32,288},{48,304},{64,320},{80,336},{96,352},{112... | collective-permute-start | bytes 393224 | tf_op jit(solution)/shard_map/ppermute | solution.py:45
  31.2 5.8 %collective-permute-done.3 = f32[32,1024]{1,0:T(8,128)S(1)} collective-permute-done((f32[32,1024]{1,0:T(8,128)S(1)}, f32[32,1024]{1,0:T(8,128)S(1)}, u32[]{:S(2)}, u32[]{:S(2)}) %collective-permute-start.3) | collective-permute-done | bytes 131104 | tf_op jit(solution)/shard_map/ppermute | solution.py:45
  37.0 0.7 pad_maximum_fusion
  37.8 0.0 all-gather.2.cloned.1.call-update
  37.8 0.8 broadcast_in_dim.6
  38.6 8.1 %all-to-all-start = ((f32[4,32,1024]{2,1,0:T(8,128)}), f32[4,32,1024]{2,1,0:T(8,128)S(1)}, u32[]{:S(2)}, u32[]{:S(2)}) async-start(f32[4,32,1024]{2,1,0:T(8,128)} %broadcast_in_dim.6), calls=%async_computation | async-start | bytes 1048576 | tf_op jit(solution)/shard_map/all_to_all | solution.py:187
  46.7 12.6 %all-to-all-done = f32[4,32,1024]{2,1,0:T(8,128)S(1)} async-done(((f32[4,32,1024]{2,1,0:T(8,128)}), f32[4,32,1024]{2,1,0:T(8,128)S(1)}, u32[]{:S(2)}, u32[]{:S(2)}) %all-to-all-start) | async-done | bytes 524320 | tf_op jit(solution)/shard_map/all_to_all | solution.py:187
  59.3 1.1 broadcast_in_dim.7
  60.4 8.7 %all-to-all-start.1 = ((f32[4,128,512]{2,1,0:T(8,128)}), f32[4,128,512]{2,1,0:T(8,128)S(1)}, u32[]{:S(2)}, u32[]{:S(2)}) async-start(f32[4,128,512]{2,1,0:T(8,128)} %broadcast_in_dim.7), calls=%async_computation.1 | async-start | bytes 2097152 | tf_op jit(solution)/shard_map/all_to_all | solution.py:187
  69.0 0.1 pad_add_fusion.where
  69.1 4.1 %fusion = (f32[512,1,512]{2,1,0:T(1,128)S(1)}, f32[512,1,512]{2,1,0:T(1,128)S(1)}) fusion(f32[512,2,512]{2,1,0:T(2,128)} %param.4), kind=kLoop, calls=%fused_computation.5 | loop fusion | bytes 4194304 | tf_op jit(solution)/shard_map/slice | solution.py:214
  73.2 0.0 copy-start.2
  73.2 1.2 copy_bitcast_fusion
  74.4 7.7 %all-to-all-done.1 = f32[4,128,512]{2,1,0:T(8,128)S(1)} async-done(((f32[4,128,512]{2,1,0:T(8,128)}), f32[4,128,512]{2,1,0:T(8,128)S(1)}, u32[]{:S(2)}, u32[]{:S(2)}) %all-to-all-start.1) | async-done | bytes 1048608 | tf_op jit(solution)/shard_map/all_to_all | solution.py:187
  82.0 0.0 copy-done.2
  82.0 0.0 copy-start.1
  82.0 1.2 copy-done.1
  83.3 3.5 %left.1 = (f32[256,1024]{1,0:T(8,128)}, f32[256,1024]{1,0:T(8,128)S(1)}) custom-call(s32[2]{0:T(128)S(1)} %pad_add_fusion.where, s32[2,32]{1,0:T(2,128)S(1)} %copy-done.2, f32[4,4,32,512]{3,2,1,0:T(8,128)S(1)} %bitcast.14, f32[512,512]{1,0:T(8,128)S(1)} %copy-done.1, f32[512,512]{1,0:T(8,128)S(1)} %get-tuple-element.43.h1), custom_call_target="tpu_custom_call" | custom-call | flops 1610612736 | bytes 7340032 | tf_op jit(solution)/shard_map/left/pallas_call | solution.py:205
  86.8 1.9 %collective-permute-start.7 = (f32[256,1024]{1,0:T(8,128)}, f32[256,1024]{1,0:T(8,128)}, u32[]{:S(2)}, u32[]{:S(2)}) collective-permute-start(f32[256,1024]{1,0:T(8,128)} %get-tuple-element.32.own), channel_id=1, source_target_pairs={{0,16},{1,17},{2,18},{3,19},{4,20},{5,21},{6,22},{7,23},{8,24},{9,... | collective-permute-start | bytes 3145736 | tf_op jit(solution)/shard_map/ppermute | solution.py:49
  88.7 1.9 %collective-permute-start.1 = (f32[256,1024]{1,0:T(8,128)S(1)}, f32[256,1024]{1,0:T(8,128)S(1)}, u32[]{:S(2)}, u32[]{:S(2)}) collective-permute-start(f32[256,1024]{1,0:T(8,128)S(1)} %get-tuple-element.22.own), channel_id=1, source_target_pairs={{16,32},{17,33},{18,34},{19,35},{20,36},{21,37},{22,38},{23,39},{2... | collective-permute-start | bytes 3145736 | tf_op jit(solution)/shard_map/ppermute | solution.py:49
  90.6 0.1 broadcast_in_dim.8
  90.8 17.1 %all_to_all.15 = f32[4,128,512]{2,1,0:T(8,128)S(1)} all-to-all(f32[4,128,512]{2,1,0:T(8,128)S(1)} %broadcast_in_dim.8), channel_id=1, replica_groups={{0,1,2,3},{4,5,6,7},{8,9,10,11},{12,13,14,15},{16,17,18,19},{20,21,22,2..., dimensions={0} | all-to-all | bytes 2097152 | tf_op jit(solution)/shard_map/all_to_all | solution.py:187
  107.9 0.1 borders.1
  108.0 0.0 all-gather.2.cloned.1.call-done
  108.0 0.0 copy-start
  108.0 2.2 %copy-done = f32[1024,1024]{1,0:T(8,128)S(1)} copy-done((f32[1024,1024]{1,0:T(8,128)S(1)}, f32[1024,1024]{1,0:T(8,128)}, u32[]{:S(2)}) %copy-start) | copy-done | bytes 4194328
  110.2 1.4 prepare.1
  111.6 0.0 collective-permute-done.7.got
  111.6 4.0 %middle.3 = (f32[4,256,256]{2,1,0:T(8,128)S(1)}, f32[2,256,256]{2,1,0:T(8,128)S(1)}, f32[256,256]{1,0:T(8,128)S(1)}, f32[256,256]{1,0:T(8,128)S(1)}) custom-call(s32[2]{0:T(128)S(1)} %pad_add_fusion.where, s32[2,32]{1,0:T(2,128)S(1)} %copy-done.2, f32[256,1024]{1,0:T(8,128)} %get-tuple-element.32.own, f32[256,1024]{1,0:T(8,128)} %collective-permute-done.7.got, ...), custom_call_target="tpu_custom_call" | custom-call | flops 1610612736 | bytes 4194304 | tf_op jit(solution)/shard_map/middle/pallas_call | solution.py:235
  115.6 4.8 %collective-permute-start.9 = (f32[256,256]{1,0:T(8,128)S(1)}, f32[256,256]{1,0:T(8,128)S(1)}, u32[]{:S(2)}, u32[]{:S(2)}) collective-permute-start(f32[256,256]{1,0:T(8,128)S(1)} %get-tuple-element.35), channel_id=1, source_target_pairs={{1,2},{3,4},{5,6},{7,8},{9,10},{11,12},{13,14},{17,18},{19,20},{21... | collective-permute-start | bytes 786440 | tf_op jit(solution)/shard_map/ppermute | solution.py:49
  120.5 1.9 %collective-permute-start.8 = (f32[2,256,256]{2,1,0:T(8,128)S(1)}, f32[2,256,256]{2,1,0:T(8,128)S(1)}, u32[]{:S(2)}, u32[]{:S(2)}) collective-permute-start(f32[2,256,256]{2,1,0:T(8,128)S(1)} %get-tuple-element.34), channel_id=1, source_target_pairs={{0,1},{2,3},{4,5},{6,7},{8,9},{10,11},{12,13},{14,15},{16,17},{18,... | collective-permute-start | bytes 1572872 | tf_op jit(solution)/shard_map/ppermute | solution.py:49
  122.4 0.0 collective-permute-done.1.got
  122.4 3.0 %middle.2 = (f32[4,256,256]{2,1,0:T(8,128)S(1)}, f32[2,256,256]{2,1,0:T(8,128)S(1)}, f32[256,256]{1,0:T(8,128)S(1)}, f32[256,256]{1,0:T(8,128)S(1)}) custom-call(s32[2]{0:T(128)S(1)} %pad_add_fusion.where, s32[2,32]{1,0:T(2,128)S(1)} %copy-done.2, f32[256,1024]{1,0:T(8,128)S(1)} %get-tuple-element.22.own, f32[256,1024]{1,0:T(8,128)S(1)} %collective-permute-done.1.got, ...), custom_call_target="tpu_custom_call" | custom-call | flops 1610612736 | bytes 4194304 | tf_op jit(solution)/shard_map/middle/pallas_call | solution.py:235
  125.4 3.9 %collective-permute-start.4 = (f32[2,256,256]{2,1,0:T(8,128)S(1)}, f32[2,256,256]{2,1,0:T(8,128)S(1)}, u32[]{:S(2)}, u32[]{:S(2)}) collective-permute-start(f32[2,256,256]{2,1,0:T(8,128)S(1)} %get-tuple-element.29), channel_id=1, source_target_pairs={{0,1},{2,3},{4,5},{6,7},{8,9},{10,11},{12,13},{14,15},{16,17},{18,... | collective-permute-start | bytes 1572872 | tf_op jit(solution)/shard_map/ppermute | solution.py:49
  129.4 5.2 %collective-permute-start.10 = (f32[256,256]{1,0:T(8,128)S(1)}, f32[256,256]{1,0:T(8,128)S(1)}, u32[]{:S(2)}, u32[]{:S(2)}) collective-permute-start(f32[256,256]{1,0:T(8,128)S(1)} %get-tuple-element.36), channel_id=1, source_target_pairs={{1,2},{3,4},{5,6},{7,8},{9,10},{11,12},{13,14},{15,0},{17,18},{19,... | collective-permute-start | bytes 786440 | tf_op jit(solution)/shard_map/ppermute | solution.py:49
  134.6 4.8 %collective-permute-start.5 = (f32[256,256]{1,0:T(8,128)S(1)}, f32[256,256]{1,0:T(8,128)S(1)}, u32[]{:S(2)}, u32[]{:S(2)}) collective-permute-start(f32[256,256]{1,0:T(8,128)S(1)} %get-tuple-element.30), channel_id=1, source_target_pairs={{1,2},{3,4},{5,6},{7,8},{9,10},{11,12},{13,14},{17,18},{19,20},{21... | collective-permute-start | bytes 786440 | tf_op jit(solution)/shard_map/ppermute | solution.py:49
  139.4 0.0 collective-permute-done.9.edge1
  139.5 5.2 %collective-permute-start.6 = (f32[256,256]{1,0:T(8,128)S(1)}, f32[256,256]{1,0:T(8,128)S(1)}, u32[]{:S(2)}, u32[]{:S(2)}) collective-permute-start(f32[256,256]{1,0:T(8,128)S(1)} %get-tuple-element.31), channel_id=1, source_target_pairs={{1,2},{3,4},{5,6},{7,8},{9,10},{11,12},{13,14},{15,0},{17,18},{19,... | collective-permute-start | bytes 786440 | tf_op jit(solution)/shard_map/ppermute | solution.py:49
  144.7 0.0 collective-permute-done.10.edge0
  144.7 0.0 collective-permute-done.8.side
  144.7 3.4 %last.2.rest_0_ = f32[512,2,512]{2,1,0:T(2,128)} custom-call(s32[2]{0:T(128)S(1)} %pad_add_fusion.where, s32[2,32]{1,0:T(2,128)S(1)} %copy-done.2, f32[4,256,256]{2,1,0:T(8,128)S(1)} %get-tuple-element.33.kept, f32[2,256,256]{2,1,0:T(8,128)S(1)} %collective-permute-done.8.side, f32[256,256]{1,0:T(8,128)S(1)} %collective-permute-done.9.edge1, ...), custom_call_target="tpu_custom_call" | custom-call | flops 805306368 | bytes 4194304 | tf_op jit(solution)/shard_map/last/pallas_call | solution.py:265
  148.1 7.2 %collective-permute-done.5.edge1 = f32[256,256]{1,0:T(8,128)S(1)} collective-permute-done((f32[256,256]{1,0:T(8,128)S(1)}, f32[256,256]{1,0:T(8,128)S(1)}, u32[]{:S(2)}, u32[]{:S(2)}) %collective-permute-start.5) | collective-permute-done | bytes 262176 | tf_op jit(solution)/shard_map/ppermute | solution.py:49
  155.3 5.2 %collective-permute-done.6.edge0 = f32[256,256]{1,0:T(8,128)S(1)} collective-permute-done((f32[256,256]{1,0:T(8,128)S(1)}, f32[256,256]{1,0:T(8,128)S(1)}, u32[]{:S(2)}, u32[]{:S(2)}) %collective-permute-start.6) | collective-permute-done | bytes 262176 | tf_op jit(solution)/shard_map/ppermute | solution.py:49
  160.6 0.0 collective-permute-done.4.side
  160.6 3.4 %last.3 = f32[512,2,512]{2,1,0:T(2,128)} custom-call(s32[2]{0:T(128)S(1)} %pad_add_fusion.where, s32[2,32]{1,0:T(2,128)S(1)} %copy-done.2, f32[4,256,256]{2,1,0:T(8,128)S(1)} %get-tuple-element.28.kept, f32[2,256,256]{2,1,0:T(8,128)S(1)} %collective-permute-done.4.side, f32[256,256]{1,0:T(8,128)S(1)} %collective-permute-done.5.edge1, ...), custom_call_target="tpu_custom_call", output_to_operand_aliasing={{}: (8, {})} | custom-call | flops 805306368 | bytes 4194304 | tf_op jit(solution)/shard_map/last/pallas_call | solution.py:265
  (1 shorter events, 0.0 us)
Async XLA Ops:
  6.5 101.5 %all-gather.2.cloned.1.call-start = ((), (), s32[]{:S(2)}) async-start(), calls=%async_computation.3 | async-start | bytes 4456448 | tf_op jit(solution)/shard_map/all_gather | solution.py:182
  7.3 5.2 %collective-permute-start = (f32[32,256]{1,0:T(8,128)S(1)}, f32[32,256]{1,0:T(8,128)S(1)}, u32[]{:S(2)}, u32[]{:S(2)}) collective-permute-start(f32[32,256]{1,0:T(8,128)S(1)} %get-tuple-element.42), channel_id=1, source_target_pairs={{0,16},{16,32},{32,48},{48,64},{64,80},{80,96},{96,112},{112,128},... | collective-permute-start | bytes 98312 | tf_op jit(solution)/shard_map/ppermute | solution.py:45
  13.4 15.5 %collective-permute-start.2 = (f32[32,1024]{1,0:T(8,128)S(1)}, f32[32,1024]{1,0:T(8,128)S(1)}, u32[]{:S(2)}, u32[]{:S(2)}) collective-permute-start(f32[32,1024]{1,0:T(8,128)S(1)} %pad_maximum_fusion.1), channel_id=1, source_target_pairs={{0,0},{1,16},{2,32},{3,48},{4,64},{5,80},{6,96},{7,112},{8,128},{9... | collective-permute-start | bytes 393224 | tf_op jit(solution)/shard_map/ppermute | solution.py:49
  28.9 8.1 %collective-permute-start.3 = (f32[32,1024]{1,0:T(8,128)S(1)}, f32[32,1024]{1,0:T(8,128)S(1)}, u32[]{:S(2)}, u32[]{:S(2)}) collective-permute-start(f32[32,1024]{1,0:T(8,128)S(1)} %collective-permute-done.2), channel_id=1, source_target_pairs={{0,256},{16,272},{32,288},{48,304},{64,320},{80,336},{96,352},{112... | collective-permute-start | bytes 393224 | tf_op jit(solution)/shard_map/ppermute | solution.py:45
  38.6 20.6 %all-to-all-start = ((f32[4,32,1024]{2,1,0:T(8,128)}), f32[4,32,1024]{2,1,0:T(8,128)S(1)}, u32[]{:S(2)}, u32[]{:S(2)}) async-start(f32[4,32,1024]{2,1,0:T(8,128)} %broadcast_in_dim.6), calls=%async_computation | async-start | bytes 1048576 | tf_op jit(solution)/shard_map/all_to_all | solution.py:187
  60.4 21.6 %all-to-all-start.1 = ((f32[4,128,512]{2,1,0:T(8,128)}), f32[4,128,512]{2,1,0:T(8,128)S(1)}, u32[]{:S(2)}, u32[]{:S(2)}) async-start(f32[4,128,512]{2,1,0:T(8,128)} %broadcast_in_dim.7), calls=%async_computation.1 | async-start | bytes 2097152 | tf_op jit(solution)/shard_map/all_to_all | solution.py:187
  73.2 8.8 %copy-start.2 = (s32[2,32]{1,0:T(2,128)S(1)}, s32[2,32]{1,0:T(2,128)}, u32[]{:S(2)}) copy-start(s32[2,32]{1,0:T(2,128)} %lives.9) | copy-start | bytes 772
  82.0 1.2 copy-start.1
  86.8 24.8 %collective-permute-start.7 = (f32[256,1024]{1,0:T(8,128)}, f32[256,1024]{1,0:T(8,128)}, u32[]{:S(2)}, u32[]{:S(2)}) collective-permute-start(f32[256,1024]{1,0:T(8,128)} %get-tuple-element.32.own), channel_id=1, source_target_pairs={{0,16},{1,17},{2,18},{3,19},{4,20},{5,21},{6,22},{7,23},{8,24},{9,... | collective-permute-start | bytes 3145736 | tf_op jit(solution)/shard_map/ppermute | solution.py:49
  88.7 33.7 %collective-permute-start.1 = (f32[256,1024]{1,0:T(8,128)S(1)}, f32[256,1024]{1,0:T(8,128)S(1)}, u32[]{:S(2)}, u32[]{:S(2)}) collective-permute-start(f32[256,1024]{1,0:T(8,128)S(1)} %get-tuple-element.22.own), channel_id=1, source_target_pairs={{16,32},{17,33},{18,34},{19,35},{20,36},{21,37},{22,38},{23,39},{2... | collective-permute-start | bytes 3145736 | tf_op jit(solution)/shard_map/ppermute | solution.py:49
  108.0 2.2 %copy-start = (f32[1024,1024]{1,0:T(8,128)S(1)}, f32[1024,1024]{1,0:T(8,128)}, u32[]{:S(2)}) copy-start(f32[1024,1024]{1,0:T(8,128)} %all-gather.2.cloned.1.call-done) | copy-start | bytes 12582916
  115.6 23.8 %collective-permute-start.9 = (f32[256,256]{1,0:T(8,128)S(1)}, f32[256,256]{1,0:T(8,128)S(1)}, u32[]{:S(2)}, u32[]{:S(2)}) collective-permute-start(f32[256,256]{1,0:T(8,128)S(1)} %get-tuple-element.35), channel_id=1, source_target_pairs={{1,2},{3,4},{5,6},{7,8},{9,10},{11,12},{13,14},{17,18},{19,20},{21... | collective-permute-start | bytes 786440 | tf_op jit(solution)/shard_map/ppermute | solution.py:49
  120.5 24.2 %collective-permute-start.8 = (f32[2,256,256]{2,1,0:T(8,128)S(1)}, f32[2,256,256]{2,1,0:T(8,128)S(1)}, u32[]{:S(2)}, u32[]{:S(2)}) collective-permute-start(f32[2,256,256]{2,1,0:T(8,128)S(1)} %get-tuple-element.34), channel_id=1, source_target_pairs={{0,1},{2,3},{4,5},{6,7},{8,9},{10,11},{12,13},{14,15},{16,17},{18,... | collective-permute-start | bytes 1572872 | tf_op jit(solution)/shard_map/ppermute | solution.py:49
  125.4 35.1 %collective-permute-start.4 = (f32[2,256,256]{2,1,0:T(8,128)S(1)}, f32[2,256,256]{2,1,0:T(8,128)S(1)}, u32[]{:S(2)}, u32[]{:S(2)}) collective-permute-start(f32[2,256,256]{2,1,0:T(8,128)S(1)} %get-tuple-element.29), channel_id=1, source_target_pairs={{0,1},{2,3},{4,5},{6,7},{8,9},{10,11},{12,13},{14,15},{16,17},{18,... | collective-permute-start | bytes 1572872 | tf_op jit(solution)/shard_map/ppermute | solution.py:49
  129.4 15.3 %collective-permute-start.10 = (f32[256,256]{1,0:T(8,128)S(1)}, f32[256,256]{1,0:T(8,128)S(1)}, u32[]{:S(2)}, u32[]{:S(2)}) collective-permute-start(f32[256,256]{1,0:T(8,128)S(1)} %get-tuple-element.36), channel_id=1, source_target_pairs={{1,2},{3,4},{5,6},{7,8},{9,10},{11,12},{13,14},{15,0},{17,18},{19,... | collective-permute-start | bytes 786440 | tf_op jit(solution)/shard_map/ppermute | solution.py:49
  134.6 20.7 %collective-permute-start.5 = (f32[256,256]{1,0:T(8,128)S(1)}, f32[256,256]{1,0:T(8,128)S(1)}, u32[]{:S(2)}, u32[]{:S(2)}) collective-permute-start(f32[256,256]{1,0:T(8,128)S(1)} %get-tuple-element.30), channel_id=1, source_target_pairs={{1,2},{3,4},{5,6},{7,8},{9,10},{11,12},{13,14},{17,18},{19,20},{21... | collective-permute-start | bytes 786440 | tf_op jit(solution)/shard_map/ppermute | solution.py:49
  139.5 21.1 %collective-permute-start.6 = (f32[256,256]{1,0:T(8,128)S(1)}, f32[256,256]{1,0:T(8,128)S(1)}, u32[]{:S(2)}, u32[]{:S(2)}) collective-permute-start(f32[256,256]{1,0:T(8,128)S(1)} %get-tuple-element.31), channel_id=1, source_target_pairs={{1,2},{3,4},{5,6},{7,8},{9,10},{11,12},{13,14},{15,0},{17,18},{19,... | collective-permute-start | bytes 786440 | tf_op jit(solution)/shard_map/ppermute | solution.py:49
Sparse Core Ops, SparseCore 0:
  37.9 47.6 all-gather.1

commit v5 on v4

--- a/solution.py
+++ b/solution.py
@@ -59,27 +59,18 @@
     return moved_on(value, pairs + [(b, a) for a, b in pairs])
 
 
-def in_order(pieces, x, y):
-    return slice((y * RING + x) * 32, (y * RING + x) * 32 + 32), split(pieces[x, y])
-
-
-def borders_kernel(pieces, fb_high, fb_low):
-    for x in range(RING):
-        for y in range(RING):
-            rows, (high, low) = in_order(pieces, x, y)
-            for side in range(2):
-                lanes = slice(side * HALF, side * HALF + HALF)
-                fb_high[side, rows, :] = high[:, lanes]
-                fb_low[side, rows, :] = low[:, lanes]
-
-
-def left_kernel(where, lives, pieces, h0, h1, send_a, send_b, d_high, d_low):
+def left_kernel(where, lives, pieces, h0, h1, send_a, send_b, fb_high, fb_low, d_high, d_low):
     row, col = where[0], where[1]
     for x in range(RING):
         for y in range(RING):
-            rows, (high, low) = in_order(pieces, x, y)
-            d_high[rows, :] = high
-            d_low[rows, :] = low
+            rows = slice((y * RING + x) * 32, (y * RING + x) * 32 + 32)
+            high, low = split(pieces[x, y])
+            for side in range(2):
+                lanes = slice(W + side * HALF, W + side * HALF + HALF)
+                fb_high[side, rows, :] = high[:, lanes]
+                fb_low[side, rows, :] = low[:, lanes]
+            d_high[rows, :] = high[:, :W]
+            d_low[rows, :] = low[:, :W]
     odd = lax.rem(row, 2) == 1
     live_row = live(lives, 0, row)
     factor = (d_high[...], d_low[...])
@@ -187,31 +178,19 @@
         return lax.all_to_all(every, "col", 0, 0, axis_index_groups=groups)
 
     by_y = shared(piece, [[x + RING * y for y in range(RING)] for x in range(RING)])
-    by_y = by_y.reshape(RING * 32, 2 * W)
     along_x = [[x + RING * y for x in range(RING)] for y in range(RING)]
-    diag_row = shared(by_y[:, :W], along_x).reshape(RING, RING, 32, W)
-    diag_row, border_y = lax.optimization_barrier((diag_row, by_y[:, W:]))
-    border_row = shared(border_y, along_x).reshape(RING, RING, 32, W)
-    fb_high, fb_low = pl.pallas_call(
-        borders_kernel,
-        out_shape=[shape((2, W, HALF), BF16)] * 2,
-        in_specs=[VMEM],
-        out_specs=[VMEM] * 2,
-        compiler_params=PARAMS,
-        cost_estimate=cost(0, 2),
-        name="borders",
-    )(border_row)
-
-    send_a, send_b = pl.pallas_call(
+    by_row = shared(by_y.reshape(RING * 32, 2 * W), along_x).reshape(RING, RING, 32, 2 * W)
+
+    send_a, send_b, fb_high, fb_low = pl.pallas_call(
         left_kernel,
-        out_shape=[shape((HALF, 2 * W), F32)] * 2,
+        out_shape=[shape((HALF, 2 * W), F32)] * 2 + [shape((2, W, HALF), BF16)] * 2,
         in_specs=[SMEM, SMEM] + [VMEM] * 3,
-        out_specs=[VMEM] * 2,
+        out_specs=[VMEM] * 4,
         scratch_shapes=[pltpu.VMEM((W, W), BF16)] * 2,
         compiler_params=PARAMS,
         cost_estimate=cost(2, 7),
         name="left",
-    )(where, window_live, diag_row, hessenberg[:, 0], hessenberg[:, 1])
+    )(where, window_live, by_row, hessenberg[:, 0], hessenberg[:, 1])
 
     every_col = range(GRID_COLS)
     got_b = swapped(send_b, [((r, c), (r + 1, c)) for r in range(1, 31, 2) for c in every_col])

time: 172 us -> 175 us (1.017)
  the two profiles are of different devices: /device:TPU:150 before, /device:TPU:8 now
where the time goes in v5:
time: 175 us; the launch traced here: 174 us
  waiting for transfers between devices  50.6 us (29%)
  starting transfers between devices  43.2 us (25%)
  blocking collectives  33.1 us (19%)
  Pallas kernels  19.5 us (11%)
  between operations  13.6 us (8%)
  local copies, waits for them, and re-layouts  12.7 us (7%)
    all_to_all x1, blocking collectives, shared(): return lax.all_to_all(every, 'col', 0, 0, axis_index_groups=groups)  33.1 us
    ppermute x9, starting transfers between devices, moved_on(): lax.ppermute(value, ('row', 'col'), [(r * GRID_COLS + c, t * GRID_COLS +...  32.3 us
    ppermute x9, waiting for transfers between devices, moved_on(): lax.ppermute(value, ('row', 'col'), [(r * GRID_COLS + c, t * GRID_COLS +...  22.9 us
    ppermute x2, waiting for transfers between devices, moved(): lax.ppermute(value, axis, [(i, j) for i, j in pairs if 0 <= j < count])  14.9 us
    all_to_all x1, waiting for transfers between devices, shared(): return lax.all_to_all(every, 'col', 0, 0, axis_index_groups=groups)  12.8 us
    pallas_call x2, Pallas kernels, middle(): pl.pallas_call(functools.partial(middle_kernel, first), out_shape=[shape(...  7.32 us
    all_to_all x1, starting transfers between devices, shared(): return lax.all_to_all(every, 'col', 0, 0, axis_index_groups=groups)  7.02 us
    pallas_call x2, Pallas kernels, last(): pl.pallas_call(functools.partial(last_kernel, first), out_shape=shape((W,...  6.79 us
  transfers between devices with their start and end apart: 13, of which 5 were waited for; matrix products, arithmetic and copies ran while one was open for 4% of the time, Pallas kernels for 9%

profile of v5, /device:TPU:8, one launch (start us, length us, event | category | flops | bytes accessed | tf_op | source)
XLA Modules:
  0.0 174.4 jit_solution(14336813371242710322)
XLA Ops:
  6.5 0.0 all-gather.2.cloned.1.call-start
  6.5 0.8 fusion.1
  7.3 1.9 %collective-permute-start = (f32[32,256]{1,0:T(8,128)S(1)}, f32[32,256]{1,0:T(8,128)S(1)}, u32[]{:S(2)}, u32[]{:S(2)}) collective-permute-start(f32[32,256]{1,0:T(8,128)S(1)} %get-tuple-element.36), channel_id=1, source_target_pairs={{0,16},{16,32},{32,48},{48,64},{64,80},{80,96},{96,112},{112,128},... | collective-permute-start | bytes 98312 | tf_op jit(solution)/shard_map/ppermute | solution.py:45
  9.2 9.9 %collective-permute-done = f32[32,256]{1,0:T(8,128)S(1)} collective-permute-done((f32[32,256]{1,0:T(8,128)S(1)}, f32[32,256]{1,0:T(8,128)S(1)}, u32[]{:S(2)}, u32[]{:S(2)}) %collective-permute-start) | collective-permute-done | bytes 32800 | tf_op jit(solution)/shard_map/ppermute | solution.py:45
  19.2 0.8 pad_maximum_fusion.1
  20.0 0.7 collective-permute-start.2
  20.7 0.0 collective-permute-done.2
  20.7 1.9 %collective-permute-start.3 = (f32[32,1024]{1,0:T(8,128)S(1)}, f32[32,1024]{1,0:T(8,128)S(1)}, u32[]{:S(2)}, u32[]{:S(2)}) collective-permute-start(f32[32,1024]{1,0:T(8,128)S(1)} %collective-permute-done.2), channel_id=1, source_target_pairs={{0,256},{16,272},{32,288},{48,304},{64,320},{80,336},{96,352},{112... | collective-permute-start | bytes 393224 | tf_op jit(solution)/shard_map/ppermute | solution.py:45
  22.6 4.9 %collective-permute-done.3 = f32[32,1024]{1,0:T(8,128)S(1)} collective-permute-done((f32[32,1024]{1,0:T(8,128)S(1)}, f32[32,1024]{1,0:T(8,128)S(1)}, u32[]{:S(2)}, u32[]{:S(2)}) %collective-permute-start.3) | collective-permute-done | bytes 131104 | tf_op jit(solution)/shard_map/ppermute | solution.py:45
  27.6 0.7 pad_maximum_fusion
  28.3 0.0 all-gather.2.cloned.1.call-update
  28.4 33.1 %all_to_all.10 = f32[4,32,1024]{2,1,0:T(8,128)S(1)} all-to-all(f32[4,32,1024]{2,1,0:T(8,128)S(1)} %broadcast_in_dim.6), channel_id=1, replica_groups={{0,4,8,12},{1,5,9,13},{2,6,10,14},{3,7,11,15},{16,20,24,28},{17,21,25,2..., dimensions={0} | all-to-all | bytes 1048576 | tf_op jit(solution)/shard_map/all_to_all | solution.py:178
  61.5 1.6 broadcast_in_dim.15
  63.1 7.0 %all-to-all-start.1 = ((f32[4,128,1024]{2,1,0:T(8,128)}), f32[4,128,1024]{2,1,0:T(8,128)S(1)}, u32[]{:S(2)}, u32[]{:S(2)}) async-start(f32[4,128,1024]{2,1,0:T(8,128)} %broadcast_in_dim.15), calls=%async_computation.1 | async-start | bytes 4194304 | tf_op jit(solution)/shard_map/all_to_all | solution.py:178
  70.1 0.1 pad_add_fusion.where
  70.2 4.1 %fusion = (f32[512,1,512]{2,1,0:T(1,128)S(1)}, f32[512,1,512]{2,1,0:T(1,128)S(1)}) fusion(f32[512,2,512]{2,1,0:T(2,128)} %param.4), kind=kLoop, calls=%fused_computation.5 | loop fusion | bytes 4194304 | tf_op jit(solution)/shard_map/slice | solution.py:193
  74.3 0.0 copy-start.3
  74.3 1.5 copy_bitcast_fusion
  75.9 12.8 %all-to-all-done.1 = f32[4,128,1024]{2,1,0:T(8,128)S(1)} async-done(((f32[4,128,1024]{2,1,0:T(8,128)}), f32[4,128,1024]{2,1,0:T(8,128)S(1)}, u32[]{:S(2)}, u32[]{:S(2)}) %all-to-all-start.1) | async-done | bytes 2097184 | tf_op jit(solution)/shard_map/all_to_all | solution.py:178
  88.7 0.0 copy-done.3
  88.7 0.0 copy-start.1
  88.7 1.2 copy-done.1
  89.9 0.0 copy-start.2
  89.9 1.2 copy-done.2
  91.1 4.0 %left.1 = (f32[256,1024]{1,0:T(8,128)}, f32[256,1024]{1,0:T(8,128)}, bf16[2,512,256]{2,1,0:T(8,128)(2,1)S(1)}, bf16[2,512,256]{2,1,0:T(8,128)(2,1)S(1)}) custom-call(s32[2]{0:T(128)S(1)} %pad_add_fusion.where, s32[2,32]{1,0:T(2,128)S(1)} %copy-done.3, f32[4,4,32,1024]{3,2,1,0:T(8,128)S(1)} %bitcast.12, f32[512,512]{1,0:T(8,128)S(1)} %copy-done.2, ...), custom_call_target="tpu_custom_call" | custom-call | flops 1610612736 | bytes 7340032 | tf_op jit(solution)/shard_map/left/pallas_call | solution.py:184
  95.1 1.9 %collective-permute-start.7 = (f32[256,1024]{1,0:T(8,128)}, f32[256,1024]{1,0:T(8,128)S(1)}, u32[]{:S(2)}, u32[]{:S(2)}) collective-permute-start(f32[256,1024]{1,0:T(8,128)} %get-tuple-element.28.own), channel_id=1, source_target_pairs={{0,16},{1,17},{2,18},{3,19},{4,20},{5,21},{6,22},{7,23},{8,24},{9,... | collective-permute-start | bytes 3145736 | tf_op jit(solution)/shard_map/ppermute | solution.py:49
  97.0 12.7 %collective-permute-start.1 = (f32[256,1024]{1,0:T(8,128)}, f32[256,1024]{1,0:T(8,128)S(1)}, u32[]{:S(2)}, u32[]{:S(2)}) collective-permute-start(f32[256,1024]{1,0:T(8,128)} %get-tuple-element.19.own), channel_id=1, source_target_pairs={{16,32},{17,33},{18,34},{19,35},{20,36},{21,37},{22,38},{23,39},{2... | collective-permute-start | bytes 3145736 | tf_op jit(solution)/shard_map/ppermute | solution.py:49
  109.7 0.0 all-gather.2.cloned.1.call-done
  109.7 0.0 copy-start
  109.7 2.2 %copy-done = f32[1024,1024]{1,0:T(8,128)S(1)} copy-done((f32[1024,1024]{1,0:T(8,128)S(1)}, f32[1024,1024]{1,0:T(8,128)}, u32[]{:S(2)}) %copy-start) | copy-done | bytes 4194328
  111.9 1.4 prepare.1
  113.3 0.0 collective-permute-done.7.got
  113.4 3.6 %middle.3 = (f32[4,256,256]{2,1,0:T(8,128)S(1)}, f32[2,256,256]{2,1,0:T(8,128)S(1)}, f32[256,256]{1,0:T(8,128)S(1)}, f32[256,256]{1,0:T(8,128)S(1)}) custom-call(s32[2]{0:T(128)S(1)} %pad_add_fusion.where, s32[2,32]{1,0:T(2,128)S(1)} %copy-done.3, f32[256,1024]{1,0:T(8,128)} %get-tuple-element.28.own, f32[256,1024]{1,0:T(8,128)S(1)} %collective-permute-done.7.got, ...), custom_call_target="tpu_custom_call" | custom-call | flops 1610612736 | bytes 4194304 | tf_op jit(solution)/shard_map/middle/pallas_call | solution.py:214
  117.0 0.7 collective-permute-start.9
  117.7 3.7 %collective-permute-start.8 = (f32[2,256,256]{2,1,0:T(8,128)S(1)}, f32[2,256,256]{2,1,0:T(8,128)S(1)}, u32[]{:S(2)}, u32[]{:S(2)}) collective-permute-start(f32[2,256,256]{2,1,0:T(8,128)S(1)} %get-tuple-element.30), channel_id=1, source_target_pairs={{0,1},{2,3},{4,5},{6,7},{8,9},{10,11},{12,13},{14,15},{16,17},{18,... | collective-permute-start | bytes 1572872 | tf_op jit(solution)/shard_map/ppermute | solution.py:49
  121.5 21.2 %collective-permute-done.1.got = f32[256,1024]{1,0:T(8,128)S(1)} collective-permute-done((f32[256,1024]{1,0:T(8,128)}, f32[256,1024]{1,0:T(8,128)S(1)}, u32[]{:S(2)}, u32[]{:S(2)}) %collective-permute-start.1) | collective-permute-done | bytes 1048608 | tf_op jit(solution)/shard_map/ppermute | solution.py:49
  142.6 3.7 %middle.2 = (f32[4,256,256]{2,1,0:T(8,128)S(1)}, f32[2,256,256]{2,1,0:T(8,128)S(1)}, f32[256,256]{1,0:T(8,128)S(1)}, f32[256,256]{1,0:T(8,128)S(1)}) custom-call(s32[2]{0:T(128)S(1)} %pad_add_fusion.where, s32[2,32]{1,0:T(2,128)S(1)} %copy-done.3, f32[256,1024]{1,0:T(8,128)} %get-tuple-element.19.own, f32[256,1024]{1,0:T(8,128)S(1)} %collective-permute-done.1.got, ...), custom_call_target="tpu_custom_call" | custom-call | flops 1610612736 | bytes 4194304 | tf_op jit(solution)/shard_map/middle/pallas_call | solution.py:214
  146.3 1.9 %collective-permute-start.4 = (f32[2,256,256]{2,1,0:T(8,128)S(1)}, f32[2,256,256]{2,1,0:T(8,128)S(1)}, u32[]{:S(2)}, u32[]{:S(2)}) collective-permute-start(f32[2,256,256]{2,1,0:T(8,128)S(1)} %get-tuple-element.25), channel_id=1, source_target_pairs={{0,1},{2,3},{4,5},{6,7},{8,9},{10,11},{12,13},{14,15},{16,17},{18,... | collective-permute-start | bytes 1572872 | tf_op jit(solution)/shard_map/ppermute | solution.py:49
  148.2 1.9 %collective-permute-start.10 = (f32[256,256]{1,0:T(8,128)S(1)}, f32[256,256]{1,0:T(8,128)S(1)}, u32[]{:S(2)}, u32[]{:S(2)}) collective-permute-start(f32[256,256]{1,0:T(8,128)S(1)} %get-tuple-element.32), channel_id=1, source_target_pairs={{1,2},{3,4},{5,6},{7,8},{9,10},{11,12},{13,14},{15,0},{17,18},{19,... | collective-permute-start | bytes 786440 | tf_op jit(solution)/shard_map/ppermute | solution.py:49
  150.1 0.7 collective-permute-start.5
  150.8 0.0 collective-permute-done.9.edge1
  150.8 8.1 %collective-permute-start.6 = (f32[256,256]{1,0:T(8,128)S(1)}, f32[256,256]{1,0:T(8,128)S(1)}, u32[]{:S(2)}, u32[]{:S(2)}) collective-permute-start(f32[256,256]{1,0:T(8,128)S(1)} %get-tuple-element.27), channel_id=1, source_target_pairs={{1,2},{3,4},{5,6},{7,8},{9,10},{11,12},{13,14},{15,0},{17,18},{19,... | collective-permute-start | bytes 786440 | tf_op jit(solution)/shard_map/ppermute | solution.py:49
  159.0 1.7 collective-permute-done.10.edge0
  160.7 0.0 collective-permute-done.8.side
  160.7 3.4 %last.2.rest_0_ = f32[512,2,512]{2,1,0:T(2,128)} custom-call(s32[2]{0:T(128)S(1)} %pad_add_fusion.where, s32[2,32]{1,0:T(2,128)S(1)} %copy-done.3, f32[4,256,256]{2,1,0:T(8,128)S(1)} %get-tuple-element.29.kept, f32[2,256,256]{2,1,0:T(8,128)S(1)} %collective-permute-done.8.side, f32[256,256]{1,0:T(8,128)S(1)} %collective-permute-done.9.edge1, ...), custom_call_target="tpu_custom_call" | custom-call | flops 805306368 | bytes 4194304 | tf_op jit(solution)/shard_map/last/pallas_call | solution.py:244
  164.1 0.0 collective-permute-done.5.edge1
  164.1 0.0 collective-permute-done.6.edge0
  164.1 0.0 collective-permute-done.4.side
  164.1 3.4 %last.3 = f32[512,2,512]{2,1,0:T(2,128)} custom-call(s32[2]{0:T(128)S(1)} %pad_add_fusion.where, s32[2,32]{1,0:T(2,128)S(1)} %copy-done.3, f32[4,256,256]{2,1,0:T(8,128)S(1)} %get-tuple-element.24.kept, f32[2,256,256]{2,1,0:T(8,128)S(1)} %collective-permute-done.4.side, f32[256,256]{1,0:T(8,128)S(1)} %collective-permute-done.5.edge1, ...), custom_call_target="tpu_custom_call", output_to_operand_aliasing={{}: (8, {})} | custom-call | flops 805306368 | bytes 4194304 | tf_op jit(solution)/shard_map/last/pallas_call | solution.py:244
  (1 shorter events, 0.0 us)
Async XLA Ops:
  6.5 103.2 %all-gather.2.cloned.1.call-start = ((), (), s32[]{:S(2)}) async-start(), calls=%async_computation.2 | async-start | bytes 4456448 | tf_op jit(solution)/shard_map/all_gather | solution.py:173
  7.3 11.9 %collective-permute-start = (f32[32,256]{1,0:T(8,128)S(1)}, f32[32,256]{1,0:T(8,128)S(1)}, u32[]{:S(2)}, u32[]{:S(2)}) collective-permute-start(f32[32,256]{1,0:T(8,128)S(1)} %get-tuple-element.36), channel_id=1, source_target_pairs={{0,16},{16,32},{32,48},{48,64},{64,80},{80,96},{96,112},{112,128},... | collective-permute-start | bytes 98312 | tf_op jit(solution)/shard_map/ppermute | solution.py:45
  20.0 0.7 collective-permute-start.2
  20.7 6.9 %collective-permute-start.3 = (f32[32,1024]{1,0:T(8,128)S(1)}, f32[32,1024]{1,0:T(8,128)S(1)}, u32[]{:S(2)}, u32[]{:S(2)}) collective-permute-start(f32[32,1024]{1,0:T(8,128)S(1)} %collective-permute-done.2), channel_id=1, source_target_pairs={{0,256},{16,272},{32,288},{48,304},{64,320},{80,336},{96,352},{112... | collective-permute-start | bytes 393224 | tf_op jit(solution)/shard_map/ppermute | solution.py:45
  63.1 25.6 %all-to-all-start.1 = ((f32[4,128,1024]{2,1,0:T(8,128)}), f32[4,128,1024]{2,1,0:T(8,128)S(1)}, u32[]{:S(2)}, u32[]{:S(2)}) async-start(f32[4,128,1024]{2,1,0:T(8,128)} %broadcast_in_dim.15), calls=%async_computation.1 | async-start | bytes 4194304 | tf_op jit(solution)/shard_map/all_to_all | solution.py:178
  74.3 14.4 %copy-start.3 = (s32[2,32]{1,0:T(2,128)S(1)}, s32[2,32]{1,0:T(2,128)}, u32[]{:S(2)}) copy-start(s32[2,32]{1,0:T(2,128)} %lives.9) | copy-start | bytes 772
  88.7 1.2 copy-start.1
  89.9 1.2 copy-start.2
  95.1 18.2 %collective-permute-start.7 = (f32[256,1024]{1,0:T(8,128)}, f32[256,1024]{1,0:T(8,128)S(1)}, u32[]{:S(2)}, u32[]{:S(2)}) collective-permute-start(f32[256,1024]{1,0:T(8,128)} %get-tuple-element.28.own), channel_id=1, source_target_pairs={{0,16},{1,17},{2,18},{3,19},{4,20},{5,21},{6,22},{7,23},{8,24},{9,... | collective-permute-start | bytes 3145736 | tf_op jit(solution)/shard_map/ppermute | solution.py:49
  97.0 45.6 %collective-permute-start.1 = (f32[256,1024]{1,0:T(8,128)}, f32[256,1024]{1,0:T(8,128)S(1)}, u32[]{:S(2)}, u32[]{:S(2)}) collective-permute-start(f32[256,1024]{1,0:T(8,128)} %get-tuple-element.19.own), channel_id=1, source_target_pairs={{16,32},{17,33},{18,34},{19,35},{20,36},{21,37},{22,38},{23,39},{2... | collective-permute-start | bytes 3145736 | tf_op jit(solution)/shard_map/ppermute | solution.py:49
  109.7 2.2 %copy-start = (f32[1024,1024]{1,0:T(8,128)S(1)}, f32[1024,1024]{1,0:T(8,128)}, u32[]{:S(2)}) copy-start(f32[1024,1024]{1,0:T(8,128)} %all-gather.2.cloned.1.call-done) | copy-start | bytes 12582916
  117.0 33.8 %collective-permute-start.9 = (f32[256,256]{1,0:T(8,128)S(1)}, f32[256,256]{1,0:T(8,128)S(1)}, u32[]{:S(2)}, u32[]{:S(2)}) collective-permute-start(f32[256,256]{1,0:T(8,128)S(1)} %get-tuple-element.31), channel_id=1, source_target_pairs={{1,2},{3,4},{5,6},{7,8},{9,10},{11,12},{13,14},{17,18},{19,20},{21... | collective-permute-start | bytes 786440 | tf_op jit(solution)/shard_map/ppermute | solution.py:49
  117.7 43.0 %collective-permute-start.8 = (f32[2,256,256]{2,1,0:T(8,128)S(1)}, f32[2,256,256]{2,1,0:T(8,128)S(1)}, u32[]{:S(2)}, u32[]{:S(2)}) collective-permute-start(f32[2,256,256]{2,1,0:T(8,128)S(1)} %get-tuple-element.30), channel_id=1, source_target_pairs={{0,1},{2,3},{4,5},{6,7},{8,9},{10,11},{12,13},{14,15},{16,17},{18,... | collective-permute-start | bytes 1572872 | tf_op jit(solution)/shard_map/ppermute | solution.py:49
  146.3 17.8 %collective-permute-start.4 = (f32[2,256,256]{2,1,0:T(8,128)S(1)}, f32[2,256,256]{2,1,0:T(8,128)S(1)}, u32[]{:S(2)}, u32[]{:S(2)}) collective-permute-start(f32[2,256,256]{2,1,0:T(8,128)S(1)} %get-tuple-element.25), channel_id=1, source_target_pairs={{0,1},{2,3},{4,5},{6,7},{8,9},{10,11},{12,13},{14,15},{16,17},{18,... | collective-permute-start | bytes 1572872 | tf_op jit(solution)/shard_map/ppermute | solution.py:49
  148.2 12.5 %collective-permute-start.10 = (f32[256,256]{1,0:T(8,128)S(1)}, f32[256,256]{1,0:T(8,128)S(1)}, u32[]{:S(2)}, u32[]{:S(2)}) collective-permute-start(f32[256,256]{1,0:T(8,128)S(1)} %get-tuple-element.32), channel_id=1, source_target_pairs={{1,2},{3,4},{5,6},{7,8},{9,10},{11,12},{13,14},{15,0},{17,18},{19,... | collective-permute-start | bytes 786440 | tf_op jit(solution)/shard_map/ppermute | solution.py:49
  150.1 14.0 %collective-permute-start.5 = (f32[256,256]{1,0:T(8,128)S(1)}, f32[256,256]{1,0:T(8,128)S(1)}, u32[]{:S(2)}, u32[]{:S(2)}) collective-permute-start(f32[256,256]{1,0:T(8,128)S(1)} %get-tuple-element.26), channel_id=1, source_target_pairs={{1,2},{3,4},{5,6},{7,8},{9,10},{11,12},{13,14},{17,18},{19,20},{21... | collective-permute-start | bytes 786440 | tf_op jit(solution)/shard_map/ppermute | solution.py:49
  150.8 13.3 %collective-permute-start.6 = (f32[256,256]{1,0:T(8,128)S(1)}, f32[256,256]{1,0:T(8,128)S(1)}, u32[]{:S(2)}, u32[]{:S(2)}) collective-permute-start(f32[256,256]{1,0:T(8,128)S(1)} %get-tuple-element.27), channel_id=1, source_target_pairs={{1,2},{3,4},{5,6},{7,8},{9,10},{11,12},{13,14},{15,0},{17,18},{19,... | collective-permute-start | bytes 786440 | tf_op jit(solution)/shard_map/ppermute | solution.py:49
Sparse Core Ops, SparseCore 0:
  28.4 60.4 all-gather.1

commit v6 on v4

--- a/solution.py
+++ b/solution.py
@@ -190,7 +190,7 @@
     by_y = by_y.reshape(RING * 32, 2 * W)
     along_x = [[x + RING * y for x in range(RING)] for y in range(RING)]
     diag_row = shared(by_y[:, :W], along_x).reshape(RING, RING, 32, W)
-    diag_row, border_y = lax.optimization_barrier((diag_row, by_y[:, W:]))
+    border_y, gathered = lax.optimization_barrier((by_y[:, W:], gathered))
     border_row = shared(border_y, along_x).reshape(RING, RING, 32, W)
     fb_high, fb_low = pl.pallas_call(
         borders_kernel,

time: 172 us -> 174 us (1.012)
  the two profiles are of different devices: /device:TPU:150 before, /device:TPU:96 now
where the time goes in v6:
time: 174 us
  waiting for transfers between devices  65.1 us (37%)
  starting transfers between devices  62.3 us (36%)
  Pallas kernels  20.1 us (12%)
  between operations  13.6 us (8%)
  local copies, waits for them, and re-layouts  10.8 us (6%)
    ppermute x9, starting transfers between devices, moved_on(): lax.ppermute(value, ('row', 'col'), [(r * GRID_COLS + c, t * GRID_COLS +...  40.9 us
    all_to_all x3, waiting for transfers between devices, shared(): return lax.all_to_all(every, 'col', 0, 0, axis_index_groups=groups)  28.6 us
    ppermute x9, waiting for transfers between devices, moved_on(): lax.ppermute(value, ('row', 'col'), [(r * GRID_COLS + c, t * GRID_COLS +...  25 us
    all_to_all x3, starting transfers between devices, shared(): return lax.all_to_all(every, 'col', 0, 0, axis_index_groups=groups)  15 us
    pallas_call x2, Pallas kernels, middle(): pl.pallas_call(functools.partial(middle_kernel, first), out_shape=[shape(...  7.97 us
    ppermute x2, waiting for transfers between devices, moved(): lax.ppermute(value, axis, [(i, j) for i, j in pairs if 0 <= j < count])  7.13 us
    pallas_call x2, Pallas kernels, last(): pl.pallas_call(functools.partial(last_kernel, first), out_shape=shape((W,...  6.8 us
    ppermute x2, starting transfers between devices, moved(): lax.ppermute(value, axis, [(i, j) for i, j in pairs if 0 <= j < count])  6.45 us
  transfers between devices with their start and end apart: 15, of which 9 were waited for; matrix products, arithmetic and copies ran while one was open for 3% of the time, Pallas kernels for 10%

profile of v6, /device:TPU:96, one launch (start us, length us, event | category | flops | bytes accessed | tf_op | source)
XLA Modules:
  0.0 173.6 jit_solution(5672939119009657649)
XLA Ops:
  6.5 0.0 all-gather.2.cloned.1.call-start
  6.5 0.8 fusion.2
  7.3 1.9 %collective-permute-start = (f32[32,256]{1,0:T(8,128)S(1)}, f32[32,256]{1,0:T(8,128)S(1)}, u32[]{:S(2)}, u32[]{:S(2)}) collective-permute-start(f32[32,256]{1,0:T(8,128)S(1)} %get-tuple-element.42), channel_id=1, source_target_pairs={{0,16},{16,32},{32,48},{48,64},{64,80},{80,96},{96,112},{112,128},... | collective-permute-start | bytes 98312 | tf_op jit(solution)/shard_map/ppermute | solution.py:45
  9.2 3.3 %collective-permute-done = f32[32,256]{1,0:T(8,128)S(1)} collective-permute-done((f32[32,256]{1,0:T(8,128)S(1)}, f32[32,256]{1,0:T(8,128)S(1)}, u32[]{:S(2)}, u32[]{:S(2)}) %collective-permute-start) | collective-permute-done | bytes 32800 | tf_op jit(solution)/shard_map/ppermute | solution.py:45
  12.5 0.8 pad_maximum_fusion.1
  13.4 12.0 %collective-permute-start.2 = (f32[32,1024]{1,0:T(8,128)S(1)}, f32[32,1024]{1,0:T(8,128)S(1)}, u32[]{:S(2)}, u32[]{:S(2)}) collective-permute-start(f32[32,1024]{1,0:T(8,128)S(1)} %pad_maximum_fusion.1), channel_id=1, source_target_pairs={{0,0},{1,16},{2,32},{3,48},{4,64},{5,80},{6,96},{7,112},{8,128},{9... | collective-permute-start | bytes 393224 | tf_op jit(solution)/shard_map/ppermute | solution.py:49
  25.4 6.7 %collective-permute-done.2 = f32[32,1024]{1,0:T(8,128)S(1)} collective-permute-done((f32[32,1024]{1,0:T(8,128)S(1)}, f32[32,1024]{1,0:T(8,128)S(1)}, u32[]{:S(2)}, u32[]{:S(2)}) %collective-permute-start.2) | collective-permute-done | bytes 131104 | tf_op jit(solution)/shard_map/ppermute | solution.py:49
  32.1 4.5 %collective-permute-start.3 = (f32[32,1024]{1,0:T(8,128)S(1)}, f32[32,1024]{1,0:T(8,128)S(1)}, u32[]{:S(2)}, u32[]{:S(2)}) collective-permute-start(f32[32,1024]{1,0:T(8,128)S(1)} %collective-permute-done.2), channel_id=1, source_target_pairs={{0,256},{16,272},{32,288},{48,304},{64,320},{80,336},{96,352},{112... | collective-permute-start | bytes 393224 | tf_op jit(solution)/shard_map/ppermute | solution.py:45
  36.7 3.8 %collective-permute-done.3 = f32[32,1024]{1,0:T(8,128)S(1)} collective-permute-done((f32[32,1024]{1,0:T(8,128)S(1)}, f32[32,1024]{1,0:T(8,128)S(1)}, u32[]{:S(2)}, u32[]{:S(2)}) %collective-permute-start.3) | collective-permute-done | bytes 131104 | tf_op jit(solution)/shard_map/ppermute | solution.py:45
  40.5 0.7 pad_maximum_fusion
  41.3 0.0 all-gather.2.cloned.1.call-update
  41.3 0.8 broadcast_in_dim.6
  42.1 7.2 %all-to-all-start = ((f32[4,32,1024]{2,1,0:T(8,128)}), f32[4,32,1024]{2,1,0:T(8,128)S(1)}, u32[]{:S(2)}, u32[]{:S(2)}) async-start(f32[4,32,1024]{2,1,0:T(8,128)} %broadcast_in_dim.6), calls=%async_computation | async-start | bytes 1048576 | tf_op jit(solution)/shard_map/all_to_all | solution.py:187
  49.3 9.3 %all-to-all-done = f32[4,32,1024]{2,1,0:T(8,128)S(1)} async-done(((f32[4,32,1024]{2,1,0:T(8,128)}), f32[4,32,1024]{2,1,0:T(8,128)S(1)}, u32[]{:S(2)}, u32[]{:S(2)}) %all-to-all-start) | async-done | bytes 524320 | tf_op jit(solution)/shard_map/all_to_all | solution.py:187
  58.6 0.0 copy-start.4
  58.7 1.1 broadcast_in_dim.7
  59.8 3.5 %all-to-all-start.1 = ((f32[4,128,512]{2,1,0:T(8,128)}), f32[4,128,512]{2,1,0:T(8,128)S(1)}, u32[]{:S(2)}, u32[]{:S(2)}) async-start(f32[4,128,512]{2,1,0:T(8,128)} %broadcast_in_dim.7), calls=%async_computation.1 | async-start | bytes 2097152 | tf_op jit(solution)/shard_map/all_to_all | solution.py:187
  63.3 0.1 pad_add_fusion.where
  63.4 0.0 copy-done.4
  63.4 1.6 fusion
  65.0 0.0 copy-start.3
  65.0 0.2 copy_bitcast_fusion
  65.2 9.4 %all-to-all-done.1 = f32[4,128,512]{2,1,0:T(8,128)S(1)} async-done(((f32[4,128,512]{2,1,0:T(8,128)}), f32[4,128,512]{2,1,0:T(8,128)S(1)}, u32[]{:S(2)}, u32[]{:S(2)}) %all-to-all-start.1) | async-done | bytes 1048608 | tf_op jit(solution)/shard_map/all_to_all | solution.py:187
  74.6 0.0 copy-done.3
  74.6 3.8 %left.1 = (f32[256,1024]{1,0:T(8,128)}, f32[256,1024]{1,0:T(8,128)}) custom-call(s32[2]{0:T(128)S(1)} %pad_add_fusion.where, s32[2,32]{1,0:T(2,128)S(1)} %copy-done.3, f32[4,4,32,512]{3,2,1,0:T(8,128)S(1)} %bitcast.14, f32[512,512]{1,0:T(8,128)S(1)} %get-tuple-element.44.h0, f32[512,512]{1,0:T(8,128)S(1)} %get-tuple-element.43.h1), custom_call_target="tpu_custom_call" | custom-call | flops 1610612736 | bytes 7340032 | tf_op jit(solution)/shard_map/left/pallas_call | solution.py:205
  78.4 1.9 %collective-permute-start.7 = (f32[256,1024]{1,0:T(8,128)}, f32[256,1024]{1,0:T(8,128)}, u32[]{:S(2)}, u32[]{:S(2)}) collective-permute-start(f32[256,1024]{1,0:T(8,128)} %get-tuple-element.32.own), channel_id=1, source_target_pairs={{0,16},{1,17},{2,18},{3,19},{4,20},{5,21},{6,22},{7,23},{8,24},{9,... | collective-permute-start | bytes 3145736 | tf_op jit(solution)/shard_map/ppermute | solution.py:49
  80.3 2.4 %collective-permute-start.1 = (f32[256,1024]{1,0:T(8,128)}, f32[256,1024]{1,0:T(8,128)}, u32[]{:S(2)}, u32[]{:S(2)}) collective-permute-start(f32[256,1024]{1,0:T(8,128)} %get-tuple-element.21.own), channel_id=1, source_target_pairs={{16,32},{17,33},{18,34},{19,35},{20,36},{21,37},{22,38},{23,39},{2... | collective-permute-start | bytes 3145736 | tf_op jit(solution)/shard_map/ppermute | solution.py:49
  82.7 4.4 %all-gather.2.cloned.1.call-done = f32[1024,1024]{1,0:T(8,128)} async-done(((f32[64,1024]{1,0:T(8,128)}), f32[1024,1024]{1,0:T(8,128)}) %all-gather.2.cloned.1.call-update) | async-done | bytes 4194320 | tf_op jit(solution)/shard_map/all_gather | solution.py:182
  87.1 1.2 broadcast_in_dim.8
  88.3 4.3 %all-to-all-start.2 = ((f32[4,128,512]{2,1,0:T(8,128)}), f32[4,128,512]{2,1,0:T(8,128)S(1)}, u32[]{:S(2)}, u32[]{:S(2)}) async-start(f32[4,128,512]{2,1,0:T(8,128)} %broadcast_in_dim.8), calls=%async_computation.2 | async-start | bytes 2097152 | tf_op jit(solution)/shard_map/all_to_all | solution.py:187
  92.6 0.0 copy-start.2
  92.6 2.2 %copy-done.2 = f32[1024,1024]{1,0:T(8,128)S(1)} copy-done((f32[1024,1024]{1,0:T(8,128)S(1)}, f32[1024,1024]{1,0:T(8,128)}, u32[]{:S(2)}) %copy-start.2) | copy-done | bytes 4194328
  94.8 1.4 prepare.1
  96.2 0.0 copy-start
  96.2 1.3 copy-done
  97.5 9.9 %all-to-all-done.2 = f32[4,128,512]{2,1,0:T(8,128)S(1)} async-done(((f32[4,128,512]{2,1,0:T(8,128)}), f32[4,128,512]{2,1,0:T(8,128)S(1)}, u32[]{:S(2)}, u32[]{:S(2)}) %all-to-all-start.2) | async-done | bytes 1048608 | tf_op jit(solution)/shard_map/all_to_all | solution.py:187
  107.4 0.1 borders.1
  107.5 0.0 collective-permute-done.7.got
  107.5 0.0 copy-start.1
  107.6 1.6 copy-done.1
  109.1 4.0 %middle.3 = (f32[4,256,256]{2,1,0:T(8,128)S(1)}, f32[2,256,256]{2,1,0:T(8,128)S(1)}, f32[256,256]{1,0:T(8,128)S(1)}, f32[256,256]{1,0:T(8,128)S(1)}) custom-call(s32[2]{0:T(128)S(1)} %pad_add_fusion.where, s32[2,32]{1,0:T(2,128)S(1)} %copy-done.3, f32[256,1024]{1,0:T(8,128)} %get-tuple-element.32.own, f32[256,1024]{1,0:T(8,128)} %collective-permute-done.7.got, ...), custom_call_target="tpu_custom_call" | custom-call | flops 1610612736 | bytes 4194304 | tf_op jit(solution)/shard_map/middle/pallas_call | solution.py:235
  113.1 2.5 %collective-permute-start.8 = (f32[2,256,256]{2,1,0:T(8,128)S(1)}, f32[2,256,256]{2,1,0:T(8,128)S(1)}, u32[]{:S(2)}, u32[]{:S(2)}) collective-permute-start(f32[2,256,256]{2,1,0:T(8,128)S(1)} %get-tuple-element.34), channel_id=1, source_target_pairs={{0,1},{2,3},{4,5},{6,7},{8,9},{10,11},{12,13},{14,15},{16,17},{18,... | collective-permute-start | bytes 1572872 | tf_op jit(solution)/shard_map/ppermute | solution.py:49
  115.6 1.9 %collective-permute-start.10 = (f32[256,256]{1,0:T(8,128)S(1)}, f32[256,256]{1,0:T(8,128)S(1)}, u32[]{:S(2)}, u32[]{:S(2)}) collective-permute-start(f32[256,256]{1,0:T(8,128)S(1)} %get-tuple-element.36), channel_id=1, source_target_pairs={{1,2},{3,4},{5,6},{7,8},{9,10},{11,12},{13,14},{15,0},{17,18},{19,... | collective-permute-start | bytes 786440 | tf_op jit(solution)/shard_map/ppermute | solution.py:49
  117.5 0.0 collective-permute-done.1.got
  117.5 4.0 %middle.2 = (f32[4,256,256]{2,1,0:T(8,128)S(1)}, f32[2,256,256]{2,1,0:T(8,128)S(1)}, f32[256,256]{1,0:T(8,128)S(1)}, f32[256,256]{1,0:T(8,128)S(1)}) custom-call(s32[2]{0:T(128)S(1)} %pad_add_fusion.where, s32[2,32]{1,0:T(2,128)S(1)} %copy-done.3, f32[256,1024]{1,0:T(8,128)} %get-tuple-element.21.own, f32[256,1024]{1,0:T(8,128)} %collective-permute-done.1.got, ...), custom_call_target="tpu_custom_call" | custom-call | flops 1610612736 | bytes 4194304 | tf_op jit(solution)/shard_map/middle/pallas_call | solution.py:235
  121.5 3.9 %collective-permute-start.4 = (f32[2,256,256]{2,1,0:T(8,128)S(1)}, f32[2,256,256]{2,1,0:T(8,128)S(1)}, u32[]{:S(2)}, u32[]{:S(2)}) collective-permute-start(f32[2,256,256]{2,1,0:T(8,128)S(1)} %get-tuple-element.29), channel_id=1, source_target_pairs={{0,1},{2,3},{4,5},{6,7},{8,9},{10,11},{12,13},{14,15},{16,17},{18,... | collective-permute-start | bytes 1572872 | tf_op jit(solution)/shard_map/ppermute | solution.py:49
  125.5 6.1 %collective-permute-start.9 = (f32[256,256]{1,0:T(8,128)S(1)}, f32[256,256]{1,0:T(8,128)S(1)}, u32[]{:S(2)}, u32[]{:S(2)}) collective-permute-start(f32[256,256]{1,0:T(8,128)S(1)} %get-tuple-element.35), channel_id=1, source_target_pairs={{1,2},{3,4},{5,6},{7,8},{9,10},{11,12},{13,14},{17,18},{19,20},{21... | collective-permute-start | bytes 786440 | tf_op jit(solution)/shard_map/ppermute | solution.py:49
  131.6 3.9 %collective-permute-start.5 = (f32[256,256]{1,0:T(8,128)S(1)}, f32[256,256]{1,0:T(8,128)S(1)}, u32[]{:S(2)}, u32[]{:S(2)}) collective-permute-start(f32[256,256]{1,0:T(8,128)S(1)} %get-tuple-element.30), channel_id=1, source_target_pairs={{1,2},{3,4},{5,6},{7,8},{9,10},{11,12},{13,14},{17,18},{19,20},{21... | collective-permute-start | bytes 786440 | tf_op jit(solution)/shard_map/ppermute | solution.py:49
  135.5 0.0 collective-permute-done.10.edge0
  135.6 6.1 %collective-permute-start.6 = (f32[256,256]{1,0:T(8,128)S(1)}, f32[256,256]{1,0:T(8,128)S(1)}, u32[]{:S(2)}, u32[]{:S(2)}) collective-permute-start(f32[256,256]{1,0:T(8,128)S(1)} %get-tuple-element.31), channel_id=1, source_target_pairs={{1,2},{3,4},{5,6},{7,8},{9,10},{11,12},{13,14},{15,0},{17,18},{19,... | collective-permute-start | bytes 786440 | tf_op jit(solution)/shard_map/ppermute | solution.py:49
  141.7 0.0 collective-permute-done.9.edge1
  141.7 0.0 collective-permute-done.8.side
  141.7 3.4 %last.2.rest_0_ = f32[512,2,512]{2,1,0:T(2,128)} custom-call(s32[2]{0:T(128)S(1)} %pad_add_fusion.where, s32[2,32]{1,0:T(2,128)S(1)} %copy-done.3, f32[4,256,256]{2,1,0:T(8,128)S(1)} %get-tuple-element.33.kept, f32[2,256,256]{2,1,0:T(8,128)S(1)} %collective-permute-done.8.side, f32[256,256]{1,0:T(8,128)S(1)} %collective-permute-done.9.edge1, ...), custom_call_target="tpu_custom_call" | custom-call | flops 805306368 | bytes 4194304 | tf_op jit(solution)/shard_map/last/pallas_call | solution.py:265
  145.1 6.2 %collective-permute-done.5.edge1 = f32[256,256]{1,0:T(8,128)S(1)} collective-permute-done((f32[256,256]{1,0:T(8,128)S(1)}, f32[256,256]{1,0:T(8,128)S(1)}, u32[]{:S(2)}, u32[]{:S(2)}) %collective-permute-start.5) | collective-permute-done | bytes 262176 | tf_op jit(solution)/shard_map/ppermute | solution.py:49
  151.4 12.0 %collective-permute-done.6.edge0 = f32[256,256]{1,0:T(8,128)S(1)} collective-permute-done((f32[256,256]{1,0:T(8,128)S(1)}, f32[256,256]{1,0:T(8,128)S(1)}, u32[]{:S(2)}, u32[]{:S(2)}) %collective-permute-start.6) | collective-permute-done | bytes 262176 | tf_op jit(solution)/shard_map/ppermute | solution.py:49
  163.4 0.0 collective-permute-done.4.side
  163.4 3.4 %last.3 = f32[512,2,512]{2,1,0:T(2,128)} custom-call(s32[2]{0:T(128)S(1)} %pad_add_fusion.where, s32[2,32]{1,0:T(2,128)S(1)} %copy-done.3, f32[4,256,256]{2,1,0:T(8,128)S(1)} %get-tuple-element.28.kept, f32[2,256,256]{2,1,0:T(8,128)S(1)} %collective-permute-done.4.side, f32[256,256]{1,0:T(8,128)S(1)} %collective-permute-done.5.edge1, ...), custom_call_target="tpu_custom_call", output_to_operand_aliasing={{}: (8, {})} | custom-call | flops 805306368 | bytes 4194304 | tf_op jit(solution)/shard_map/last/pallas_call | solution.py:265
  (1 shorter events, 0.0 us)
Async XLA Ops:
  6.5 80.6 %all-gather.2.cloned.1.call-start = ((), (), s32[]{:S(2)}) async-start(), calls=%async_computation.3 | async-start | bytes 4456448 | tf_op jit(solution)/shard_map/all_gather | solution.py:182
  7.3 5.2 %collective-permute-start = (f32[32,256]{1,0:T(8,128)S(1)}, f32[32,256]{1,0:T(8,128)S(1)}, u32[]{:S(2)}, u32[]{:S(2)}) collective-permute-start(f32[32,256]{1,0:T(8,128)S(1)} %get-tuple-element.42), channel_id=1, source_target_pairs={{0,16},{16,32},{32,48},{48,64},{64,80},{80,96},{96,112},{112,128},... | collective-permute-start | bytes 98312 | tf_op jit(solution)/shard_map/ppermute | solution.py:45
  13.4 18.8 %collective-permute-start.2 = (f32[32,1024]{1,0:T(8,128)S(1)}, f32[32,1024]{1,0:T(8,128)S(1)}, u32[]{:S(2)}, u32[]{:S(2)}) collective-permute-start(f32[32,1024]{1,0:T(8,128)S(1)} %pad_maximum_fusion.1), channel_id=1, source_target_pairs={{0,0},{1,16},{2,32},{3,48},{4,64},{5,80},{6,96},{7,112},{8,128},{9... | collective-permute-start | bytes 393224 | tf_op jit(solution)/shard_map/ppermute | solution.py:49
  32.1 8.4 %collective-permute-start.3 = (f32[32,1024]{1,0:T(8,128)S(1)}, f32[32,1024]{1,0:T(8,128)S(1)}, u32[]{:S(2)}, u32[]{:S(2)}) collective-permute-start(f32[32,1024]{1,0:T(8,128)S(1)} %collective-permute-done.2), channel_id=1, source_target_pairs={{0,256},{16,272},{32,288},{48,304},{64,320},{80,336},{96,352},{112... | collective-permute-start | bytes 393224 | tf_op jit(solution)/shard_map/ppermute | solution.py:45
  42.1 16.5 %all-to-all-start = ((f32[4,32,1024]{2,1,0:T(8,128)}), f32[4,32,1024]{2,1,0:T(8,128)S(1)}, u32[]{:S(2)}, u32[]{:S(2)}) async-start(f32[4,32,1024]{2,1,0:T(8,128)} %broadcast_in_dim.6), calls=%async_computation | async-start | bytes 1048576 | tf_op jit(solution)/shard_map/all_to_all | solution.py:187
  58.6 4.7 %copy-start.4 = (f32[512,2,512]{2,1,0:T(2,128)S(1)}, f32[512,2,512]{2,1,0:T(2,128)}, u32[]{:S(2)}) copy-start(f32[512,2,512]{2,1,0:T(2,128)} %param.4) | copy-start | bytes 6291460
  59.8 14.8 %all-to-all-start.1 = ((f32[4,128,512]{2,1,0:T(8,128)}), f32[4,128,512]{2,1,0:T(8,128)S(1)}, u32[]{:S(2)}, u32[]{:S(2)}) async-start(f32[4,128,512]{2,1,0:T(8,128)} %broadcast_in_dim.7), calls=%async_computation.1 | async-start | bytes 2097152 | tf_op jit(solution)/shard_map/all_to_all | solution.py:187
  65.0 9.6 %copy-start.3 = (s32[2,32]{1,0:T(2,128)S(1)}, s32[2,32]{1,0:T(2,128)}, u32[]{:S(2)}) copy-start(s32[2,32]{1,0:T(2,128)} %lives.9) | copy-start | bytes 772
  78.4 29.1 %collective-permute-start.7 = (f32[256,1024]{1,0:T(8,128)}, f32[256,1024]{1,0:T(8,128)}, u32[]{:S(2)}, u32[]{:S(2)}) collective-permute-start(f32[256,1024]{1,0:T(8,128)} %get-tuple-element.32.own), channel_id=1, source_target_pairs={{0,16},{1,17},{2,18},{3,19},{4,20},{5,21},{6,22},{7,23},{8,24},{9,... | collective-permute-start | bytes 3145736 | tf_op jit(solution)/shard_map/ppermute | solution.py:49
  80.3 37.2 %collective-permute-start.1 = (f32[256,1024]{1,0:T(8,128)}, f32[256,1024]{1,0:T(8,128)}, u32[]{:S(2)}, u32[]{:S(2)}) collective-permute-start(f32[256,1024]{1,0:T(8,128)} %get-tuple-element.21.own), channel_id=1, source_target_pairs={{16,32},{17,33},{18,34},{19,35},{20,36},{21,37},{22,38},{23,39},{2... | collective-permute-start | bytes 3145736 | tf_op jit(solution)/shard_map/ppermute | solution.py:49
  88.3 19.1 %all-to-all-start.2 = ((f32[4,128,512]{2,1,0:T(8,128)}), f32[4,128,512]{2,1,0:T(8,128)S(1)}, u32[]{:S(2)}, u32[]{:S(2)}) async-start(f32[4,128,512]{2,1,0:T(8,128)} %broadcast_in_dim.8), calls=%async_computation.2 | async-start | bytes 2097152 | tf_op jit(solution)/shard_map/all_to_all | solution.py:187
  92.6 2.2 %copy-start.2 = (f32[1024,1024]{1,0:T(8,128)S(1)}, f32[1024,1024]{1,0:T(8,128)}, u32[]{:S(2)}) copy-start(f32[1024,1024]{1,0:T(8,128)} %all-gather.2.cloned.1.call-done) | copy-start | bytes 12582916
  96.2 1.3 copy-start
  107.5 1.6 copy-start.1
  113.1 28.6 %collective-permute-start.8 = (f32[2,256,256]{2,1,0:T(8,128)S(1)}, f32[2,256,256]{2,1,0:T(8,128)S(1)}, u32[]{:S(2)}, u32[]{:S(2)}) collective-permute-start(f32[2,256,256]{2,1,0:T(8,128)S(1)} %get-tuple-element.34), channel_id=1, source_target_pairs={{0,1},{2,3},{4,5},{6,7},{8,9},{10,11},{12,13},{14,15},{16,17},{18,... | collective-permute-start | bytes 1572872 | tf_op jit(solution)/shard_map/ppermute | solution.py:49
  115.6 19.9 %collective-permute-start.10 = (f32[256,256]{1,0:T(8,128)S(1)}, f32[256,256]{1,0:T(8,128)S(1)}, u32[]{:S(2)}, u32[]{:S(2)}) collective-permute-start(f32[256,256]{1,0:T(8,128)S(1)} %get-tuple-element.36), channel_id=1, source_target_pairs={{1,2},{3,4},{5,6},{7,8},{9,10},{11,12},{13,14},{15,0},{17,18},{19,... | collective-permute-start | bytes 786440 | tf_op jit(solution)/shard_map/ppermute | solution.py:49
  121.5 41.8 %collective-permute-start.4 = (f32[2,256,256]{2,1,0:T(8,128)S(1)}, f32[2,256,256]{2,1,0:T(8,128)S(1)}, u32[]{:S(2)}, u32[]{:S(2)}) collective-permute-start(f32[2,256,256]{2,1,0:T(8,128)S(1)} %get-tuple-element.29), channel_id=1, source_target_pairs={{0,1},{2,3},{4,5},{6,7},{8,9},{10,11},{12,13},{14,15},{16,17},{18,... | collective-permute-start | bytes 1572872 | tf_op jit(solution)/shard_map/ppermute | solution.py:49
  125.5 16.2 %collective-permute-start.9 = (f32[256,256]{1,0:T(8,128)S(1)}, f32[256,256]{1,0:T(8,128)S(1)}, u32[]{:S(2)}, u32[]{:S(2)}) collective-permute-start(f32[256,256]{1,0:T(8,128)S(1)} %get-tuple-element.35), channel_id=1, source_target_pairs={{1,2},{3,4},{5,6},{7,8},{9,10},{11,12},{13,14},{17,18},{19,20},{21... | collective-permute-start | bytes 786440 | tf_op jit(solution)/shard_map/ppermute | solution.py:49
  131.6 19.7 %collective-permute-start.5 = (f32[256,256]{1,0:T(8,128)S(1)}, f32[256,256]{1,0:T(8,128)S(1)}, u32[]{:S(2)}, u32[]{:S(2)}) collective-permute-start(f32[256,256]{1,0:T(8,128)S(1)} %get-tuple-element.30), channel_id=1, source_target_pairs={{1,2},{3,4},{5,6},{7,8},{9,10},{11,12},{13,14},{17,18},{19,20},{21... | collective-permute-start | bytes 786440 | tf_op jit(solution)/shard_map/ppermute | solution.py:49
  135.6 27.8 %collective-permute-start.6 = (f32[256,256]{1,0:T(8,128)S(1)}, f32[256,256]{1,0:T(8,128)S(1)}, u32[]{:S(2)}, u32[]{:S(2)}) collective-permute-start(f32[256,256]{1,0:T(8,128)S(1)} %get-tuple-element.31), channel_id=1, source_target_pairs={{1,2},{3,4},{5,6},{7,8},{9,10},{11,12},{13,14},{15,0},{17,18},{19,... | collective-permute-start | bytes 786440 | tf_op jit(solution)/shard_map/ppermute | solution.py:49
Sparse Core Ops, SparseCore 0:
  41.4 45.6 all-gather.1

commit v7 on v5

--- a/solution.py
+++ b/solution.py
@@ -59,7 +59,7 @@
     return moved_on(value, pairs + [(b, a) for a, b in pairs])
 
 
-def left_kernel(where, lives, pieces, h0, h1, send_a, send_b, fb_high, fb_low, d_high, d_low):
+def left_kernel(where, lives, pieces, h0, h1, send_a, send_b0, send_b1, fb_high, fb_low, d_high, d_low):
     row, col = where[0], where[1]
     for x in range(RING):
         for y in range(RING):
@@ -80,7 +80,7 @@
         turned = product(factor, split(value), ((0,), (0,)))
         value = jnp.where((col + GRID_COLS * s >= row) & live_row, turned, value)
         send_a[:, lanes] = jnp.where(odd, value[:HALF], value[HALF:])
-        send_b[:, lanes] = jnp.where(odd, value[HALF:], value[:HALF])
+        (send_b0, send_b1)[s][...] = jnp.where(odd, value[HALF:], value[:HALF])
 
 
 def prepare_kernel(where, gathered, high, low):
@@ -89,7 +89,7 @@
         high[0, rows, :], low[0, rows, :] = split(gathered[lax.rem(where[1] + index, 16), 0])
 
 
-def middle_kernel(first, where, lives, own, got, fb_high, fb_low, c_high, c_low, kept, side, edge0, edge1):
+def middle_kernel(first, where, lives, own0, own1, got0, got1, fb_high, fb_low, c_high, c_low, kept, side, edge0, edge1):
     row, col = where[0], where[1]
     odd = lax.rem(row, 2) == 1
     top = odd if first else ~odd
@@ -101,11 +101,12 @@
     is_corner = (lax.broadcasted_iota(jnp.int32, (HALF, 128), 0) == 0) & (
         lax.broadcasted_iota(jnp.int32, (HALF, 128), 1) == 127
     )
+    part = lambda ref, lanes: ref[:, lanes] if first else ref[...]
     ends = []
     for s in range(2):
         lanes = slice(s * W, s * W + W)
         tile = col + GRID_COLS * s
-        own_raw, got_raw = own[:, lanes], got[:, lanes]
+        own_raw, got_raw = (part((own0, own1)[s], lanes), part((got0, got1)[s], lanes))
         own_value = jnp.where(top & (tile < row), 0.0, own_raw)
         got_value = jnp.where(top | (tile > row), got_raw, 0.0)
         acted = active & (tile >= jnp.where(top, row - 1, row))
@@ -181,11 +182,11 @@
     along_x = [[x + RING * y for x in range(RING)] for y in range(RING)]
     by_row = shared(by_y.reshape(RING * 32, 2 * W), along_x).reshape(RING, RING, 32, 2 * W)
 
-    send_a, send_b, fb_high, fb_low = pl.pallas_call(
+    send_a, send_b0, send_b1, fb_high, fb_low = pl.pallas_call(
         left_kernel,
-        out_shape=[shape((HALF, 2 * W), F32)] * 2 + [shape((2, W, HALF), BF16)] * 2,
+        out_shape=[shape((HALF, 2 * W), F32)] + [shape((HALF, W), F32)] * 2 + [shape((2, W, HALF), BF16)] * 2,
         in_specs=[SMEM, SMEM] + [VMEM] * 3,
-        out_specs=[VMEM] * 4,
+        out_specs=[VMEM] * 5,
         scratch_shapes=[pltpu.VMEM((W, W), BF16)] * 2,
         compiler_params=PARAMS,
         cost_estimate=cost(2, 7),
@@ -193,7 +194,9 @@
     )(where, window_live, by_row, hessenberg[:, 0], hessenberg[:, 1])
 
     every_col = range(GRID_COLS)
-    got_b = swapped(send_b, [((r, c), (r + 1, c)) for r in range(1, 31, 2) for c in every_col])
+    pairs = [((r, c), (r + 1, c)) for r in range(1, 31, 2) for c in every_col]
+    got_b1 = swapped(send_b1, [(a, b) for a, b in pairs if a[1] + GRID_COLS >= a[0]])
+    got_b0 = swapped(send_b0, [(a, b) for a, b in pairs if a[1] >= a[0]])
     got_a = swapped(send_a, [((r, c), (r + 1, c)) for r in range(0, 32, 2) for c in every_col])
 
     c_high, c_low = pl.pallas_call(
@@ -210,16 +213,16 @@
         name="prepare",
     )(where, gathered)
 
-    def middle(first, own, got):
+    def middle(first, *parts):
         return pl.pallas_call(
             functools.partial(middle_kernel, first),
             out_shape=[shape((4, HALF, HALF), F32), shape((2, HALF, HALF), F32)] + [shape((HALF, HALF), F32)] * 2,
-            in_specs=[SMEM, SMEM] + [VMEM] * 6,
+            in_specs=[SMEM, SMEM] + [VMEM] * 8,
             out_specs=[VMEM] * 4,
             compiler_params=PARAMS,
             cost_estimate=cost(2, 4),
             name="middle",
-        )(where, window_live, own, got, fb_high, fb_low, c_high, c_low)
+        )(where, window_live, *parts, fb_high, fb_low, c_high, c_low)
 
     def exchanged(side, edge0, edge1):
         rows = range(GRID_ROWS)
@@ -256,9 +259,9 @@
             name="last",
         )(where, window_live, kept, *moved_parts, c_high, c_low, *done)
 
-    kept_a, *ends_a = middle(True, send_a, got_a)
+    kept_a, *ends_a = middle(True, send_a, send_a, got_a, got_a)
     parts_a = exchanged(*ends_a)
-    kept_b, *ends_b = middle(False, send_b, got_b)
+    kept_b, *ends_b = middle(False, send_b0, send_b1, got_b0, got_b1)
     parts_b = exchanged(*ends_b)
     out = last(True, kept_a, parts_a)
     return last(False, kept_b, parts_b, out)

time: 175 us -> 170 us (0.971)
  the two profiles are of different devices: /device:TPU:8 before, /device:TPU:150 now
where the time goes in v7:
time: 170 us
  starting transfers between devices  53 us (31%)
  waiting for transfers between devices  48.1 us (28%)
  blocking collectives  20.4 us (12%)
  Pallas kernels  18.4 us (11%)
  local copies, waits for them, and re-layouts  14.3 us (8%)
  between operations  13.6 us (8%)
    ppermute x10, starting transfers between devices, moved_on(): lax.ppermute(value, ('row', 'col'), [(r * GRID_COLS + c, t * GRID_COLS +...  40.4 us
    all_to_all x1, blocking collectives, shared(): return lax.all_to_all(every, 'col', 0, 0, axis_index_groups=groups)  20.4 us
    ppermute x10, waiting for transfers between devices, moved_on(): lax.ppermute(value, ('row', 'col'), [(r * GRID_COLS + c, t * GRID_COLS +...  20.1 us
    all_to_all x1, waiting for transfers between devices, shared(): return lax.all_to_all(every, 'col', 0, 0, axis_index_groups=groups)  18.9 us
    ppermute x2, waiting for transfers between devices, moved(): lax.ppermute(value, axis, [(i, j) for i, j in pairs if 0 <= j < count])  9.08 us
    all_to_all x1, starting transfers between devices, shared(): return lax.all_to_all(every, 'col', 0, 0, axis_index_groups=groups)  8.32 us
    pallas_call x2, Pallas kernels, last(): pl.pallas_call(functools.partial(last_kernel, first), out_shape=shape((W,...  6.83 us
    pallas_call x2, Pallas kernels, middle(): pl.pallas_call(functools.partial(middle_kernel, first), out_shape=[shape(...  6.68 us
  transfers between devices with their start and end apart: 14, of which 6 were waited for; matrix products, arithmetic and copies ran while one was open for 4% of the time, Pallas kernels for 9%

profile of v7, /device:TPU:150, one launch (start us, length us, event | category | flops | bytes accessed | tf_op | source)
XLA Modules:
  0.0 169.5 jit_solution(14273251112444249900)
XLA Ops:
  6.5 0.0 all-gather.2.cloned.1.call-start
  6.5 0.8 fusion.1
  7.3 1.9 %collective-permute-start = (f32[32,256]{1,0:T(8,128)S(1)}, f32[32,256]{1,0:T(8,128)S(1)}, u32[]{:S(2)}, u32[]{:S(2)}) collective-permute-start(f32[32,256]{1,0:T(8,128)S(1)} %get-tuple-element.38), channel_id=1, source_target_pairs={{0,16},{16,32},{32,48},{48,64},{64,80},{80,96},{96,112},{112,128},... | collective-permute-start | bytes 98312 | tf_op jit(solution)/shard_map/ppermute | solution.py:45
  9.2 3.3 %collective-permute-done = f32[32,256]{1,0:T(8,128)S(1)} collective-permute-done((f32[32,256]{1,0:T(8,128)S(1)}, f32[32,256]{1,0:T(8,128)S(1)}, u32[]{:S(2)}, u32[]{:S(2)}) %collective-permute-start) | collective-permute-done | bytes 32800 | tf_op jit(solution)/shard_map/ppermute | solution.py:45
  12.5 0.8 pad_maximum_fusion.1
  13.4 7.0 %collective-permute-start.3 = (f32[32,1024]{1,0:T(8,128)S(1)}, f32[32,1024]{1,0:T(8,128)S(1)}, u32[]{:S(2)}, u32[]{:S(2)}) collective-permute-start(f32[32,1024]{1,0:T(8,128)S(1)} %pad_maximum_fusion.1), channel_id=1, source_target_pairs={{0,0},{1,16},{2,32},{3,48},{4,64},{5,80},{6,96},{7,112},{8,128},{9... | collective-permute-start | bytes 393224 | tf_op jit(solution)/shard_map/ppermute | solution.py:49
  20.4 8.5 %collective-permute-done.3 = f32[32,1024]{1,0:T(8,128)S(1)} collective-permute-done((f32[32,1024]{1,0:T(8,128)S(1)}, f32[32,1024]{1,0:T(8,128)S(1)}, u32[]{:S(2)}, u32[]{:S(2)}) %collective-permute-start.3) | collective-permute-done | bytes 131104 | tf_op jit(solution)/shard_map/ppermute | solution.py:49
  28.9 2.4 %collective-permute-start.4 = (f32[32,1024]{1,0:T(8,128)S(1)}, f32[32,1024]{1,0:T(8,128)S(1)}, u32[]{:S(2)}, u32[]{:S(2)}) collective-permute-start(f32[32,1024]{1,0:T(8,128)S(1)} %collective-permute-done.3), channel_id=1, source_target_pairs={{0,256},{16,272},{32,288},{48,304},{64,320},{80,336},{96,352},{112... | collective-permute-start | bytes 393224 | tf_op jit(solution)/shard_map/ppermute | solution.py:45
  31.2 5.8 %collective-permute-done.4 = f32[32,1024]{1,0:T(8,128)S(1)} collective-permute-done((f32[32,1024]{1,0:T(8,128)S(1)}, f32[32,1024]{1,0:T(8,128)S(1)}, u32[]{:S(2)}, u32[]{:S(2)}) %collective-permute-start.4) | collective-permute-done | bytes 131104 | tf_op jit(solution)/shard_map/ppermute | solution.py:45
  37.0 0.7 pad_maximum_fusion
  37.8 0.0 all-gather.2.cloned.1.call-update
  37.8 20.4 %all_to_all.10 = f32[4,32,1024]{2,1,0:T(8,128)S(1)} all-to-all(f32[4,32,1024]{2,1,0:T(8,128)S(1)} %broadcast_in_dim.6), channel_id=1, replica_groups={{0,4,8,12},{1,5,9,13},{2,6,10,14},{3,7,11,15},{16,20,24,28},{17,21,25,2..., dimensions={0} | all-to-all | bytes 1048576 | tf_op jit(solution)/shard_map/all_to_all | solution.py:179
  58.3 1.6 broadcast_in_dim.15
  59.9 8.3 %all-to-all-start.1 = ((f32[4,128,1024]{2,1,0:T(8,128)}), f32[4,128,1024]{2,1,0:T(8,128)S(1)}, u32[]{:S(2)}, u32[]{:S(2)}) async-start(f32[4,128,1024]{2,1,0:T(8,128)} %broadcast_in_dim.15), calls=%async_computation.1 | async-start | bytes 4194304 | tf_op jit(solution)/shard_map/all_to_all | solution.py:179
  68.2 0.1 pad_add_fusion.where
  68.3 4.1 %fusion = (f32[512,1,512]{2,1,0:T(1,128)S(1)}, f32[512,1,512]{2,1,0:T(1,128)S(1)}) fusion(f32[512,2,512]{2,1,0:T(2,128)} %param.4), kind=kLoop, calls=%fused_computation.5 | loop fusion | bytes 4194304 | tf_op jit(solution)/shard_map/slice | solution.py:194
  72.4 0.0 copy-start.7
  72.4 1.5 copy_bitcast_fusion
  73.9 18.9 %all-to-all-done.1 = f32[4,128,1024]{2,1,0:T(8,128)S(1)} async-done(((f32[4,128,1024]{2,1,0:T(8,128)}), f32[4,128,1024]{2,1,0:T(8,128)S(1)}, u32[]{:S(2)}, u32[]{:S(2)}) %all-to-all-start.1) | async-done | bytes 2097184 | tf_op jit(solution)/shard_map/all_to_all | solution.py:179
  92.8 0.0 copy-done.7
  92.8 0.0 copy-start.5
  92.8 1.2 copy-done.5
  94.1 0.0 copy-start.6
  94.1 1.2 copy-done.6
  95.3 3.5 %left.1 = (f32[256,1024]{1,0:T(8,128)S(1)}, f32[256,512]{1,0:T(8,128)}, f32[256,512]{1,0:T(8,128)}, bf16[2,512,256]{2,1,0:T(8,128)(2,1)S(1)}, bf16[2,512,256]{2,1,0:T(8,128)(2,1)S(1)}) custom-call(s32[2]{0:T(128)S(1)} %pad_add_fusion.where, s32[2,32]{1,0:T(2,128)S(1)} %copy-done.7, f32[4,4,32,1024]{3,2,1,0:T(8,128)S(1)} %bitcast.12, ...), custom_call_target="tpu_custom_call" | custom-call | flops 1610612736 | bytes 7340032 | tf_op jit(solution)/shard_map/left/pallas_call | solution.py:185
  98.8 0.0 copy-start.1
  98.8 0.8 copy-done.1
  99.6 0.0 copy-start.3
  99.6 0.8 copy-done.3
  100.4 1.9 %collective-permute-start.8 = (f32[256,1024]{1,0:T(8,128)S(1)}, f32[256,1024]{1,0:T(8,128)S(1)}, u32[]{:S(2)}, u32[]{:S(2)}) collective-permute-start(f32[256,1024]{1,0:T(8,128)S(1)} %get-tuple-element.30.own0.own1), channel_id=1, source_target_pairs={{0,16},{1,17},{2,18},{3,19},{4,20},{5,21},{6,22},{7,23},{8,24},{9,... | collective-permute-start | bytes 3145736 | tf_op jit(solution)/shard_map/ppermute | solution.py:49
  102.3 1.9 %collective-permute-start.1 = (f32[256,512]{1,0:T(8,128)}, f32[256,512]{1,0:T(8,128)S(1)}, u32[]{:S(2)}, u32[]{:S(2)}) collective-permute-start(f32[256,512]{1,0:T(8,128)} %get-tuple-element.20.own0), channel_id=1, source_target_pairs={{17,33},{18,34},{19,35},{20,36},{21,37},{22,38},{23,39},{24,40},{2... | collective-permute-start | bytes 1572872 | tf_op jit(solution)/shard_map/ppermute | solution.py:49
  104.2 3.6 %collective-permute-start.2 = (f32[256,512]{1,0:T(8,128)}, f32[256,512]{1,0:T(8,128)S(1)}, u32[]{:S(2)}, u32[]{:S(2)}) collective-permute-start(f32[256,512]{1,0:T(8,128)} %get-tuple-element.21.own1), channel_id=1, source_target_pairs={{16,32},{17,33},{18,34},{19,35},{20,36},{21,37},{22,38},{23,39},{2... | collective-permute-start | bytes 1572872 | tf_op jit(solution)/shard_map/ppermute | solution.py:49
  107.9 0.0 all-gather.2.cloned.1.call-done
  107.9 0.0 copy-start
  107.9 2.2 %copy-done = f32[1024,1024]{1,0:T(8,128)S(1)} copy-done((f32[1024,1024]{1,0:T(8,128)S(1)}, f32[1024,1024]{1,0:T(8,128)}, u32[]{:S(2)}) %copy-start) | copy-done | bytes 4194328
  110.1 0.0 copy-start.2
  110.1 0.0 copy-start.4
  110.1 1.4 prepare.1
  111.5 0.0 collective-permute-done.8.got0.got1
  111.5 0.0 copy-done.2
  111.5 0.0 copy-done.4
  111.5 3.0 %middle.3 = (f32[4,256,256]{2,1,0:T(8,128)S(1)}, f32[2,256,256]{2,1,0:T(8,128)S(1)}, f32[256,256]{1,0:T(8,128)S(1)}, f32[256,256]{1,0:T(8,128)S(1)}) custom-call(s32[2]{0:T(128)S(1)} %pad_add_fusion.where, s32[2,32]{1,0:T(2,128)S(1)} %copy-done.7, f32[256,1024]{1,0:T(8,128)S(1)} %get-tuple-element.30.own0.own1, f32[256,1024]{1,0:T(8,128)S(1)} %get-tuple-element.30.own0.own1, ...), custom_call_target="tpu_custom_call" | custom-call | flops 1610612736 | bytes 4194304 | tf_op jit(solution)/shard_map/middle/pallas_call | solution.py:217
  114.6 4.0 %collective-permute-start.10 = (f32[256,256]{1,0:T(8,128)S(1)}, f32[256,256]{1,0:T(8,128)S(1)}, u32[]{:S(2)}, u32[]{:S(2)}) collective-permute-start(f32[256,256]{1,0:T(8,128)S(1)} %get-tuple-element.33), channel_id=1, source_target_pairs={{1,2},{3,4},{5,6},{7,8},{9,10},{11,12},{13,14},{17,18},{19,20},{21... | collective-permute-start | bytes 786440 | tf_op jit(solution)/shard_map/ppermute | solution.py:49
  118.6 1.9 %collective-permute-start.9 = (f32[2,256,256]{2,1,0:T(8,128)S(1)}, f32[2,256,256]{2,1,0:T(8,128)S(1)}, u32[]{:S(2)}, u32[]{:S(2)}) collective-permute-start(f32[2,256,256]{2,1,0:T(8,128)S(1)} %get-tuple-element.32), channel_id=1, source_target_pairs={{0,1},{2,3},{4,5},{6,7},{8,9},{10,11},{12,13},{14,15},{16,17},{18,... | collective-permute-start | bytes 1572872 | tf_op jit(solution)/shard_map/ppermute | solution.py:49
  120.5 0.0 collective-permute-done.1.got0
  120.5 0.0 collective-permute-done.2.got1
  120.6 3.7 %middle.2 = (f32[4,256,256]{2,1,0:T(8,128)S(1)}, f32[2,256,256]{2,1,0:T(8,128)S(1)}, f32[256,256]{1,0:T(8,128)S(1)}, f32[256,256]{1,0:T(8,128)S(1)}) custom-call(s32[2]{0:T(128)S(1)} %pad_add_fusion.where, s32[2,32]{1,0:T(2,128)S(1)} %copy-done.7, f32[256,512]{1,0:T(8,128)} %get-tuple-element.20.own0, f32[256,512]{1,0:T(8,128)} %get-tuple-element.21.own1, ...), custom_call_target="tpu_custom_call" | custom-call | flops 1610612736 | bytes 4194304 | tf_op jit(solution)/shard_map/middle/pallas_call | solution.py:217
  124.2 3.9 %collective-permute-start.5 = (f32[2,256,256]{2,1,0:T(8,128)S(1)}, f32[2,256,256]{2,1,0:T(8,128)S(1)}, u32[]{:S(2)}, u32[]{:S(2)}) collective-permute-start(f32[2,256,256]{2,1,0:T(8,128)S(1)} %get-tuple-element.27), channel_id=1, source_target_pairs={{0,1},{2,3},{4,5},{6,7},{8,9},{10,11},{12,13},{14,15},{16,17},{18,... | collective-permute-start | bytes 1572872 | tf_op jit(solution)/shard_map/ppermute | solution.py:49
  128.1 6.0 %collective-permute-start.11 = (f32[256,256]{1,0:T(8,128)S(1)}, f32[256,256]{1,0:T(8,128)S(1)}, u32[]{:S(2)}, u32[]{:S(2)}) collective-permute-start(f32[256,256]{1,0:T(8,128)S(1)} %get-tuple-element.34), channel_id=1, source_target_pairs={{1,2},{3,4},{5,6},{7,8},{9,10},{11,12},{13,14},{15,0},{17,18},{19,... | collective-permute-start | bytes 786440 | tf_op jit(solution)/shard_map/ppermute | solution.py:49
  134.2 4.0 %collective-permute-start.6 = (f32[256,256]{1,0:T(8,128)S(1)}, f32[256,256]{1,0:T(8,128)S(1)}, u32[]{:S(2)}, u32[]{:S(2)}) collective-permute-start(f32[256,256]{1,0:T(8,128)S(1)} %get-tuple-element.28), channel_id=1, source_target_pairs={{1,2},{3,4},{5,6},{7,8},{9,10},{11,12},{13,14},{17,18},{19,20},{21... | collective-permute-start | bytes 786440 | tf_op jit(solution)/shard_map/ppermute | solution.py:49
  138.2 0.0 collective-permute-done.10.edge1
  138.2 6.0 %collective-permute-start.7 = (f32[256,256]{1,0:T(8,128)S(1)}, f32[256,256]{1,0:T(8,128)S(1)}, u32[]{:S(2)}, u32[]{:S(2)}) collective-permute-start(f32[256,256]{1,0:T(8,128)S(1)} %get-tuple-element.29), channel_id=1, source_target_pairs={{1,2},{3,4},{5,6},{7,8},{9,10},{11,12},{13,14},{15,0},{17,18},{19,... | collective-permute-start | bytes 786440 | tf_op jit(solution)/shard_map/ppermute | solution.py:49
  144.3 0.0 collective-permute-done.11.edge0
  144.3 0.0 collective-permute-done.9.side
  144.3 3.4 %last.2.rest_0_ = f32[512,2,512]{2,1,0:T(2,128)} custom-call(s32[2]{0:T(128)S(1)} %pad_add_fusion.where, s32[2,32]{1,0:T(2,128)S(1)} %copy-done.7, f32[4,256,256]{2,1,0:T(8,128)S(1)} %get-tuple-element.31.kept, f32[2,256,256]{2,1,0:T(8,128)S(1)} %collective-permute-done.9.side, f32[256,256]{1,0:T(8,128)S(1)} %collective-permute-done.10.edge1, ...), custom_call_target="tpu_custom_call" | custom-call | flops 805306368 | bytes 4194304 | tf_op jit(solution)/shard_map/last/pallas_call | solution.py:247
  147.7 7.3 %collective-permute-done.6.edge1 = f32[256,256]{1,0:T(8,128)S(1)} collective-permute-done((f32[256,256]{1,0:T(8,128)S(1)}, f32[256,256]{1,0:T(8,128)S(1)}, u32[]{:S(2)}, u32[]{:S(2)}) %collective-permute-start.6) | collective-permute-done | bytes 262176 | tf_op jit(solution)/shard_map/ppermute | solution.py:49
  155.1 4.2 %collective-permute-done.7.edge0 = f32[256,256]{1,0:T(8,128)S(1)} collective-permute-done((f32[256,256]{1,0:T(8,128)S(1)}, f32[256,256]{1,0:T(8,128)S(1)}, u32[]{:S(2)}, u32[]{:S(2)}) %collective-permute-start.7) | collective-permute-done | bytes 262176 | tf_op jit(solution)/shard_map/ppermute | solution.py:49
  159.3 0.0 collective-permute-done.5.side
  159.3 3.4 %last.3 = f32[512,2,512]{2,1,0:T(2,128)} custom-call(s32[2]{0:T(128)S(1)} %pad_add_fusion.where, s32[2,32]{1,0:T(2,128)S(1)} %copy-done.7, f32[4,256,256]{2,1,0:T(8,128)S(1)} %get-tuple-element.26.kept, f32[2,256,256]{2,1,0:T(8,128)S(1)} %collective-permute-done.5.side, f32[256,256]{1,0:T(8,128)S(1)} %collective-permute-done.6.edge1, ...), custom_call_target="tpu_custom_call", output_to_operand_aliasing={{}: (8, {})} | custom-call | flops 805306368 | bytes 4194304 | tf_op jit(solution)/shard_map/last/pallas_call | solution.py:247
  (1 shorter events, 0.0 us)
Async XLA Ops:
  6.5 101.3 %all-gather.2.cloned.1.call-start = ((), (), s32[]{:S(2)}) async-start(), calls=%async_computation.2 | async-start | bytes 4456448 | tf_op jit(solution)/shard_map/all_gather | solution.py:174
  7.3 5.2 %collective-permute-start = (f32[32,256]{1,0:T(8,128)S(1)}, f32[32,256]{1,0:T(8,128)S(1)}, u32[]{:S(2)}, u32[]{:S(2)}) collective-permute-start(f32[32,256]{1,0:T(8,128)S(1)} %get-tuple-element.38), channel_id=1, source_target_pairs={{0,16},{16,32},{32,48},{48,64},{64,80},{80,96},{96,112},{112,128},... | collective-permute-start | bytes 98312 | tf_op jit(solution)/shard_map/ppermute | solution.py:45
  13.4 15.5 %collective-permute-start.3 = (f32[32,1024]{1,0:T(8,128)S(1)}, f32[32,1024]{1,0:T(8,128)S(1)}, u32[]{:S(2)}, u32[]{:S(2)}) collective-permute-start(f32[32,1024]{1,0:T(8,128)S(1)} %pad_maximum_fusion.1), channel_id=1, source_target_pairs={{0,0},{1,16},{2,32},{3,48},{4,64},{5,80},{6,96},{7,112},{8,128},{9... | collective-permute-start | bytes 393224 | tf_op jit(solution)/shard_map/ppermute | solution.py:49
  28.9 8.1 %collective-permute-start.4 = (f32[32,1024]{1,0:T(8,128)S(1)}, f32[32,1024]{1,0:T(8,128)S(1)}, u32[]{:S(2)}, u32[]{:S(2)}) collective-permute-start(f32[32,1024]{1,0:T(8,128)S(1)} %collective-permute-done.3), channel_id=1, source_target_pairs={{0,256},{16,272},{32,288},{48,304},{64,320},{80,336},{96,352},{112... | collective-permute-start | bytes 393224 | tf_op jit(solution)/shard_map/ppermute | solution.py:45
  59.9 33.0 %all-to-all-start.1 = ((f32[4,128,1024]{2,1,0:T(8,128)}), f32[4,128,1024]{2,1,0:T(8,128)S(1)}, u32[]{:S(2)}, u32[]{:S(2)}) async-start(f32[4,128,1024]{2,1,0:T(8,128)} %broadcast_in_dim.15), calls=%async_computation.1 | async-start | bytes 4194304 | tf_op jit(solution)/shard_map/all_to_all | solution.py:179
  72.4 20.5 %copy-start.7 = (s32[2,32]{1,0:T(2,128)S(1)}, s32[2,32]{1,0:T(2,128)}, u32[]{:S(2)}) copy-start(s32[2,32]{1,0:T(2,128)} %lives.9) | copy-start | bytes 772
  92.8 1.2 copy-start.5
  94.1 1.2 copy-start.6
  98.8 0.8 copy-start.1
  99.6 0.8 copy-start.3
  100.4 11.1 %collective-permute-start.8 = (f32[256,1024]{1,0:T(8,128)S(1)}, f32[256,1024]{1,0:T(8,128)S(1)}, u32[]{:S(2)}, u32[]{:S(2)}) collective-permute-start(f32[256,1024]{1,0:T(8,128)S(1)} %get-tuple-element.30.own0.own1), channel_id=1, source_target_pairs={{0,16},{1,17},{2,18},{3,19},{4,20},{5,21},{6,22},{7,23},{8,24},{9,... | collective-permute-start | bytes 3145736 | tf_op jit(solution)/shard_map/ppermute | solution.py:49
  102.3 18.2 %collective-permute-start.1 = (f32[256,512]{1,0:T(8,128)}, f32[256,512]{1,0:T(8,128)S(1)}, u32[]{:S(2)}, u32[]{:S(2)}) collective-permute-start(f32[256,512]{1,0:T(8,128)} %get-tuple-element.20.own0), channel_id=1, source_target_pairs={{17,33},{18,34},{19,35},{20,36},{21,37},{22,38},{23,39},{24,40},{2... | collective-permute-start | bytes 1572872 | tf_op jit(solution)/shard_map/ppermute | solution.py:49
  104.2 16.3 %collective-permute-start.2 = (f32[256,512]{1,0:T(8,128)}, f32[256,512]{1,0:T(8,128)S(1)}, u32[]{:S(2)}, u32[]{:S(2)}) collective-permute-start(f32[256,512]{1,0:T(8,128)} %get-tuple-element.21.own1), channel_id=1, source_target_pairs={{16,32},{17,33},{18,34},{19,35},{20,36},{21,37},{22,38},{23,39},{2... | collective-permute-start | bytes 1572872 | tf_op jit(solution)/shard_map/ppermute | solution.py:49
  107.9 2.2 %copy-start = (f32[1024,1024]{1,0:T(8,128)S(1)}, f32[1024,1024]{1,0:T(8,128)}, u32[]{:S(2)}) copy-start(f32[1024,1024]{1,0:T(8,128)} %all-gather.2.cloned.1.call-done) | copy-start | bytes 12582916
  110.1 1.4 copy-start.2
  110.1 1.4 copy-start.4
  114.6 23.6 %collective-permute-start.10 = (f32[256,256]{1,0:T(8,128)S(1)}, f32[256,256]{1,0:T(8,128)S(1)}, u32[]{:S(2)}, u32[]{:S(2)}) collective-permute-start(f32[256,256]{1,0:T(8,128)S(1)} %get-tuple-element.33), channel_id=1, source_target_pairs={{1,2},{3,4},{5,6},{7,8},{9,10},{11,12},{13,14},{17,18},{19,20},{21... | collective-permute-start | bytes 786440 | tf_op jit(solution)/shard_map/ppermute | solution.py:49
  118.6 25.7 %collective-permute-start.9 = (f32[2,256,256]{2,1,0:T(8,128)S(1)}, f32[2,256,256]{2,1,0:T(8,128)S(1)}, u32[]{:S(2)}, u32[]{:S(2)}) collective-permute-start(f32[2,256,256]{2,1,0:T(8,128)S(1)} %get-tuple-element.32), channel_id=1, source_target_pairs={{0,1},{2,3},{4,5},{6,7},{8,9},{10,11},{12,13},{14,15},{16,17},{18,... | collective-permute-start | bytes 1572872 | tf_op jit(solution)/shard_map/ppermute | solution.py:49
  124.2 35.1 %collective-permute-start.5 = (f32[2,256,256]{2,1,0:T(8,128)S(1)}, f32[2,256,256]{2,1,0:T(8,128)S(1)}, u32[]{:S(2)}, u32[]{:S(2)}) collective-permute-start(f32[2,256,256]{2,1,0:T(8,128)S(1)} %get-tuple-element.27), channel_id=1, source_target_pairs={{0,1},{2,3},{4,5},{6,7},{8,9},{10,11},{12,13},{14,15},{16,17},{18,... | collective-permute-start | bytes 1572872 | tf_op jit(solution)/shard_map/ppermute | solution.py:49
  128.1 16.1 %collective-permute-start.11 = (f32[256,256]{1,0:T(8,128)S(1)}, f32[256,256]{1,0:T(8,128)S(1)}, u32[]{:S(2)}, u32[]{:S(2)}) collective-permute-start(f32[256,256]{1,0:T(8,128)S(1)} %get-tuple-element.34), channel_id=1, source_target_pairs={{1,2},{3,4},{5,6},{7,8},{9,10},{11,12},{13,14},{15,0},{17,18},{19,... | collective-permute-start | bytes 786440 | tf_op jit(solution)/shard_map/ppermute | solution.py:49
  134.2 20.9 %collective-permute-start.6 = (f32[256,256]{1,0:T(8,128)S(1)}, f32[256,256]{1,0:T(8,128)S(1)}, u32[]{:S(2)}, u32[]{:S(2)}) collective-permute-start(f32[256,256]{1,0:T(8,128)S(1)} %get-tuple-element.28), channel_id=1, source_target_pairs={{1,2},{3,4},{5,6},{7,8},{9,10},{11,12},{13,14},{17,18},{19,20},{21... | collective-permute-start | bytes 786440 | tf_op jit(solution)/shard_map/ppermute | solution.py:49
  138.2 21.0 %collective-permute-start.7 = (f32[256,256]{1,0:T(8,128)S(1)}, f32[256,256]{1,0:T(8,128)S(1)}, u32[]{:S(2)}, u32[]{:S(2)}) collective-permute-start(f32[256,256]{1,0:T(8,128)S(1)} %get-tuple-element.29), channel_id=1, source_target_pairs={{1,2},{3,4},{5,6},{7,8},{9,10},{11,12},{13,14},{15,0},{17,18},{19,... | collective-permute-start | bytes 786440 | tf_op jit(solution)/shard_map/ppermute | solution.py:49
Sparse Core Ops, SparseCore 0:
  37.9 47.6 all-gather.1

commit v8 on v7

--- a/solution.py
+++ b/solution.py
@@ -59,18 +59,25 @@
     return moved_on(value, pairs + [(b, a) for a, b in pairs])
 
 
-def left_kernel(where, lives, pieces, h0, h1, send_a, send_b0, send_b1, fb_high, fb_low, d_high, d_low):
+def borders_kernel(pieces, fb_high, fb_low):
+    for x in range(RING):
+        for y in range(RING):
+            rows = slice((y * RING + x) * 32, (y * RING + x) * 32 + 32)
+            high, low = split(pieces[x, y, :, W:])
+            for side in range(2):
+                lanes = slice(side * HALF, side * HALF + HALF)
+                fb_high[side, rows, :] = high[:, lanes]
+                fb_low[side, rows, :] = low[:, lanes]
+
+
+def left_kernel(where, lives, pieces, h0, h1, send_a, send_b0, send_b1, d_high, d_low):
     row, col = where[0], where[1]
     for x in range(RING):
         for y in range(RING):
             rows = slice((y * RING + x) * 32, (y * RING + x) * 32 + 32)
-            high, low = split(pieces[x, y])
-            for side in range(2):
-                lanes = slice(W + side * HALF, W + side * HALF + HALF)
-                fb_high[side, rows, :] = high[:, lanes]
-                fb_low[side, rows, :] = low[:, lanes]
-            d_high[rows, :] = high[:, :W]
-            d_low[rows, :] = low[:, :W]
+            high, low = split(pieces[x, y, :, :W])
+            d_high[rows, :] = high
+            d_low[rows, :] = low
     odd = lax.rem(row, 2) == 1
     live_row = live(lives, 0, row)
     factor = (d_high[...], d_low[...])
@@ -182,16 +189,25 @@
     along_x = [[x + RING * y for x in range(RING)] for y in range(RING)]
     by_row = shared(by_y.reshape(RING * 32, 2 * W), along_x).reshape(RING, RING, 32, 2 * W)
 
-    send_a, send_b0, send_b1, fb_high, fb_low = pl.pallas_call(
+    send_a, send_b0, send_b1 = pl.pallas_call(
         left_kernel,
-        out_shape=[shape((HALF, 2 * W), F32)] + [shape((HALF, W), F32)] * 2 + [shape((2, W, HALF), BF16)] * 2,
+        out_shape=[shape((HALF, 2 * W), F32)] + [shape((HALF, W), F32)] * 2,
         in_specs=[SMEM, SMEM] + [VMEM] * 3,
-        out_specs=[VMEM] * 5,
+        out_specs=[VMEM] * 3,
         scratch_shapes=[pltpu.VMEM((W, W), BF16)] * 2,
         compiler_params=PARAMS,
         cost_estimate=cost(2, 7),
         name="left",
     )(where, window_live, by_row, hessenberg[:, 0], hessenberg[:, 1])
+    fb_high, fb_low = pl.pallas_call(
+        borders_kernel,
+        out_shape=[shape((2, W, HALF), BF16)] * 2,
+        in_specs=[VMEM],
+        out_specs=[VMEM] * 2,
+        compiler_params=PARAMS,
+        cost_estimate=cost(0, 2),
+        name="borders",
+    )(by_row)
 
     every_col = range(GRID_COLS)
     pairs = [((r, c), (r + 1, c)) for r in range(1, 31, 2) for c in every_col]

time: 170 us -> 172 us (1.012)
  no operation moved by 1% of the time
where the time goes in v8:
time: 172 us; the launch traced here: 171 us
  starting transfers between devices  53 us (31%)
  waiting for transfers between devices  48.1 us (28%)
  blocking collectives  20.4 us (12%)
  Pallas kernels  19.5 us (11%)
  local copies, waits for them, and re-layouts  14.3 us (8%)
  between operations  13.6 us (8%)
    ppermute x10, starting transfers between devices, moved_on(): lax.ppermute(value, ('row', 'col'), [(r * GRID_COLS + c, t * GRID_COLS +...  40.4 us
    all_to_all x1, blocking collectives, shared(): return lax.all_to_all(every, 'col', 0, 0, axis_index_groups=groups)  20.4 us
    ppermute x10, waiting for transfers between devices, moved_on(): lax.ppermute(value, ('row', 'col'), [(r * GRID_COLS + c, t * GRID_COLS +...  20.1 us
    all_to_all x1, waiting for transfers between devices, shared(): return lax.all_to_all(every, 'col', 0, 0, axis_index_groups=groups)  18.9 us
    ppermute x2, waiting for transfers between devices, moved(): lax.ppermute(value, axis, [(i, j) for i, j in pairs if 0 <= j < count])  9.08 us
    all_to_all x1, starting transfers between devices, shared(): return lax.all_to_all(every, 'col', 0, 0, axis_index_groups=groups)  8.32 us
    pallas_call x2, Pallas kernels, middle(): pl.pallas_call(functools.partial(middle_kernel, first), out_shape=[shape(...  7.96 us
    pallas_call x2, Pallas kernels, last(): pl.pallas_call(functools.partial(last_kernel, first), out_shape=shape((W,...  6.71 us
  transfers between devices with their start and end apart: 14, of which 6 were waited for; matrix products, arithmetic and copies ran while one was open for 4% of the time, Pallas kernels for 9%

profile of v8, /device:TPU:150, one launch (start us, length us, event | category | flops | bytes accessed | tf_op | source)
XLA Modules:
  0.0 170.7 jit_solution(5084609083865885048)
XLA Ops:
  6.5 0.0 all-gather.2.cloned.1.call-start
  6.5 0.8 fusion.1
  7.3 1.9 %collective-permute-start = (f32[32,256]{1,0:T(8,128)S(1)}, f32[32,256]{1,0:T(8,128)S(1)}, u32[]{:S(2)}, u32[]{:S(2)}) collective-permute-start(f32[32,256]{1,0:T(8,128)S(1)} %get-tuple-element.38), channel_id=1, source_target_pairs={{0,16},{16,32},{32,48},{48,64},{64,80},{80,96},{96,112},{112,128},... | collective-permute-start | bytes 98312 | tf_op jit(solution)/shard_map/ppermute | solution.py:45
  9.2 3.3 %collective-permute-done = f32[32,256]{1,0:T(8,128)S(1)} collective-permute-done((f32[32,256]{1,0:T(8,128)S(1)}, f32[32,256]{1,0:T(8,128)S(1)}, u32[]{:S(2)}, u32[]{:S(2)}) %collective-permute-start) | collective-permute-done | bytes 32800 | tf_op jit(solution)/shard_map/ppermute | solution.py:45
  12.5 0.8 pad_maximum_fusion.1
  13.4 7.0 %collective-permute-start.3 = (f32[32,1024]{1,0:T(8,128)S(1)}, f32[32,1024]{1,0:T(8,128)S(1)}, u32[]{:S(2)}, u32[]{:S(2)}) collective-permute-start(f32[32,1024]{1,0:T(8,128)S(1)} %pad_maximum_fusion.1), channel_id=1, source_target_pairs={{0,0},{1,16},{2,32},{3,48},{4,64},{5,80},{6,96},{7,112},{8,128},{9... | collective-permute-start | bytes 393224 | tf_op jit(solution)/shard_map/ppermute | solution.py:49
  20.4 8.5 %collective-permute-done.3 = f32[32,1024]{1,0:T(8,128)S(1)} collective-permute-done((f32[32,1024]{1,0:T(8,128)S(1)}, f32[32,1024]{1,0:T(8,128)S(1)}, u32[]{:S(2)}, u32[]{:S(2)}) %collective-permute-start.3) | collective-permute-done | bytes 131104 | tf_op jit(solution)/shard_map/ppermute | solution.py:49
  28.9 2.4 %collective-permute-start.4 = (f32[32,1024]{1,0:T(8,128)S(1)}, f32[32,1024]{1,0:T(8,128)S(1)}, u32[]{:S(2)}, u32[]{:S(2)}) collective-permute-start(f32[32,1024]{1,0:T(8,128)S(1)} %collective-permute-done.3), channel_id=1, source_target_pairs={{0,256},{16,272},{32,288},{48,304},{64,320},{80,336},{96,352},{112... | collective-permute-start | bytes 393224 | tf_op jit(solution)/shard_map/ppermute | solution.py:45
  31.2 5.8 %collective-permute-done.4 = f32[32,1024]{1,0:T(8,128)S(1)} collective-permute-done((f32[32,1024]{1,0:T(8,128)S(1)}, f32[32,1024]{1,0:T(8,128)S(1)}, u32[]{:S(2)}, u32[]{:S(2)}) %collective-permute-start.4) | collective-permute-done | bytes 131104 | tf_op jit(solution)/shard_map/ppermute | solution.py:45
  37.0 0.8 pad_maximum_fusion
  37.8 0.0 all-gather.2.cloned.1.call-update
  37.9 20.4 %all_to_all.10 = f32[4,32,1024]{2,1,0:T(8,128)S(1)} all-to-all(f32[4,32,1024]{2,1,0:T(8,128)S(1)} %broadcast_in_dim.6), channel_id=1, replica_groups={{0,4,8,12},{1,5,9,13},{2,6,10,14},{3,7,11,15},{16,20,24,28},{17,21,25,2..., dimensions={0} | all-to-all | bytes 1048576 | tf_op jit(solution)/shard_map/all_to_all | solution.py:186
  58.3 1.6 broadcast_in_dim.15
  59.9 8.3 %all-to-all-start.1 = ((f32[4,128,1024]{2,1,0:T(8,128)}), f32[4,128,1024]{2,1,0:T(8,128)S(1)}, u32[]{:S(2)}, u32[]{:S(2)}) async-start(f32[4,128,1024]{2,1,0:T(8,128)} %broadcast_in_dim.15), calls=%async_computation.1 | async-start | bytes 4194304 | tf_op jit(solution)/shard_map/all_to_all | solution.py:186
  68.2 0.1 pad_add_fusion.where
  68.3 4.1 %fusion = (f32[512,1,512]{2,1,0:T(1,128)S(1)}, f32[512,1,512]{2,1,0:T(1,128)S(1)}) fusion(f32[512,2,512]{2,1,0:T(2,128)} %param.4), kind=kLoop, calls=%fused_computation.5 | loop fusion | bytes 4194304 | tf_op jit(solution)/shard_map/slice | solution.py:201
  72.4 0.0 copy-start.7
  72.4 1.5 copy_bitcast_fusion
  74.0 18.9 %all-to-all-done.1 = f32[4,128,1024]{2,1,0:T(8,128)S(1)} async-done(((f32[4,128,1024]{2,1,0:T(8,128)}), f32[4,128,1024]{2,1,0:T(8,128)S(1)}, u32[]{:S(2)}, u32[]{:S(2)}) %all-to-all-start.1) | async-done | bytes 2097184 | tf_op jit(solution)/shard_map/all_to_all | solution.py:186
  92.9 0.0 copy-done.7
  92.9 0.0 copy-start.5
  92.9 1.2 copy-done.5
  94.1 0.0 copy-start.6
  94.1 1.2 copy-done.6
  95.3 3.3 %left.1 = (f32[256,1024]{1,0:T(8,128)S(1)}, f32[256,512]{1,0:T(8,128)}, f32[256,512]{1,0:T(8,128)}) custom-call(s32[2]{0:T(128)S(1)} %pad_add_fusion.where, s32[2,32]{1,0:T(2,128)S(1)} %copy-done.7, f32[4,4,32,1024]{3,2,1,0:T(8,128)S(1)} %bitcast.11, f32[512,512]{1,0:T(8,128)S(1)} %copy-done.6, f32[512,512]{1,0:T(8,128)S(1)} %copy-done.5), custom_call_target="tpu_custom_call" | custom-call | flops 1610612736 | bytes 7340032 | tf_op jit(solution)/shard_map/left/pallas_call | solution.py:192
  98.6 1.9 %collective-permute-start.8 = (f32[256,1024]{1,0:T(8,128)S(1)}, f32[256,1024]{1,0:T(8,128)}, u32[]{:S(2)}, u32[]{:S(2)}) collective-permute-start(f32[256,1024]{1,0:T(8,128)S(1)} %get-tuple-element.30.own0.own1), channel_id=1, source_target_pairs={{0,16},{1,17},{2,18},{3,19},{4,20},{5,21},{6,22},{7,23},{8,24},{9,... | collective-permute-start | bytes 3145736 | tf_op jit(solution)/shard_map/ppermute | solution.py:49
  100.5 1.9 %collective-permute-start.1 = (f32[256,512]{1,0:T(8,128)}, f32[256,512]{1,0:T(8,128)}, u32[]{:S(2)}, u32[]{:S(2)}) collective-permute-start(f32[256,512]{1,0:T(8,128)} %get-tuple-element.20.own0), channel_id=1, source_target_pairs={{17,33},{18,34},{19,35},{20,36},{21,37},{22,38},{23,39},{24,40},{2... | collective-permute-start | bytes 1572872 | tf_op jit(solution)/shard_map/ppermute | solution.py:49
  102.4 3.6 %collective-permute-start.2 = (f32[256,512]{1,0:T(8,128)}, f32[256,512]{1,0:T(8,128)}, u32[]{:S(2)}, u32[]{:S(2)}) collective-permute-start(f32[256,512]{1,0:T(8,128)} %get-tuple-element.21.own1), channel_id=1, source_target_pairs={{16,32},{17,33},{18,34},{19,35},{20,36},{21,37},{22,38},{23,39},{2... | collective-permute-start | bytes 1572872 | tf_op jit(solution)/shard_map/ppermute | solution.py:49
  106.1 0.1 borders.1
  106.2 0.0 copy-start.1
  106.2 0.8 copy-done.1
  107.0 0.0 copy-start.3
  107.0 0.8 copy-done.3
  107.8 0.0 all-gather.2.cloned.1.call-done
  107.8 0.0 copy-start
  107.8 2.2 %copy-done = f32[1024,1024]{1,0:T(8,128)S(1)} copy-done((f32[1024,1024]{1,0:T(8,128)S(1)}, f32[1024,1024]{1,0:T(8,128)}, u32[]{:S(2)}) %copy-start) | copy-done | bytes 4194328
  110.0 0.0 copy-start.2
  110.0 0.0 copy-start.4
  110.0 1.4 prepare.1
  111.4 0.0 collective-permute-done.8.got0.got1
  111.4 0.0 copy-done.2
  111.5 0.0 copy-done.4
  111.5 4.1 %middle.3 = (f32[4,256,256]{2,1,0:T(8,128)S(1)}, f32[2,256,256]{2,1,0:T(8,128)S(1)}, f32[256,256]{1,0:T(8,128)S(1)}, f32[256,256]{1,0:T(8,128)S(1)}) custom-call(s32[2]{0:T(128)S(1)} %pad_add_fusion.where, s32[2,32]{1,0:T(2,128)S(1)} %copy-done.7, f32[256,1024]{1,0:T(8,128)S(1)} %get-tuple-element.30.own0.own1, f32[256,1024]{1,0:T(8,128)S(1)} %get-tuple-element.30.own0.own1, ...), custom_call_target="tpu_custom_call" | custom-call | flops 1610612736 | bytes 4194304 | tf_op jit(solution)/shard_map/middle/pallas_call | solution.py:233
  115.5 4.0 %collective-permute-start.10 = (f32[256,256]{1,0:T(8,128)S(1)}, f32[256,256]{1,0:T(8,128)S(1)}, u32[]{:S(2)}, u32[]{:S(2)}) collective-permute-start(f32[256,256]{1,0:T(8,128)S(1)} %get-tuple-element.33), channel_id=1, source_target_pairs={{1,2},{3,4},{5,6},{7,8},{9,10},{11,12},{13,14},{17,18},{19,20},{21... | collective-permute-start | bytes 786440 | tf_op jit(solution)/shard_map/ppermute | solution.py:49
  119.6 1.9 %collective-permute-start.9 = (f32[2,256,256]{2,1,0:T(8,128)S(1)}, f32[2,256,256]{2,1,0:T(8,128)S(1)}, u32[]{:S(2)}, u32[]{:S(2)}) collective-permute-start(f32[2,256,256]{2,1,0:T(8,128)S(1)} %get-tuple-element.32), channel_id=1, source_target_pairs={{0,1},{2,3},{4,5},{6,7},{8,9},{10,11},{12,13},{14,15},{16,17},{18,... | collective-permute-start | bytes 1572872 | tf_op jit(solution)/shard_map/ppermute | solution.py:49
  121.5 0.0 collective-permute-done.1.got0
  121.5 0.0 collective-permute-done.2.got1
  121.5 3.9 %middle.2 = (f32[4,256,256]{2,1,0:T(8,128)S(1)}, f32[2,256,256]{2,1,0:T(8,128)S(1)}, f32[256,256]{1,0:T(8,128)S(1)}, f32[256,256]{1,0:T(8,128)S(1)}) custom-call(s32[2]{0:T(128)S(1)} %pad_add_fusion.where, s32[2,32]{1,0:T(2,128)S(1)} %copy-done.7, f32[256,512]{1,0:T(8,128)} %get-tuple-element.20.own0, f32[256,512]{1,0:T(8,128)} %get-tuple-element.21.own1, ...), custom_call_target="tpu_custom_call" | custom-call | flops 1610612736 | bytes 4194304 | tf_op jit(solution)/shard_map/middle/pallas_call | solution.py:233
  125.4 3.9 %collective-permute-start.5 = (f32[2,256,256]{2,1,0:T(8,128)S(1)}, f32[2,256,256]{2,1,0:T(8,128)S(1)}, u32[]{:S(2)}, u32[]{:S(2)}) collective-permute-start(f32[2,256,256]{2,1,0:T(8,128)S(1)} %get-tuple-element.27), channel_id=1, source_target_pairs={{0,1},{2,3},{4,5},{6,7},{8,9},{10,11},{12,13},{14,15},{16,17},{18,... | collective-permute-start | bytes 1572872 | tf_op jit(solution)/shard_map/ppermute | solution.py:49
  129.3 6.0 %collective-permute-start.11 = (f32[256,256]{1,0:T(8,128)S(1)}, f32[256,256]{1,0:T(8,128)S(1)}, u32[]{:S(2)}, u32[]{:S(2)}) collective-permute-start(f32[256,256]{1,0:T(8,128)S(1)} %get-tuple-element.34), channel_id=1, source_target_pairs={{1,2},{3,4},{5,6},{7,8},{9,10},{11,12},{13,14},{15,0},{17,18},{19,... | collective-permute-start | bytes 786440 | tf_op jit(solution)/shard_map/ppermute | solution.py:49
  135.4 4.0 %collective-permute-start.6 = (f32[256,256]{1,0:T(8,128)S(1)}, f32[256,256]{1,0:T(8,128)S(1)}, u32[]{:S(2)}, u32[]{:S(2)}) collective-permute-start(f32[256,256]{1,0:T(8,128)S(1)} %get-tuple-element.28), channel_id=1, source_target_pairs={{1,2},{3,4},{5,6},{7,8},{9,10},{11,12},{13,14},{17,18},{19,20},{21... | collective-permute-start | bytes 786440 | tf_op jit(solution)/shard_map/ppermute | solution.py:49
  139.4 0.0 collective-permute-done.10.edge1
  139.4 6.0 %collective-permute-start.7 = (f32[256,256]{1,0:T(8,128)S(1)}, f32[256,256]{1,0:T(8,128)S(1)}, u32[]{:S(2)}, u32[]{:S(2)}) collective-permute-start(f32[256,256]{1,0:T(8,128)S(1)} %get-tuple-element.29), channel_id=1, source_target_pairs={{1,2},{3,4},{5,6},{7,8},{9,10},{11,12},{13,14},{15,0},{17,18},{19,... | collective-permute-start | bytes 786440 | tf_op jit(solution)/shard_map/ppermute | solution.py:49
  145.5 0.0 collective-permute-done.11.edge0
  145.5 0.0 collective-permute-done.9.side
  145.5 3.4 %last.2.rest_0_ = f32[512,2,512]{2,1,0:T(2,128)} custom-call(s32[2]{0:T(128)S(1)} %pad_add_fusion.where, s32[2,32]{1,0:T(2,128)S(1)} %copy-done.7, f32[4,256,256]{2,1,0:T(8,128)S(1)} %get-tuple-element.31.kept, f32[2,256,256]{2,1,0:T(8,128)S(1)} %collective-permute-done.9.side, f32[256,256]{1,0:T(8,128)S(1)} %collective-permute-done.10.edge1, ...), custom_call_target="tpu_custom_call" | custom-call | flops 805306368 | bytes 4194304 | tf_op jit(solution)/shard_map/last/pallas_call | solution.py:263
  148.9 7.4 %collective-permute-done.6.edge1 = f32[256,256]{1,0:T(8,128)S(1)} collective-permute-done((f32[256,256]{1,0:T(8,128)S(1)}, f32[256,256]{1,0:T(8,128)S(1)}, u32[]{:S(2)}, u32[]{:S(2)}) %collective-permute-start.6) | collective-permute-done | bytes 262176 | tf_op jit(solution)/shard_map/ppermute | solution.py:49
  156.3 4.2 %collective-permute-done.7.edge0 = f32[256,256]{1,0:T(8,128)S(1)} collective-permute-done((f32[256,256]{1,0:T(8,128)S(1)}, f32[256,256]{1,0:T(8,128)S(1)}, u32[]{:S(2)}, u32[]{:S(2)}) %collective-permute-start.7) | collective-permute-done | bytes 262176 | tf_op jit(solution)/shard_map/ppermute | solution.py:49
  160.5 0.0 collective-permute-done.5.side
  160.5 3.4 %last.3 = f32[512,2,512]{2,1,0:T(2,128)} custom-call(s32[2]{0:T(128)S(1)} %pad_add_fusion.where, s32[2,32]{1,0:T(2,128)S(1)} %copy-done.7, f32[4,256,256]{2,1,0:T(8,128)S(1)} %get-tuple-element.26.kept, f32[2,256,256]{2,1,0:T(8,128)S(1)} %collective-permute-done.5.side, f32[256,256]{1,0:T(8,128)S(1)} %collective-permute-done.6.edge1, ...), custom_call_target="tpu_custom_call", output_to_operand_aliasing={{}: (8, {})} | custom-call | flops 805306368 | bytes 4194304 | tf_op jit(solution)/shard_map/last/pallas_call | solution.py:263
  (1 shorter events, 0.0 us)
Async XLA Ops:
  6.5 101.3 %all-gather.2.cloned.1.call-start = ((), (), s32[]{:S(2)}) async-start(), calls=%async_computation.2 | async-start | bytes 4456448 | tf_op jit(solution)/shard_map/all_gather | solution.py:181
  7.3 5.2 %collective-permute-start = (f32[32,256]{1,0:T(8,128)S(1)}, f32[32,256]{1,0:T(8,128)S(1)}, u32[]{:S(2)}, u32[]{:S(2)}) collective-permute-start(f32[32,256]{1,0:T(8,128)S(1)} %get-tuple-element.38), channel_id=1, source_target_pairs={{0,16},{16,32},{32,48},{48,64},{64,80},{80,96},{96,112},{112,128},... | collective-permute-start | bytes 98312 | tf_op jit(solution)/shard_map/ppermute | solution.py:45
  13.4 15.5 %collective-permute-start.3 = (f32[32,1024]{1,0:T(8,128)S(1)}, f32[32,1024]{1,0:T(8,128)S(1)}, u32[]{:S(2)}, u32[]{:S(2)}) collective-permute-start(f32[32,1024]{1,0:T(8,128)S(1)} %pad_maximum_fusion.1), channel_id=1, source_target_pairs={{0,0},{1,16},{2,32},{3,48},{4,64},{5,80},{6,96},{7,112},{8,128},{9... | collective-permute-start | bytes 393224 | tf_op jit(solution)/shard_map/ppermute | solution.py:49
  28.9 8.1 %collective-permute-start.4 = (f32[32,1024]{1,0:T(8,128)S(1)}, f32[32,1024]{1,0:T(8,128)S(1)}, u32[]{:S(2)}, u32[]{:S(2)}) collective-permute-start(f32[32,1024]{1,0:T(8,128)S(1)} %collective-permute-done.3), channel_id=1, source_target_pairs={{0,256},{16,272},{32,288},{48,304},{64,320},{80,336},{96,352},{112... | collective-permute-start | bytes 393224 | tf_op jit(solution)/shard_map/ppermute | solution.py:45
  59.9 33.0 %all-to-all-start.1 = ((f32[4,128,1024]{2,1,0:T(8,128)}), f32[4,128,1024]{2,1,0:T(8,128)S(1)}, u32[]{:S(2)}, u32[]{:S(2)}) async-start(f32[4,128,1024]{2,1,0:T(8,128)} %broadcast_in_dim.15), calls=%async_computation.1 | async-start | bytes 4194304 | tf_op jit(solution)/shard_map/all_to_all | solution.py:186
  72.4 20.5 %copy-start.7 = (s32[2,32]{1,0:T(2,128)S(1)}, s32[2,32]{1,0:T(2,128)}, u32[]{:S(2)}) copy-start(s32[2,32]{1,0:T(2,128)} %lives.9) | copy-start | bytes 772
  92.9 1.2 copy-start.5
  94.1 1.2 copy-start.6
  98.6 12.9 %collective-permute-start.8 = (f32[256,1024]{1,0:T(8,128)S(1)}, f32[256,1024]{1,0:T(8,128)}, u32[]{:S(2)}, u32[]{:S(2)}) collective-permute-start(f32[256,1024]{1,0:T(8,128)S(1)} %get-tuple-element.30.own0.own1), channel_id=1, source_target_pairs={{0,16},{1,17},{2,18},{3,19},{4,20},{5,21},{6,22},{7,23},{8,24},{9,... | collective-permute-start | bytes 3145736 | tf_op jit(solution)/shard_map/ppermute | solution.py:49
  100.5 21.0 %collective-permute-start.1 = (f32[256,512]{1,0:T(8,128)}, f32[256,512]{1,0:T(8,128)}, u32[]{:S(2)}, u32[]{:S(2)}) collective-permute-start(f32[256,512]{1,0:T(8,128)} %get-tuple-element.20.own0), channel_id=1, source_target_pairs={{17,33},{18,34},{19,35},{20,36},{21,37},{22,38},{23,39},{24,40},{2... | collective-permute-start | bytes 1572872 | tf_op jit(solution)/shard_map/ppermute | solution.py:49
  102.4 19.1 %collective-permute-start.2 = (f32[256,512]{1,0:T(8,128)}, f32[256,512]{1,0:T(8,128)}, u32[]{:S(2)}, u32[]{:S(2)}) collective-permute-start(f32[256,512]{1,0:T(8,128)} %get-tuple-element.21.own1), channel_id=1, source_target_pairs={{16,32},{17,33},{18,34},{19,35},{20,36},{21,37},{22,38},{23,39},{2... | collective-permute-start | bytes 1572872 | tf_op jit(solution)/shard_map/ppermute | solution.py:49
  106.2 0.8 copy-start.1
  107.0 0.8 copy-start.3
  107.8 2.2 %copy-start = (f32[1024,1024]{1,0:T(8,128)S(1)}, f32[1024,1024]{1,0:T(8,128)}, u32[]{:S(2)}) copy-start(f32[1024,1024]{1,0:T(8,128)} %all-gather.2.cloned.1.call-done) | copy-start | bytes 12582916
  110.0 1.4 copy-start.2
  110.0 1.4 copy-start.4
  115.5 23.9 %collective-permute-start.10 = (f32[256,256]{1,0:T(8,128)S(1)}, f32[256,256]{1,0:T(8,128)S(1)}, u32[]{:S(2)}, u32[]{:S(2)}) collective-permute-start(f32[256,256]{1,0:T(8,128)S(1)} %get-tuple-element.33), channel_id=1, source_target_pairs={{1,2},{3,4},{5,6},{7,8},{9,10},{11,12},{13,14},{17,18},{19,20},{21... | collective-permute-start | bytes 786440 | tf_op jit(solution)/shard_map/ppermute | solution.py:49
  119.6 25.9 %collective-permute-start.9 = (f32[2,256,256]{2,1,0:T(8,128)S(1)}, f32[2,256,256]{2,1,0:T(8,128)S(1)}, u32[]{:S(2)}, u32[]{:S(2)}) collective-permute-start(f32[2,256,256]{2,1,0:T(8,128)S(1)} %get-tuple-element.32), channel_id=1, source_target_pairs={{0,1},{2,3},{4,5},{6,7},{8,9},{10,11},{12,13},{14,15},{16,17},{18,... | collective-permute-start | bytes 1572872 | tf_op jit(solution)/shard_map/ppermute | solution.py:49
  125.4 35.0 %collective-permute-start.5 = (f32[2,256,256]{2,1,0:T(8,128)S(1)}, f32[2,256,256]{2,1,0:T(8,128)S(1)}, u32[]{:S(2)}, u32[]{:S(2)}) collective-permute-start(f32[2,256,256]{2,1,0:T(8,128)S(1)} %get-tuple-element.27), channel_id=1, source_target_pairs={{0,1},{2,3},{4,5},{6,7},{8,9},{10,11},{12,13},{14,15},{16,17},{18,... | collective-permute-start | bytes 1572872 | tf_op jit(solution)/shard_map/ppermute | solution.py:49
  129.3 16.1 %collective-permute-start.11 = (f32[256,256]{1,0:T(8,128)S(1)}, f32[256,256]{1,0:T(8,128)S(1)}, u32[]{:S(2)}, u32[]{:S(2)}) collective-permute-start(f32[256,256]{1,0:T(8,128)S(1)} %get-tuple-element.34), channel_id=1, source_target_pairs={{1,2},{3,4},{5,6},{7,8},{9,10},{11,12},{13,14},{15,0},{17,18},{19,... | collective-permute-start | bytes 786440 | tf_op jit(solution)/shard_map/ppermute | solution.py:49
  135.4 20.9 %collective-permute-start.6 = (f32[256,256]{1,0:T(8,128)S(1)}, f32[256,256]{1,0:T(8,128)S(1)}, u32[]{:S(2)}, u32[]{:S(2)}) collective-permute-start(f32[256,256]{1,0:T(8,128)S(1)} %get-tuple-element.28), channel_id=1, source_target_pairs={{1,2},{3,4},{5,6},{7,8},{9,10},{11,12},{13,14},{17,18},{19,20},{21... | collective-permute-start | bytes 786440 | tf_op jit(solution)/shard_map/ppermute | solution.py:49
  139.4 21.0 %collective-permute-start.7 = (f32[256,256]{1,0:T(8,128)S(1)}, f32[256,256]{1,0:T(8,128)S(1)}, u32[]{:S(2)}, u32[]{:S(2)}) collective-permute-start(f32[256,256]{1,0:T(8,128)S(1)} %get-tuple-element.29), channel_id=1, source_target_pairs={{1,2},{3,4},{5,6},{7,8},{9,10},{11,12},{13,14},{15,0},{17,18},{19,... | collective-permute-start | bytes 786440 | tf_op jit(solution)/shard_map/ppermute | solution.py:49
Sparse Core Ops, SparseCore 0:
  37.9 47.6 all-gather.1

commit v9 on v7

--- a/solution.py
+++ b/solution.py
@@ -182,23 +182,6 @@
     along_x = [[x + RING * y for x in range(RING)] for y in range(RING)]
     by_row = shared(by_y.reshape(RING * 32, 2 * W), along_x).reshape(RING, RING, 32, 2 * W)
 
-    send_a, send_b0, send_b1, fb_high, fb_low = pl.pallas_call(
-        left_kernel,
-        out_shape=[shape((HALF, 2 * W), F32)] + [shape((HALF, W), F32)] * 2 + [shape((2, W, HALF), BF16)] * 2,
-        in_specs=[SMEM, SMEM] + [VMEM] * 3,
-        out_specs=[VMEM] * 5,
-        scratch_shapes=[pltpu.VMEM((W, W), BF16)] * 2,
-        compiler_params=PARAMS,
-        cost_estimate=cost(2, 7),
-        name="left",
-    )(where, window_live, by_row, hessenberg[:, 0], hessenberg[:, 1])
-
-    every_col = range(GRID_COLS)
-    pairs = [((r, c), (r + 1, c)) for r in range(1, 31, 2) for c in every_col]
-    got_b1 = swapped(send_b1, [(a, b) for a, b in pairs if a[1] + GRID_COLS >= a[0]])
-    got_b0 = swapped(send_b0, [(a, b) for a, b in pairs if a[1] >= a[0]])
-    got_a = swapped(send_a, [((r, c), (r + 1, c)) for r in range(0, 32, 2) for c in every_col])
-
     c_high, c_low = pl.pallas_call(
         prepare_kernel,
         out_shape=[shape((2, W, 2 * W), BF16)] * 2,
@@ -212,6 +195,24 @@
         cost_estimate=cost(0, 8),
         name="prepare",
     )(where, gathered)
+    by_row, c_high, c_low = lax.optimization_barrier((by_row, c_high, c_low))
+
+    send_a, send_b0, send_b1, fb_high, fb_low = pl.pallas_call(
+        left_kernel,
+        out_shape=[shape((HALF, 2 * W), F32)] + [shape((HALF, W), F32)] * 2 + [shape((2, W, HALF), BF16)] * 2,
+        in_specs=[SMEM, SMEM] + [VMEM] * 3,
+        out_specs=[VMEM] * 5,
+        scratch_shapes=[pltpu.VMEM((W, W), BF16)] * 2,
+        compiler_params=PARAMS,
+        cost_estimate=cost(2, 7),
+        name="left",
+    )(where, window_live, by_row, hessenberg[:, 0], hessenberg[:, 1])
+
+    every_col = range(GRID_COLS)
+    pairs = [((r, c), (r + 1, c)) for r in range(1, 31, 2) for c in every_col]
+    got_b1 = swapped(send_b1, [(a, b) for a, b in pairs if a[1] + GRID_COLS >= a[0]])
+    got_b0 = swapped(send_b0, [(a, b) for a, b in pairs if a[1] >= a[0]])
+    got_a = swapped(send_a, [((r, c), (r + 1, c)) for r in range(0, 32, 2) for c in every_col])
 
     def middle(first, *parts):
         return pl.pallas_call(

time: 170 us -> 165 us (0.971)
  local copies, waits for them, and re-layouts: 14.3 us -> 9.92 us
    all_to_all x1, waiting for transfers between devices: 18.9 us -> 3.34 us  [shared(): return lax.all_to_all(every, 'col', 0, 0, axis_index_groups=groups)]
    all_gather x1, waiting for transfers between devices: 0.02 us -> 13.6 us  [shards(): lax.all_gather(jnp.concatenate([mine, other], 0), 'row', axis=0, tiled=Tr...]
    slice x1, local copies, waits for them, and re-layouts: 4.1 us -> 1.62 us  [shards(): hessenberg[:, 1]]
    unnamed x16 -> x12, local copies, waits for them, and re-layouts: 6.26 us -> 4.76 us
  transfers between devices with their start and end apart: 14 -> 14, of which waited for: 6 -> 8; matrix products, arithmetic and copies ran while one was open for 4% -> 3% of each run, Pallas kernels for 9% -> 7%
where the time goes in v9:
time: 165 us; the launch traced here: 164 us
  starting transfers between devices  52.5 us (32%)
  waiting for transfers between devices  47.6 us (29%)
  blocking collectives  20.4 us (12%)
  Pallas kernels  18.1 us (11%)
  between operations  13.6 us (8%)
  local copies, waits for them, and re-layouts  9.92 us (6%)
    ppermute x10, starting transfers between devices, moved_on(): lax.ppermute(value, ('row', 'col'), [(r * GRID_COLS + c, t * GRID_COLS +...  39 us
    ppermute x10, waiting for transfers between devices, moved_on(): lax.ppermute(value, ('row', 'col'), [(r * GRID_COLS + c, t * GRID_COLS +...  21.5 us
    all_to_all x1, blocking collectives, shared(): return lax.all_to_all(every, 'col', 0, 0, axis_index_groups=groups)  20.4 us
    all_gather x1, waiting for transfers between devices, shards(): lax.all_gather(jnp.concatenate([mine, other], 0), 'row', axis=0, tiled=Tr...  13.6 us
    all_to_all x1, starting transfers between devices, shared(): return lax.all_to_all(every, 'col', 0, 0, axis_index_groups=groups)  9.29 us
    ppermute x2, waiting for transfers between devices, moved(): lax.ppermute(value, axis, [(i, j) for i, j in pairs if 0 <= j < count])  9.08 us
    pallas_call x2, Pallas kernels, last(): pl.pallas_call(functools.partial(last_kernel, first), out_shape=shape((W,...  6.8 us
    pallas_call x2, Pallas kernels, middle(): pl.pallas_call(functools.partial(middle_kernel, first), out_shape=[shape(...  6.09 us
  transfers between devices with their start and end apart: 14, of which 8 were waited for; matrix products, arithmetic and copies ran while one was open for 3% of the time, Pallas kernels for 7%

profile of v9, /device:TPU:150, one launch (start us, length us, event | category | flops | bytes accessed | tf_op | source)
XLA Modules:
  0.0 163.9 jit_solution(10308146602641389316)
XLA Ops:
  6.5 0.0 all-gather.2.cloned.1.call-start
  6.5 0.8 fusion.1
  7.3 1.9 %collective-permute-start = (f32[32,256]{1,0:T(8,128)S(1)}, f32[32,256]{1,0:T(8,128)S(1)}, u32[]{:S(2)}, u32[]{:S(2)}) collective-permute-start(f32[32,256]{1,0:T(8,128)S(1)} %get-tuple-element.44), channel_id=1, source_target_pairs={{0,16},{16,32},{32,48},{48,64},{64,80},{80,96},{96,112},{112,128},... | collective-permute-start | bytes 98312 | tf_op jit(solution)/shard_map/ppermute | solution.py:45
  9.2 3.3 %collective-permute-done = f32[32,256]{1,0:T(8,128)S(1)} collective-permute-done((f32[32,256]{1,0:T(8,128)S(1)}, f32[32,256]{1,0:T(8,128)S(1)}, u32[]{:S(2)}, u32[]{:S(2)}) %collective-permute-start) | collective-permute-done | bytes 32800 | tf_op jit(solution)/shard_map/ppermute | solution.py:45
  12.5 0.8 pad_maximum_fusion.1
  13.4 7.0 %collective-permute-start.1 = (f32[32,1024]{1,0:T(8,128)S(1)}, f32[32,1024]{1,0:T(8,128)S(1)}, u32[]{:S(2)}, u32[]{:S(2)}) collective-permute-start(f32[32,1024]{1,0:T(8,128)S(1)} %pad_maximum_fusion.1), channel_id=1, source_target_pairs={{0,0},{1,16},{2,32},{3,48},{4,64},{5,80},{6,96},{7,112},{8,128},{9... | collective-permute-start | bytes 393224 | tf_op jit(solution)/shard_map/ppermute | solution.py:49
  20.4 8.5 %collective-permute-done.1 = f32[32,1024]{1,0:T(8,128)S(1)} collective-permute-done((f32[32,1024]{1,0:T(8,128)S(1)}, f32[32,1024]{1,0:T(8,128)S(1)}, u32[]{:S(2)}, u32[]{:S(2)}) %collective-permute-start.1) | collective-permute-done | bytes 131104 | tf_op jit(solution)/shard_map/ppermute | solution.py:49
  28.9 2.4 %collective-permute-start.2 = (f32[32,1024]{1,0:T(8,128)S(1)}, f32[32,1024]{1,0:T(8,128)S(1)}, u32[]{:S(2)}, u32[]{:S(2)}) collective-permute-start(f32[32,1024]{1,0:T(8,128)S(1)} %collective-permute-done.1), channel_id=1, source_target_pairs={{0,256},{16,272},{32,288},{48,304},{64,320},{80,336},{96,352},{112... | collective-permute-start | bytes 393224 | tf_op jit(solution)/shard_map/ppermute | solution.py:45
  31.2 5.8 %collective-permute-done.2 = f32[32,1024]{1,0:T(8,128)S(1)} collective-permute-done((f32[32,1024]{1,0:T(8,128)S(1)}, f32[32,1024]{1,0:T(8,128)S(1)}, u32[]{:S(2)}, u32[]{:S(2)}) %collective-permute-start.2) | collective-permute-done | bytes 131104 | tf_op jit(solution)/shard_map/ppermute | solution.py:45
  37.0 0.7 pad_maximum_fusion
  37.7 0.0 all-gather.2.cloned.1.call-update
  37.8 20.4 %all_to_all.10 = f32[4,32,1024]{2,1,0:T(8,128)S(1)} all-to-all(f32[4,32,1024]{2,1,0:T(8,128)S(1)} %broadcast_in_dim.6), channel_id=1, replica_groups={{0,4,8,12},{1,5,9,13},{2,6,10,14},{3,7,11,15},{16,20,24,28},{17,21,25,2..., dimensions={0} | all-to-all | bytes 1048576 | tf_op jit(solution)/shard_map/all_to_all | solution.py:179
  58.3 1.6 broadcast_in_dim.15
  59.9 0.0 copy-start.5
  59.9 9.3 %all-to-all-start.1 = ((f32[4,128,1024]{2,1,0:T(8,128)}), f32[4,128,1024]{2,1,0:T(8,128)}, u32[]{:S(2)}, u32[]{:S(2)}) async-start(f32[4,128,1024]{2,1,0:T(8,128)} %broadcast_in_dim.15), calls=%async_computation.1 | async-start | bytes 4194304 | tf_op jit(solution)/shard_map/all_to_all | solution.py:179
  69.2 0.1 pad_add_fusion.where
  69.2 0.0 copy-done.5
  69.2 1.6 fusion
  70.9 1.1 copy_bitcast_fusion
  72.0 13.6 %all-gather.2.cloned.1.call-done = f32[1024,1024]{1,0:T(8,128)} async-done(((f32[64,1024]{1,0:T(8,128)}), f32[1024,1024]{1,0:T(8,128)}) %all-gather.2.cloned.1.call-update) | async-done | bytes 4194320 | tf_op jit(solution)/shard_map/all_gather | solution.py:174
  85.6 0.0 copy-start.2
  85.6 2.2 %copy-done.2 = f32[1024,1024]{1,0:T(8,128)S(1)} copy-done((f32[1024,1024]{1,0:T(8,128)S(1)}, f32[1024,1024]{1,0:T(8,128)}, u32[]{:S(2)}) %copy-start.2) | copy-done | bytes 4194328
  87.8 0.0 copy-start.4
  87.8 1.4 prepare.1
  89.2 0.0 copy-start
  89.2 1.3 copy-done
  90.6 3.3 %all-to-all-done.1 = f32[4,128,1024]{2,1,0:T(8,128)} async-done(((f32[4,128,1024]{2,1,0:T(8,128)}), f32[4,128,1024]{2,1,0:T(8,128)}, u32[]{:S(2)}, u32[]{:S(2)}) %all-to-all-start.1) | async-done | bytes 2097184 | tf_op jit(solution)/shard_map/all_to_all | solution.py:179
  93.9 0.0 copy-done.4
  93.9 0.0 copy-start.3
  93.9 1.2 copy-done.3
  95.1 0.0 copy-start.1
  95.1 3.8 %left.1 = (f32[256,1024]{1,0:T(8,128)S(1)}, f32[256,512]{1,0:T(8,128)S(1)}, f32[256,512]{1,0:T(8,128)S(1)}, bf16[2,512,256]{2,1,0:T(8,128)(2,1)S(1)}, bf16[2,512,256]{2,1,0:T(8,128)(2,1)S(1)}) custom-call(s32[2]{0:T(128)S(1)} %pad_add_fusion.where, s32[2,32]{1,0:T(2,128)S(1)} %copy-done.4, f32[4,4,32,1024]{3,2,1,0:T(8,128)} %bitcast.5.pieces, ...), custom_call_target="tpu_custom_call" | custom-call | flops 1610612736 | bytes 7340032 | tf_op jit(solution)/shard_map/left/pallas_call | solution.py:200
  98.9 1.9 %collective-permute-start.8 = (f32[256,1024]{1,0:T(8,128)S(1)}, f32[256,1024]{1,0:T(8,128)S(1)}, u32[]{:S(2)}, u32[]{:S(2)}) collective-permute-start(f32[256,1024]{1,0:T(8,128)S(1)} %get-tuple-element.36.own0.own1), channel_id=1, source_target_pairs={{0,16},{1,17},{2,18},{3,19},{4,20},{5,21},{6,22},{7,23},{8,24},{9,... | collective-permute-start | bytes 3145736 | tf_op jit(solution)/shard_map/ppermute | solution.py:49
  100.9 1.9 %collective-permute-start.3 = (f32[256,512]{1,0:T(8,128)S(1)}, f32[256,512]{1,0:T(8,128)S(1)}, u32[]{:S(2)}, u32[]{:S(2)}) collective-permute-start(f32[256,512]{1,0:T(8,128)S(1)} %get-tuple-element.26.own0), channel_id=1, source_target_pairs={{17,33},{18,34},{19,35},{20,36},{21,37},{22,38},{23,39},{24,40},{2... | collective-permute-start | bytes 1572872 | tf_op jit(solution)/shard_map/ppermute | solution.py:49
  102.8 3.6 %collective-permute-start.4 = (f32[256,512]{1,0:T(8,128)S(1)}, f32[256,512]{1,0:T(8,128)S(1)}, u32[]{:S(2)}, u32[]{:S(2)}) collective-permute-start(f32[256,512]{1,0:T(8,128)S(1)} %get-tuple-element.27.own1), channel_id=1, source_target_pairs={{16,32},{17,33},{18,34},{19,35},{20,36},{21,37},{22,38},{23,39},{2... | collective-permute-start | bytes 1572872 | tf_op jit(solution)/shard_map/ppermute | solution.py:49
  106.5 0.0 collective-permute-done.8.got0.got1
  106.5 0.0 copy-done.1
  106.5 3.1 %middle.3 = (f32[4,256,256]{2,1,0:T(8,128)S(1)}, f32[2,256,256]{2,1,0:T(8,128)S(1)}, f32[256,256]{1,0:T(8,128)S(1)}, f32[256,256]{1,0:T(8,128)S(1)}) custom-call(s32[2]{0:T(128)S(1)} %pad_add_fusion.where, s32[2,32]{1,0:T(2,128)S(1)} %copy-done.4, f32[256,1024]{1,0:T(8,128)S(1)} %get-tuple-element.36.own0.own1, f32[256,1024]{1,0:T(8,128)S(1)} %get-tuple-element.36.own0.own1, ...), custom_call_target="tpu_custom_call" | custom-call | flops 1610612736 | bytes 4194304 | tf_op jit(solution)/shard_map/middle/pallas_call | solution.py:218
  109.5 4.0 %collective-permute-start.10 = (f32[256,256]{1,0:T(8,128)S(1)}, f32[256,256]{1,0:T(8,128)S(1)}, u32[]{:S(2)}, u32[]{:S(2)}) collective-permute-start(f32[256,256]{1,0:T(8,128)S(1)} %get-tuple-element.39), channel_id=1, source_target_pairs={{1,2},{3,4},{5,6},{7,8},{9,10},{11,12},{13,14},{17,18},{19,20},{21... | collective-permute-start | bytes 786440 | tf_op jit(solution)/shard_map/ppermute | solution.py:49
  113.6 1.9 %collective-permute-start.9 = (f32[2,256,256]{2,1,0:T(8,128)S(1)}, f32[2,256,256]{2,1,0:T(8,128)S(1)}, u32[]{:S(2)}, u32[]{:S(2)}) collective-permute-start(f32[2,256,256]{2,1,0:T(8,128)S(1)} %get-tuple-element.38), channel_id=1, source_target_pairs={{0,1},{2,3},{4,5},{6,7},{8,9},{10,11},{12,13},{14,15},{16,17},{18,... | collective-permute-start | bytes 1572872 | tf_op jit(solution)/shard_map/ppermute | solution.py:49
  115.5 0.0 collective-permute-done.3.got0
  115.5 1.5 collective-permute-done.4.got1
  117.0 3.0 %middle.2 = (f32[4,256,256]{2,1,0:T(8,128)S(1)}, f32[2,256,256]{2,1,0:T(8,128)S(1)}, f32[256,256]{1,0:T(8,128)S(1)}, f32[256,256]{1,0:T(8,128)S(1)}) custom-call(s32[2]{0:T(128)S(1)} %pad_add_fusion.where, s32[2,32]{1,0:T(2,128)S(1)} %copy-done.4, f32[256,512]{1,0:T(8,128)S(1)} %get-tuple-element.26.own0, f32[256,512]{1,0:T(8,128)S(1)} %get-tuple-element.27.own1, ...), custom_call_target="tpu_custom_call" | custom-call | flops 1610612736 | bytes 4194304 | tf_op jit(solution)/shard_map/middle/pallas_call | solution.py:218
  120.0 2.4 %collective-permute-start.5 = (f32[2,256,256]{2,1,0:T(8,128)S(1)}, f32[2,256,256]{2,1,0:T(8,128)S(1)}, u32[]{:S(2)}, u32[]{:S(2)}) collective-permute-start(f32[2,256,256]{2,1,0:T(8,128)S(1)} %get-tuple-element.33), channel_id=1, source_target_pairs={{0,1},{2,3},{4,5},{6,7},{8,9},{10,11},{12,13},{14,15},{16,17},{18,... | collective-permute-start | bytes 1572872 | tf_op jit(solution)/shard_map/ppermute | solution.py:49
  122.5 6.0 %collective-permute-start.11 = (f32[256,256]{1,0:T(8,128)S(1)}, f32[256,256]{1,0:T(8,128)S(1)}, u32[]{:S(2)}, u32[]{:S(2)}) collective-permute-start(f32[256,256]{1,0:T(8,128)S(1)} %get-tuple-element.40), channel_id=1, source_target_pairs={{1,2},{3,4},{5,6},{7,8},{9,10},{11,12},{13,14},{15,0},{17,18},{19,... | collective-permute-start | bytes 786440 | tf_op jit(solution)/shard_map/ppermute | solution.py:49
  128.5 4.0 %collective-permute-start.6 = (f32[256,256]{1,0:T(8,128)S(1)}, f32[256,256]{1,0:T(8,128)S(1)}, u32[]{:S(2)}, u32[]{:S(2)}) collective-permute-start(f32[256,256]{1,0:T(8,128)S(1)} %get-tuple-element.34), channel_id=1, source_target_pairs={{1,2},{3,4},{5,6},{7,8},{9,10},{11,12},{13,14},{17,18},{19,20},{21... | collective-permute-start | bytes 786440 | tf_op jit(solution)/shard_map/ppermute | solution.py:49
  132.6 0.0 collective-permute-done.10.edge1
  132.6 6.0 %collective-permute-start.7 = (f32[256,256]{1,0:T(8,128)S(1)}, f32[256,256]{1,0:T(8,128)S(1)}, u32[]{:S(2)}, u32[]{:S(2)}) collective-permute-start(f32[256,256]{1,0:T(8,128)S(1)} %get-tuple-element.35), channel_id=1, source_target_pairs={{1,2},{3,4},{5,6},{7,8},{9,10},{11,12},{13,14},{15,0},{17,18},{19,... | collective-permute-start | bytes 786440 | tf_op jit(solution)/shard_map/ppermute | solution.py:49
  138.6 0.0 collective-permute-done.11.edge0
  138.6 0.0 collective-permute-done.9.side
  138.6 3.4 %last.2.rest_0_ = f32[512,2,512]{2,1,0:T(2,128)} custom-call(s32[2]{0:T(128)S(1)} %pad_add_fusion.where, s32[2,32]{1,0:T(2,128)S(1)} %copy-done.4, f32[4,256,256]{2,1,0:T(8,128)S(1)} %get-tuple-element.37.kept, f32[2,256,256]{2,1,0:T(8,128)S(1)} %collective-permute-done.9.side, f32[256,256]{1,0:T(8,128)S(1)} %collective-permute-done.10.edge1, ...), custom_call_target="tpu_custom_call" | custom-call | flops 805306368 | bytes 4194304 | tf_op jit(solution)/shard_map/last/pallas_call | solution.py:248
  142.1 6.8 %collective-permute-done.6.edge1 = f32[256,256]{1,0:T(8,128)S(1)} collective-permute-done((f32[256,256]{1,0:T(8,128)S(1)}, f32[256,256]{1,0:T(8,128)S(1)}, u32[]{:S(2)}, u32[]{:S(2)}) %collective-permute-start.6) | collective-permute-done | bytes 262176 | tf_op jit(solution)/shard_map/ppermute | solution.py:49
  148.9 4.7 %collective-permute-done.7.edge0 = f32[256,256]{1,0:T(8,128)S(1)} collective-permute-done((f32[256,256]{1,0:T(8,128)S(1)}, f32[256,256]{1,0:T(8,128)S(1)}, u32[]{:S(2)}, u32[]{:S(2)}) %collective-permute-start.7) | collective-permute-done | bytes 262176 | tf_op jit(solution)/shard_map/ppermute | solution.py:49
  153.6 0.0 collective-permute-done.5.side
  153.6 3.4 %last.3 = f32[512,2,512]{2,1,0:T(2,128)} custom-call(s32[2]{0:T(128)S(1)} %pad_add_fusion.where, s32[2,32]{1,0:T(2,128)S(1)} %copy-done.4, f32[4,256,256]{2,1,0:T(8,128)S(1)} %get-tuple-element.32.kept, f32[2,256,256]{2,1,0:T(8,128)S(1)} %collective-permute-done.5.side, f32[256,256]{1,0:T(8,128)S(1)} %collective-permute-done.6.edge1, ...), custom_call_target="tpu_custom_call", output_to_operand_aliasing={{}: (8, {})} | custom-call | flops 805306368 | bytes 4194304 | tf_op jit(solution)/shard_map/last/pallas_call | solution.py:248
  (1 shorter events, 0.0 us)
Async XLA Ops:
  6.5 79.1 %all-gather.2.cloned.1.call-start = ((), (), s32[]{:S(2)}) async-start(), calls=%async_computation.2 | async-start | bytes 4456448 | tf_op jit(solution)/shard_map/all_gather | solution.py:174
  7.3 5.2 %collective-permute-start = (f32[32,256]{1,0:T(8,128)S(1)}, f32[32,256]{1,0:T(8,128)S(1)}, u32[]{:S(2)}, u32[]{:S(2)}) collective-permute-start(f32[32,256]{1,0:T(8,128)S(1)} %get-tuple-element.44), channel_id=1, source_target_pairs={{0,16},{16,32},{32,48},{48,64},{64,80},{80,96},{96,112},{112,128},... | collective-permute-start | bytes 98312 | tf_op jit(solution)/shard_map/ppermute | solution.py:45
  13.4 15.5 %collective-permute-start.1 = (f32[32,1024]{1,0:T(8,128)S(1)}, f32[32,1024]{1,0:T(8,128)S(1)}, u32[]{:S(2)}, u32[]{:S(2)}) collective-permute-start(f32[32,1024]{1,0:T(8,128)S(1)} %pad_maximum_fusion.1), channel_id=1, source_target_pairs={{0,0},{1,16},{2,32},{3,48},{4,64},{5,80},{6,96},{7,112},{8,128},{9... | collective-permute-start | bytes 393224 | tf_op jit(solution)/shard_map/ppermute | solution.py:49
  28.9 8.1 %collective-permute-start.2 = (f32[32,1024]{1,0:T(8,128)S(1)}, f32[32,1024]{1,0:T(8,128)S(1)}, u32[]{:S(2)}, u32[]{:S(2)}) collective-permute-start(f32[32,1024]{1,0:T(8,128)S(1)} %collective-permute-done.1), channel_id=1, source_target_pairs={{0,256},{16,272},{32,288},{48,304},{64,320},{80,336},{96,352},{112... | collective-permute-start | bytes 393224 | tf_op jit(solution)/shard_map/ppermute | solution.py:45
  59.9 9.4 %copy-start.5 = (f32[512,2,512]{2,1,0:T(2,128)S(1)}, f32[512,2,512]{2,1,0:T(2,128)}, u32[]{:S(2)}) copy-start(f32[512,2,512]{2,1,0:T(2,128)} %param.4) | copy-start | bytes 6291460
  59.9 34.0 %all-to-all-start.1 = ((f32[4,128,1024]{2,1,0:T(8,128)}), f32[4,128,1024]{2,1,0:T(8,128)}, u32[]{:S(2)}, u32[]{:S(2)}) async-start(f32[4,128,1024]{2,1,0:T(8,128)} %broadcast_in_dim.15), calls=%async_computation.1 | async-start | bytes 4194304 | tf_op jit(solution)/shard_map/all_to_all | solution.py:179
  85.6 2.2 %copy-start.2 = (f32[1024,1024]{1,0:T(8,128)S(1)}, f32[1024,1024]{1,0:T(8,128)}, u32[]{:S(2)}) copy-start(f32[1024,1024]{1,0:T(8,128)} %all-gather.2.cloned.1.call-done) | copy-start | bytes 12582916
  87.8 6.1 %copy-start.4 = (s32[2,32]{1,0:T(2,128)S(1)}, s32[2,32]{1,0:T(2,128)}, u32[]{:S(2)}) copy-start(s32[2,32]{1,0:T(2,128)} %lives.9) | copy-start | bytes 772
  89.2 1.3 copy-start
  93.9 1.2 copy-start.3
  95.1 11.3 %copy-start.1 = (bf16[2,512,1024]{2,1,0:T(8,128)(2,1)S(1)}, bf16[2,512,1024]{2,1,0:T(8,128)(2,1)}, u32[]{:S(2)}) copy-start(bf16[2,512,1024]{2,1,0:T(8,128)(2,1)} %copy-done) | copy-start | bytes 6291460
  98.9 7.5 %collective-permute-start.8 = (f32[256,1024]{1,0:T(8,128)S(1)}, f32[256,1024]{1,0:T(8,128)S(1)}, u32[]{:S(2)}, u32[]{:S(2)}) collective-permute-start(f32[256,1024]{1,0:T(8,128)S(1)} %get-tuple-element.36.own0.own1), channel_id=1, source_target_pairs={{0,16},{1,17},{2,18},{3,19},{4,20},{5,21},{6,22},{7,23},{8,24},{9,... | collective-permute-start | bytes 3145736 | tf_op jit(solution)/shard_map/ppermute | solution.py:49
  100.9 14.6 %collective-permute-start.3 = (f32[256,512]{1,0:T(8,128)S(1)}, f32[256,512]{1,0:T(8,128)S(1)}, u32[]{:S(2)}, u32[]{:S(2)}) collective-permute-start(f32[256,512]{1,0:T(8,128)S(1)} %get-tuple-element.26.own0), channel_id=1, source_target_pairs={{17,33},{18,34},{19,35},{20,36},{21,37},{22,38},{23,39},{24,40},{2... | collective-permute-start | bytes 1572872 | tf_op jit(solution)/shard_map/ppermute | solution.py:49
  102.8 14.2 %collective-permute-start.4 = (f32[256,512]{1,0:T(8,128)S(1)}, f32[256,512]{1,0:T(8,128)S(1)}, u32[]{:S(2)}, u32[]{:S(2)}) collective-permute-start(f32[256,512]{1,0:T(8,128)S(1)} %get-tuple-element.27.own1), channel_id=1, source_target_pairs={{16,32},{17,33},{18,34},{19,35},{20,36},{21,37},{22,38},{23,39},{2... | collective-permute-start | bytes 1572872 | tf_op jit(solution)/shard_map/ppermute | solution.py:49
  109.5 23.0 %collective-permute-start.10 = (f32[256,256]{1,0:T(8,128)S(1)}, f32[256,256]{1,0:T(8,128)S(1)}, u32[]{:S(2)}, u32[]{:S(2)}) collective-permute-start(f32[256,256]{1,0:T(8,128)S(1)} %get-tuple-element.39), channel_id=1, source_target_pairs={{1,2},{3,4},{5,6},{7,8},{9,10},{11,12},{13,14},{17,18},{19,20},{21... | collective-permute-start | bytes 786440 | tf_op jit(solution)/shard_map/ppermute | solution.py:49
  113.6 25.1 %collective-permute-start.9 = (f32[2,256,256]{2,1,0:T(8,128)S(1)}, f32[2,256,256]{2,1,0:T(8,128)S(1)}, u32[]{:S(2)}, u32[]{:S(2)}) collective-permute-start(f32[2,256,256]{2,1,0:T(8,128)S(1)} %get-tuple-element.38), channel_id=1, source_target_pairs={{0,1},{2,3},{4,5},{6,7},{8,9},{10,11},{12,13},{14,15},{16,17},{18,... | collective-permute-start | bytes 1572872 | tf_op jit(solution)/shard_map/ppermute | solution.py:49
  120.0 33.6 %collective-permute-start.5 = (f32[2,256,256]{2,1,0:T(8,128)S(1)}, f32[2,256,256]{2,1,0:T(8,128)S(1)}, u32[]{:S(2)}, u32[]{:S(2)}) collective-permute-start(f32[2,256,256]{2,1,0:T(8,128)S(1)} %get-tuple-element.33), channel_id=1, source_target_pairs={{0,1},{2,3},{4,5},{6,7},{8,9},{10,11},{12,13},{14,15},{16,17},{18,... | collective-permute-start | bytes 1572872 | tf_op jit(solution)/shard_map/ppermute | solution.py:49
  122.5 16.1 %collective-permute-start.11 = (f32[256,256]{1,0:T(8,128)S(1)}, f32[256,256]{1,0:T(8,128)S(1)}, u32[]{:S(2)}, u32[]{:S(2)}) collective-permute-start(f32[256,256]{1,0:T(8,128)S(1)} %get-tuple-element.40), channel_id=1, source_target_pairs={{1,2},{3,4},{5,6},{7,8},{9,10},{11,12},{13,14},{15,0},{17,18},{19,... | collective-permute-start | bytes 786440 | tf_op jit(solution)/shard_map/ppermute | solution.py:49
  128.5 20.4 %collective-permute-start.6 = (f32[256,256]{1,0:T(8,128)S(1)}, f32[256,256]{1,0:T(8,128)S(1)}, u32[]{:S(2)}, u32[]{:S(2)}) collective-permute-start(f32[256,256]{1,0:T(8,128)S(1)} %get-tuple-element.34), channel_id=1, source_target_pairs={{1,2},{3,4},{5,6},{7,8},{9,10},{11,12},{13,14},{17,18},{19,20},{21... | collective-permute-start | bytes 786440 | tf_op jit(solution)/shard_map/ppermute | solution.py:49
  132.6 21.0 %collective-permute-start.7 = (f32[256,256]{1,0:T(8,128)S(1)}, f32[256,256]{1,0:T(8,128)S(1)}, u32[]{:S(2)}, u32[]{:S(2)}) collective-permute-start(f32[256,256]{1,0:T(8,128)S(1)} %get-tuple-element.35), channel_id=1, source_target_pairs={{1,2},{3,4},{5,6},{7,8},{9,10},{11,12},{13,14},{15,0},{17,18},{19,... | collective-permute-start | bytes 786440 | tf_op jit(solution)/shard_map/ppermute | solution.py:49
Sparse Core Ops, SparseCore 0:
  37.9 47.6 all-gather.1
